TPU v7x, 32 devices: a whole 2x2x4 slice. The times are simulated.
32 devices in a mesh: seq: 16 (over z, y, x), head: 2 (over core).
Axes of the slice: x: 2, y: 2, z: 4, core: 2. Of those that a mesh axis runs over, the one named last changes fastest.
Arguments:
- query_raw: bfloat16 [6144, 2048], P('seq', 'head'), may hold values from -6 to 6
- key_raw: bfloat16 [6144, 2048], P('seq', 'head'), may hold values from -6 to 6
- value_raw: bfloat16 [6144, 4096], P('seq', 'head'), may hold values from -6 to 6
- gate_raw: bfloat16 [6144, 4096], P('seq', 'head'), may hold values from -6 to 6
- query_taps: float32 [4, 2048], P(None, 'head'), may hold values from -3 to 3
- key_taps: float32 [4, 2048], P(None, 'head'), may hold values from -3 to 3
- value_taps: float32 [4, 4096], P(None, 'head'), may hold values from -3 to 3
- beta_logit: float32 [6144, 32], P('seq', 'head'), may hold values from -6 to 6
- decay_logit: float32 [6144, 32], P('seq', 'head'), may hold values from -14 to 0
- norm_gain: float32 [128], replicated, may hold values from 0.5 to 1.5
- out_weight: bfloat16 [4096, 2048], P('head'), may hold values from -0.09375 to 0.09375
Outputs:
- mixed: bfloat16 [6144, 2048], P(('seq', 'head'))
All inputs are finite; a program needn't handle non-finite values.
Results may differ from a plain program's by a relative error of at most 0.017.
Values may be sent and summed in bfloat16 or wider, within the bound.
No kernel may reach another device: no remote copies, remote signals or barrier semaphores. Data moves between devices by JAX's collectives and lax.ppermute only.
A program may use at most 128 MiB of HBM per device.

v0:
```python
import math

import jax
import jax.numpy as jnp
from jax import lax
from jax.experimental import pallas as pl
from jax.experimental.pallas import tpu as pltpu
from jax.sharding import PartitionSpec as P

DK = 128
DV = 128
CHUNK = 128
GROUP = 8
EPSILON = 1e-06
VMEM_BYTES = 60 * 1024 * 1024
F32 = jnp.float32
BF16 = jnp.bfloat16


def mul(left, right):
    return jnp.dot(left.astype(BF16), right.astype(BF16), preferred_element_type=F32)


def sigmoid(x):
    return 0.5 + 0.5 * jnp.tanh(0.5 * x)


def conv_silu(raw_ref, before_ref, taps_ref, padded):
    length, width = raw_ref.shape
    padded[5:8, :width] = before_ref[...].astype(F32)
    padded[8 : 8 + length, :width] = raw_ref[...].astype(F32)
    summed = taps_ref[0:1, :] * padded[5 : 5 + length, :width]
    for offset in range(1, 4):
        summed = summed + taps_ref[offset : offset + 1, :] * padded[5 + offset : 5 + offset + length, :width]
    return summed * sigmoid(summed)


def chunk_rows(ref, heads, chunks):
    held = ref.shape[0]
    first = (pl.program_id(0) * heads) % held
    rows = ref[:heads, :]
    for at in range(heads, held, heads):
        rows = jnp.where(first == at, ref[at : at + heads, :], rows)
    return jnp.concatenate([rows[:, c * CHUNK : (c + 1) * CHUNK] for c in range(chunks)], 0)


def log_fades(logit, upper):
    decay = -(jnp.maximum(logit, 0.0) + jnp.log(1.0 + jnp.exp(-jnp.abs(logit))))
    return jnp.dot(decay, upper, precision=lax.Precision.HIGHEST, preferred_element_type=F32)


def as_columns(blocks):
    rows = sum(block.shape[0] for block in blocks)
    return jnp.concatenate(list(blocks) + [jnp.zeros((CHUNK - rows, CHUNK), F32)], 0).T


def states_kernel(
    key_ref, value_ref, key_before, value_before, key_taps, value_taps, beta_ref, decay_ref,
    pairs_ref, fresh_ref, starts_ref, unit_ref, padded,
):
    length, width = key_ref.shape
    chunks = length // CHUNK
    key_heads = width // DK
    heads = value_ref.shape[1] // DV
    repeat_by = heads // key_heads
    packs = [(chunk, head) for chunk in range(chunks) for head in range(heads)]
    count = len(packs)

    rows = lax.broadcasted_iota(jnp.int32, (CHUNK, CHUNK), 0)
    cols = lax.broadcasted_iota(jnp.int32, (CHUNK, CHUNK), 1)
    within = rows >= cols
    strict = rows > cols
    differ = rows ^ cols
    identity = jnp.where(rows == cols, 1.0, 0.0)

    fade = log_fades(chunk_rows(decay_ref, heads, chunks), (rows <= cols).astype(F32))
    beta = sigmoid(chunk_rows(beta_ref, heads, chunks))
    last = jnp.exp(fade[:, CHUNK - 1 : CHUNK])
    tail = jnp.exp(fade[:, CHUNK - 1 : CHUNK] - fade)
    columns = as_columns((fade, beta, beta * jnp.exp(fade)))

    def column(kind, pack):
        at = kind * count + pack
        return columns[:, at : at + 1]

    def part(chunk):
        return slice(chunk * CHUNK, (chunk + 1) * CHUNK)

    key_conv = conv_silu(key_ref, key_before, key_taps, padded)
    key, key_cols, inner = {}, {}, {}
    for j in range(key_heads):
        own = key_conv[:, j * DK : (j + 1) * DK]
        unit = own * lax.rsqrt(jnp.sum(own * own, -1, keepdims=True) + EPSILON)
        unit_ref[:, j * DK : (j + 1) * DK] = unit.astype(BF16)
        for chunk in range(chunks):
            key[chunk, j] = unit[part(chunk)]
            key_cols[chunk, j] = key[chunk, j].T
            inner[chunk, j] = mul(key[chunk, j], key_cols[chunk, j])

    lower, inverse = [], []
    for pack, (chunk, head) in enumerate(packs):
        gap = column(0, pack) - fade[pack : pack + 1, :]
        ratio = jnp.exp(jnp.where(strict, gap, -1e30))
        low = column(1, pack) * ratio * inner[chunk, head // repeat_by]
        inverse.append(identity - jnp.where(differ == 1, low, 0.0))
        lower.append(low.astype(BF16))

    size = 2
    while size < CHUNK:
        band = jnp.where((differ >= size) & (differ < 4 * size), 1.0, 0.0).astype(BF16)
        inverse16 = [one.astype(BF16) for one in inverse]
        step = [mul(inverse16[p], lower[p] * band).astype(BF16) for p in range(count)]
        both = [mul(step[p], jnp.concatenate([step[p], inverse16[p]], 1)) for p in range(count)]
        inverse = [inverse[p] - both[p][:, CHUNK:] for p in range(count)]
        inverse = [inverse[p] + mul(both[p][:, :CHUNK], inverse[p]) for p in range(count)]
        size *= 4

    value = conv_silu(value_ref, value_before, value_taps, padded)
    solved = []
    for pack, (chunk, head) in enumerate(packs):
        right = jnp.concatenate(
            [
                column(1, pack) * value[part(chunk), head * DV : (head + 1) * DV],
                column(2, pack) * key[chunk, head // repeat_by],
            ],
            1,
        )
        solved.append(mul(inverse[pack], right))

    state = [None] * heads
    for chunk in range(chunks):
        for head in range(heads):
            pack = chunk * heads + head
            updates, wide = solved[pack][:, :DV], solved[pack][:, DV:]
            if chunk == 0:
                fresh = jnp.concatenate([updates, -wide], 1).astype(BF16)
                faded = jnp.concatenate(
                    [jnp.zeros((DK, DV), F32), last[pack : pack + 1, :] * identity], 1
                )
            else:
                start = state[head].astype(BF16)
                starts_ref[head, chunk - 1] = start
                fresh = (
                    jnp.concatenate([updates, jnp.zeros((CHUNK, DK), F32)], 1) - mul(wide, start)
                ).astype(BF16)
                faded = last[pack : pack + 1, :] * state[head]
            fresh_ref[head, part(chunk), :] = fresh
            state[head] = faded + mul(
                key_cols[chunk, head // repeat_by] * tail[pack : pack + 1, :], fresh
            )
    for head in range(heads):
        pairs_ref[head] = state[head].astype(BF16)


def local_kernel(
    query_ref, query_before, query_taps, unit_ref, decay_ref, fresh_ref, starts_ref, gate_ref, gain_ref,
    parts_ref, gated_ref, padded,
):
    length, width = query_ref.shape
    chunks = length // CHUNK
    key_heads = width // DK
    heads = fresh_ref.shape[0]
    repeat_by = heads // key_heads

    rows = lax.broadcasted_iota(jnp.int32, (CHUNK, CHUNK), 0)
    cols = lax.broadcasted_iota(jnp.int32, (CHUNK, CHUNK), 1)
    within = rows >= cols
    fade = log_fades(chunk_rows(decay_ref, heads, chunks), (rows <= cols).astype(F32))
    columns = as_columns((fade, jnp.exp(fade)))
    query = conv_silu(query_ref, query_before, query_taps, padded).astype(BF16)
    for head in range(heads):
        own = slice(head * DV, (head + 1) * DV)
        gate = gate_ref[:, own].astype(F32)
        gated_ref[:, own] = (gate * sigmoid(gate) * gain_ref[...]).astype(BF16)
    for chunk in range(chunks):
        part = slice(chunk * CHUNK, (chunk + 1) * CHUNK)
        for j in range(key_heads):
            own = slice(j * DK, (j + 1) * DK)
            inner = lax.dot_general(
                query[part, own], unit_ref[part, own], (((1,), (1,)), ((), ())), preferred_element_type=F32
            )
            for head in range(j * repeat_by, (j + 1) * repeat_by):
                pack = chunk * heads + head
                gap = columns[:, pack : pack + 1] - fade[pack : pack + 1, :]
                scores = inner * jnp.exp(jnp.where(within, gap, -1e30))
                grown = columns[:, chunks * heads + pack : chunks * heads + pack + 1]
                if chunk == 0:
                    carried = jnp.concatenate(
                        [jnp.zeros((CHUNK, DV), F32), grown * query[part, own].astype(F32)], 1
                    )
                else:
                    carried = grown * mul(query[part, own], starts_ref[head, chunk - 1])
                parts_ref[head, part, :] = (carried + mul(scores, fresh_ref[head, part, :])).astype(BF16)


def columns_of(rows, width, first=0):
    return pl.BlockSpec((rows, width), lambda step: (0, step + first))


def whole_of(array):
    return pl.BlockSpec(array.shape, lambda step: (0,) * array.ndim)


def local_steps(raws, before, taps, beta_logit, decay_logit, gate_raw, norm_gain):
    length = raws[0].shape[0]
    key_heads = raws[0].shape[1] // DK
    value_heads = raws[2].shape[1] // DV
    repeat_by = value_heads // key_heads
    each = 2 if key_heads % 2 == 0 else 1
    steps = key_heads // each
    heads = each * repeat_by
    narrow, wide = each * DK, heads * DV
    chunks = length // CHUNK

    def of_heads(*shape):
        return pl.BlockSpec((heads,) + shape, lambda step: (step,) + (0,) * len(shape))

    logits = (beta_logit.T, decay_logit.T)
    held = math.gcd(8, value_heads)
    logits_of = pl.BlockSpec((held, length), lambda step: (step * heads // held, 0))
    params = pltpu.CompilerParams(vmem_limit_bytes=VMEM_BYTES)
    pairs, fresh, starts, unit = pl.pallas_call(
        states_kernel,
        grid=(steps,),
        in_specs=[
            columns_of(length, narrow), columns_of(length, wide),
            columns_of(3, narrow, (repeat_by + 1) * steps), columns_of(3, wide),
            columns_of(4, narrow), columns_of(4, wide),
            logits_of, logits_of,
        ],
        out_specs=[
            of_heads(DK, DV + DK), of_heads(length, DV + DK), of_heads(chunks - 1, DK, DV + DK),
            columns_of(length, narrow),
        ],
        out_shape=[
            jax.ShapeDtypeStruct((value_heads, DK, DV + DK), BF16),
            jax.ShapeDtypeStruct((value_heads, length, DV + DK), BF16),
            jax.ShapeDtypeStruct((value_heads, chunks - 1, DK, DV + DK), BF16),
            jax.ShapeDtypeStruct(raws[1].shape, BF16),
        ],
        scratch_shapes=[pltpu.VMEM((8 + length, wide), F32)],
        compiler_params=params,
        cost_estimate=pl.CostEstimate(
            flops=40 * CHUNK * length * DV * value_heads,
            bytes_accessed=12 * length * DV * value_heads,
            transcendentals=0,
        ),
        name="states",
    )(raws[1], raws[2], before, before, taps[1], taps[2], *logits)
    gain = norm_gain.reshape(1, DV)

    def local():
        return pl.pallas_call(
            local_kernel,
            grid=(steps,),
            in_specs=[
                columns_of(length, narrow), columns_of(3, narrow, repeat_by * steps), columns_of(4, narrow),
                columns_of(length, narrow), logits_of,
                of_heads(length, DV + DK), of_heads(chunks - 1, DK, DV + DK),
                columns_of(length, wide), whole_of(gain),
            ],
            out_specs=[of_heads(length, DV + DK), columns_of(length, wide)],
            out_shape=[
                jax.ShapeDtypeStruct((value_heads, length, DV + DK), BF16),
                jax.ShapeDtypeStruct(gate_raw.shape, BF16),
            ],
            scratch_shapes=[pltpu.VMEM((8 + length, narrow), F32)],
            compiler_params=params,
            cost_estimate=pl.CostEstimate(
                flops=12 * CHUNK * length * DV * value_heads,
                bytes_accessed=16 * length * DV * value_heads,
                transcendentals=0,
            ),
            name="local",
        )(raws[0], before, taps[0], unit, logits[1], fresh, starts, gate_raw, gain)

    return pairs, local


def prefix_kernel(pairs_ref, prefix_ref, total_ref):
    count, heads = pairs_ref.shape[:2]
    running = [None] * heads
    for hop in range(count):
        for head in range(heads):
            now = pairs_ref[hop, head]
            if hop == 0:
                rows = lax.broadcasted_iota(jnp.int32, (DK, DV + DK), 0)
                cols = lax.broadcasted_iota(jnp.int32, (DK, DV + DK), 1)
                prefix_ref[hop, head] = jnp.where(cols == rows + DV, 1.0, 0.0).astype(BF16)
                running[head] = now.astype(F32)
            else:
                before = running[head].astype(BF16)
                prefix_ref[hop, head] = before
                own = jnp.concatenate([now[:, :DV].astype(F32), jnp.zeros((DK, DK), F32)], 1)
                running[head] = own + mul(now[:, DV:], before)
    for head in range(heads):
        total_ref[head] = running[head].astype(BF16)


def apply_kernel(prefix_ref, start_ref, starts_ref):
    count, heads = prefix_ref.shape[:2]
    for hop in range(count):
        for head in range(heads):
            starts_ref[hop, head] = (
                prefix_ref[hop, head, :, :DV].astype(F32)
                + mul(prefix_ref[hop, head, :, DV:], start_ref[head])
            ).astype(BF16)


def shifted(value, axis, by):
    count = lax.axis_size(axis)
    return lax.ppermute(value, axis, [(i, i + by) for i in range(count - by)])


def group_start(total, axis, group):
    groups = lax.axis_size(axis) // group
    if groups == 2:
        return shifted(total[..., :DV], axis, group)
    running = shifted(total, axis, group)
    by = 1
    while by < groups - 1:
        earlier = shifted(running, axis, by * group)
        product = jnp.einsum("bkl,blv->bkv", running[..., DV:], earlier, preferred_element_type=F32)
        own = jnp.pad(running[..., :DV], ((0, 0), (0, 0), (0, DK)))
        running = (product + own.astype(F32)).astype(BF16)
        by *= 2
    return running[..., :DV]


def starts_of(pairs, axis, beside):
    size = lax.axis_size(axis)
    heads = pairs.shape[0]
    group = math.gcd(math.gcd(size, heads), GROUP)
    groups = [[g * group + i for i in range(group)] for g in range(size // group)]
    each = heads // group
    params = pltpu.CompilerParams(vmem_limit_bytes=VMEM_BYTES)
    by_head = lax.all_to_all(pairs, axis, 0, 0, axis_index_groups=groups, tiled=True)
    by_head, done = lax.optimization_barrier((by_head, beside()))
    prefix, total = pl.pallas_call(
        prefix_kernel,
        out_shape=[
            jax.ShapeDtypeStruct((group, each, DK, DV + DK), BF16),
            jax.ShapeDtypeStruct((each, DK, DV + DK), BF16),
        ],
        compiler_params=params,
        name="prefix",
    )(by_head.reshape(group, each, DK, DV + DK))
    starts = pl.pallas_call(
        apply_kernel,
        out_shape=jax.ShapeDtypeStruct((group, each, DK, DV), BF16),
        compiler_params=params,
        name="apply",
    )(prefix, group_start(total, axis, group))
    starts = lax.all_to_all(
        starts.reshape(heads, DK, DV), axis, 0, 0, axis_index_groups=groups, tiled=True
    )
    return starts, done


def project_kernel(place_ref, parts_ref, starts_ref, gated_ref, weight_ref, out_ref, normed):
    heads = parts_ref.shape[0]

    @pl.when(pl.program_id(0) == 0)
    def _():
        for head in range(heads):
            part = slice(head * DV, (head + 1) * DV)
            core = parts_ref[head, :, :DV].astype(F32) + mul(
                parts_ref[head, :, DV:], starts_ref[head]
            )
            scale = lax.rsqrt(jnp.mean(core * core, -1, keepdims=True) + EPSILON)
            normed[:, part] = (core * scale * gated_ref[:, part].astype(F32)).astype(BF16)

    out_ref[...] = jnp.dot(
        normed[...], weight_ref[...], preferred_element_type=F32
    ).astype(out_ref.dtype)


def project(parts, starts, gated, out_weight, place, rows):
    heads = parts.shape[0]
    depth, width = out_weight.shape
    block = min(512, width)
    return pl.pallas_call(
        project_kernel,
        grid_spec=pltpu.PrefetchScalarGridSpec(
            num_scalar_prefetch=1,
            grid=(width // block,),
            in_specs=[
                pl.BlockSpec((heads, rows, DV + DK), lambda step, place: (0, place[0], 0)),
                pl.BlockSpec(starts.shape, lambda step, place: (0, 0, 0)),
                pl.BlockSpec((rows, depth), lambda step, place: (place[0], 0)),
                pl.BlockSpec((depth, block), lambda step, place: (0, step)),
            ],
            out_specs=pl.BlockSpec((rows, block), lambda step, place: (0, step)),
            scratch_shapes=[pltpu.VMEM((rows, depth), BF16)],
        ),
        out_shape=jax.ShapeDtypeStruct((rows, width), BF16),
        compiler_params=pltpu.CompilerParams(vmem_limit_bytes=VMEM_BYTES),
        cost_estimate=pl.CostEstimate(
            flops=2 * rows * depth * width, bytes_accessed=2 * depth * width, transcendentals=0
        ),
        name="project",
    )(place, parts, starts, gated, out_weight)


def projected(parts, starts, gated, out_weight, axis):
    length = parts.shape[1]
    if lax.axis_size(axis) != 2:
        partial = project(parts, starts, gated, out_weight, jnp.zeros((1,), jnp.int32), length)
        return lax.psum_scatter(partial, axis, scatter_dimension=0, tiled=True)
    here = lax.axis_index(axis).astype(jnp.int32).reshape(1)
    away = project(parts, starts, gated, out_weight, 1 - here, length // 2)
    other = lax.ppermute(away, axis, [(0, 1), (1, 0)])
    own = project(parts, starts, gated, out_weight, here, length // 2)
    return (own.astype(F32) + other.astype(F32)).astype(BF16)


def tails_kernel(value_ref, query_ref, key_ref, out_ref):
    at = 0
    for ref in (value_ref, query_ref, key_ref):
        width = ref.shape[1]
        out_ref[:, at : at + width] = ref[...].astype(F32)[13:16].astype(BF16)
        at += width


def tails(raws):
    length = raws[0].shape[0]
    order = (raws[2], raws[0], raws[1])
    width = sum(raw.shape[1] for raw in order)
    return pl.pallas_call(
        tails_kernel,
        grid=(1,),
        in_specs=[pl.BlockSpec((16, raw.shape[1]), lambda step: (length // 16 - 1, 0)) for raw in order],
        out_specs=pl.BlockSpec((3, width), lambda step: (0, 0)),
        out_shape=jax.ShapeDtypeStruct((3, width), BF16),
        compiler_params=pltpu.CompilerParams(vmem_limit_bytes=VMEM_BYTES),
        name="tails",
    )(*order)


def shards(
    query_raw, key_raw, value_raw, gate_raw, query_taps, key_taps, value_taps,
    beta_logit, decay_logit, norm_gain, out_weight,
):
    raws = (query_raw, key_raw, value_raw)
    before = shifted(tails(raws), "seq", 1)
    pairs, local = local_steps(
        raws, before, (query_taps, key_taps, value_taps), beta_logit, decay_logit, gate_raw, norm_gain
    )
    starts, (parts, gated) = starts_of(pairs, "seq", local)
    return projected(parts, starts, gated, out_weight, "head")


def solution(mesh):
    placed = (
        P("seq", "head"), P("seq", "head"), P("seq", "head"), P("seq", "head"),
        P(None, "head"), P(None, "head"), P(None, "head"),
        P("seq", "head"), P("seq", "head"), P(), P("head", None),
    )
    return jax.shard_map(
        shards, mesh=mesh, in_specs=placed, out_specs=P(("seq", "head"), None), check_vma=False
    )
```

profile of v0, /device:TPU:0, one launch (start us, length us, event | category | flops | bytes accessed | tf_op | source)
XLA Modules:
  0.0 92.0 jit_solution(15638568014029805146)
XLA Ops:
  0.0 1.5 %tails.1 = bf16[3,4096]{1,0:T(4,128)(2,1)} custom-call(bf16[384,2048]{1,0:T(8,128)(2,1)} %value_ref.3, bf16[384,1024]{1,0:T(8,128)(2,1)} %query_ref.3, bf16[384,1024]{1,0:T(8,128)(2,1)} %key_ref.3), custom_call_target="tpu_custom_call" | custom-call | tf_op jit(solution)/shard_map/tails/pallas_call | solution.py:429
  1.5 4.8 %collective-permute-start = (bf16[3,4096]{1,0:T(4,128)(2,1)}, bf16[3,4096]{1,0:T(4,128)(2,1)S(1)}, u32[]{:S(2)}, u32[]{:S(2)}) collective-permute-start(bf16[3,4096]{1,0:T(4,128)(2,1)} %tails.1), channel_id=1, source_target_pairs={{0,2},{2,4},{4,6},{6,8},{8,10},{10,12},{12,14},{14,16},{16,18},{18... | collective-permute-start | bytes 73736 | tf_op jit(solution)/shard_map/ppermute | solution.py:312
  6.3 1.9 %collective-permute-done.key_before.value_before.query_before = bf16[3,4096]{1,0:T(4,128)(2,1)S(1)} collective-permute-done((bf16[3,4096]{1,0:T(4,128)(2,1)}, bf16[3,4096]{1,0:T(4,128)(2,1)S(1)}, u32[]{:S(2)}, u32[]{:S(2)}) %collective-permute-start) | collective-permute-done | bytes 24608 | tf_op jit(solution)/shard_map/ppermute | solution.py:312
  8.2 0.0 copy-start.3
  8.2 0.6 copy-done.3
  8.8 18.3 %states.1 = (bf16[16,128,256]{2,1,0:T(8,128)(2,1)}, bf16[16,384,256]{2,1,0:T(8,128)(2,1)}, bf16[16,2,128,256]{3,2,1,0:T(8,128)(2,1)}, bf16[384,1024]{1,0:T(8,128)(2,1)}) custom-call(bf16[384,1024]{1,0:T(8,128)(2,1)} %key_ref.3, bf16[384,2048]{1,0:T(8,128)(2,1)} %value_ref.3, bf16[3,4096]{1,0:T(4,128)(2,1)} %copy-done.3, bf16[3,4096]{1,0:T(4,128)(2,1)} %copy-done.3, ...), custom_call_target="tpu_custom_call" | custom-call | flops 4026531840 | bytes 9437184 | tf_op jit(solution)/shard_map/states/pallas_call | solution.py:222
  27.1 5.5 %all-to-all-start = ((bf16[16,128,256]{2,1,0:T(8,128)(2,1)}), bf16[16,128,256]{2,1,0:T(8,128)(2,1)S(1)}, u32[]{:S(2)}, u32[]{:S(2)}) async-start(bf16[16,128,256]{2,1,0:T(8,128)(2,1)} %get-tuple-element.16), calls=%async_computation | async-start | bytes 2097152 | tf_op jit(solution)/shard_map/all_to_all | solution.py:337
  32.6 9.0 %local.1 = (bf16[16,384,256]{2,1,0:T(8,128)(2,1)}, bf16[384,2048]{1,0:T(8,128)(2,1)}) custom-call(bf16[384,1024]{1,0:T(8,128)(2,1)} %query_ref.3, bf16[3,4096]{1,0:T(4,128)(2,1)} %copy-done.3, f32[4,1024]{1,0:T(4,128)} %query_taps.1, bf16[384,1024]{1,0:T(8,128)(2,1)} %get-tuple-element.17.unit_ref, f32[16,384]{1,0:T(8,128)} %bitcast.9, ...), custom_call_target="tpu_custom_call" | custom-call | flops 1207959552 | bytes 12582912 | tf_op jit(solution)/shard_map/local/pallas_call | solution.py:253
  41.6 4.6 %all-to-all-done = bf16[16,128,256]{2,1,0:T(8,128)(2,1)S(1)} async-done(((bf16[16,128,256]{2,1,0:T(8,128)(2,1)}), bf16[16,128,256]{2,1,0:T(8,128)(2,1)S(1)}, u32[]{:S(2)}, u32[]{:S(2)}) %all-to-all-start) | async-done | bytes 1048608 | tf_op jit(solution)/shard_map/all_to_all | solution.py:337
  46.2 0.0 copy-start.1
  46.2 1.0 %copy-done.1 = bf16[16,128,256]{2,1,0:T(8,128)(2,1)} copy-done((bf16[16,128,256]{2,1,0:T(8,128)(2,1)}, bf16[16,128,256]{2,1,0:T(8,128)(2,1)S(1)}, u32[]{:S(2)}) %copy-start.1) | copy-done | bytes 1048600
  47.1 3.2 %prefix.1 = (bf16[8,2,128,256]{3,2,1,0:T(8,128)(2,1)}, bf16[2,128,256]{2,1,0:T(8,128)(2,1)}) custom-call(bf16[8,2,128,256]{3,2,1,0:T(8,128)(2,1)} %bitcast.6), custom_call_target="tpu_custom_call" | custom-call | tf_op jit(solution)/shard_map/prefix/pallas_call | solution.py:339
  50.4 0.8 slice.3
  51.2 5.3 %collective-permute-start.1 = (bf16[2,128,128]{2,1,0:T(8,128)(2,1)S(1)}, bf16[2,128,128]{2,1,0:T(8,128)(2,1)S(1)}, u32[]{:S(2)}, u32[]{:S(2)}) collective-permute-start(bf16[2,128,128]{2,1,0:T(8,128)(2,1)S(1)} %slice.3), channel_id=1, source_target_pairs={{0,16},{2,18},{4,20},{6,22},{8,24},{10,26},{12,28},{14,30},{1,17},... | collective-permute-start | bytes 196616 | tf_op jit(solution)/shard_map/ppermute | solution.py:312
  56.6 1.9 %collective-permute-done.1.start_ref = bf16[2,128,128]{2,1,0:T(8,128)(2,1)S(1)} collective-permute-done((bf16[2,128,128]{2,1,0:T(8,128)(2,1)S(1)}, bf16[2,128,128]{2,1,0:T(8,128)(2,1)S(1)}, u32[]{:S(2)}, u32[]{:S(2)}) %collective-permute-start.1) | collective-permute-done | bytes 65568 | tf_op jit(solution)/shard_map/ppermute | solution.py:312
  58.4 0.0 copy-start.2
  58.4 0.6 copy-done.2
  59.0 2.3 %apply.1 = bf16[8,2,128,128]{3,2,1,0:T(8,128)(2,1)} custom-call(bf16[8,2,128,256]{3,2,1,0:T(8,128)(2,1)} %get-tuple-element.24.prefix_ref, bf16[2,128,128]{2,1,0:T(8,128)(2,1)} %copy-done.2), custom_call_target="tpu_custom_call" | custom-call | tf_op jit(solution)/shard_map/apply/pallas_call | solution.py:348
  61.4 3.7 %all-to-all-start.1 = ((bf16[16,128,128]{2,1,0:T(8,128)(2,1)}), bf16[16,128,128]{2,1,0:T(8,128)(2,1)S(1)}, u32[]{:S(2)}, u32[]{:S(2)}) async-start(bf16[16,128,128]{2,1,0:T(8,128)(2,1)} %bitcast.7), calls=%async_computation.1 | async-start | bytes 1048576 | tf_op jit(solution)/shard_map/all_to_all | solution.py:354
  65.1 8.8 %all-to-all-done.1.starts_ref = bf16[16,128,128]{2,1,0:T(8,128)(2,1)S(1)} async-done(((bf16[16,128,128]{2,1,0:T(8,128)(2,1)}), bf16[16,128,128]{2,1,0:T(8,128)(2,1)S(1)}, u32[]{:S(2)}, u32[]{:S(2)}) %all-to-all-start.1) | async-done | bytes 524320 | tf_op jit(solution)/shard_map/all_to_all | solution.py:354
  73.9 0.0 copy-start
  73.9 0.8 copy-done
  74.7 7.5 %project.3 = bf16[192,2048]{1,0:T(8,128)(2,1)} custom-call(s32[1]{0:T(128)S(6)} %sub.3.place_ref, bf16[16,384,256]{2,1,0:T(8,128)(2,1)} %get-tuple-element.22.parts_ref, bf16[16,128,128]{2,1,0:T(8,128)(2,1)} %copy-done, bf16[384,2048]{1,0:T(8,128)(2,1)} %get-tuple-element.26.gated_ref, bf16[2048,2048]{1,0:T(8,128)(2,1)} %weight_ref.3), custom_call_target="tpu_custom_call" | custom-call | flops 1610612736 | bytes 8388608 | tf_op jit(solution)/shard_map/project/pallas_call | solution.py:382
  82.1 0.0 collective-permute-start.2
  82.1 7.6 %project.2 = bf16[192,2048]{1,0:T(8,128)(2,1)} custom-call(s32[1]{0:T(128)} %bitcast.place_ref, bf16[16,384,256]{2,1,0:T(8,128)(2,1)} %get-tuple-element.22.parts_ref, bf16[16,128,128]{2,1,0:T(8,128)(2,1)} %copy-done, bf16[384,2048]{1,0:T(8,128)(2,1)} %get-tuple-element.26.gated_ref, bf16[2048,2048]{1,0:T(8,128)(2,1)} %weight_ref.3), custom_call_target="tpu_custom_call" | custom-call | flops 1610612736 | bytes 8388608 | tf_op jit(solution)/shard_map/project/pallas_call | solution.py:382
  89.7 0.0 collective-permute-done.2
  89.7 2.3 %add_convert_fusion = bf16[192,2048]{1,0:T(8,128)(2,1)} fusion(bf16[192,2048]{1,0:T(8,128)(2,1)S(1)} %collective-permute-done.2, bf16[192,2048]{1,0:T(8,128)(2,1)} %project.2), kind=kLoop, calls=%fused_computation | loop fusion | flops 1572864 | bytes 2359296 | tf_op jit(solution)/shard_map/convert_element_type | solution.py:414
Async XLA Ops:
  1.5 6.7 %collective-permute-start = (bf16[3,4096]{1,0:T(4,128)(2,1)}, bf16[3,4096]{1,0:T(4,128)(2,1)S(1)}, u32[]{:S(2)}, u32[]{:S(2)}) collective-permute-start(bf16[3,4096]{1,0:T(4,128)(2,1)} %tails.1), channel_id=1, source_target_pairs={{0,2},{2,4},{4,6},{6,8},{8,10},{10,12},{12,14},{14,16},{16,18},{18... | collective-permute-start | bytes 73736 | tf_op jit(solution)/shard_map/ppermute | solution.py:312
  8.2 0.6 copy-start.3
  27.1 19.0 %all-to-all-start = ((bf16[16,128,256]{2,1,0:T(8,128)(2,1)}), bf16[16,128,256]{2,1,0:T(8,128)(2,1)S(1)}, u32[]{:S(2)}, u32[]{:S(2)}) async-start(bf16[16,128,256]{2,1,0:T(8,128)(2,1)} %get-tuple-element.16), calls=%async_computation | async-start | bytes 2097152 | tf_op jit(solution)/shard_map/all_to_all | solution.py:337
  46.2 1.0 %copy-start.1 = (bf16[16,128,256]{2,1,0:T(8,128)(2,1)}, bf16[16,128,256]{2,1,0:T(8,128)(2,1)S(1)}, u32[]{:S(2)}) copy-start(bf16[16,128,256]{2,1,0:T(8,128)(2,1)S(1)} %all-to-all-done) | copy-start | bytes 3145732
  51.2 7.2 %collective-permute-start.1 = (bf16[2,128,128]{2,1,0:T(8,128)(2,1)S(1)}, bf16[2,128,128]{2,1,0:T(8,128)(2,1)S(1)}, u32[]{:S(2)}, u32[]{:S(2)}) collective-permute-start(bf16[2,128,128]{2,1,0:T(8,128)(2,1)S(1)} %slice.3), channel_id=1, source_target_pairs={{0,16},{2,18},{4,20},{6,22},{8,24},{10,26},{12,28},{14,30},{1,17},... | collective-permute-start | bytes 196616 | tf_op jit(solution)/shard_map/ppermute | solution.py:312
  58.4 0.6 copy-start.2
  61.4 12.5 %all-to-all-start.1 = ((bf16[16,128,128]{2,1,0:T(8,128)(2,1)}), bf16[16,128,128]{2,1,0:T(8,128)(2,1)S(1)}, u32[]{:S(2)}, u32[]{:S(2)}) async-start(bf16[16,128,128]{2,1,0:T(8,128)(2,1)} %bitcast.7), calls=%async_computation.1 | async-start | bytes 1048576 | tf_op jit(solution)/shard_map/all_to_all | solution.py:354
  73.9 0.8 copy-start
  82.1 7.6 %collective-permute-start.2 = (bf16[192,2048]{1,0:T(8,128)(2,1)}, bf16[192,2048]{1,0:T(8,128)(2,1)S(1)}, u32[]{:S(2)}, u32[]{:S(2)}) collective-permute-start(bf16[192,2048]{1,0:T(8,128)(2,1)} %project.3), channel_id=1, source_target_pairs={{0,1},{1,0},{2,3},{3,2},{4,5},{5,4},{6,7},{7,6},{8,9},{9,8},{10,11... | collective-permute-start | bytes 2359304 | tf_op jit(solution)/shard_map/ppermute | solution.py:412
where the time goes:
time: 92.8 us; the launch traced here: 92 us
  Pallas kernels  49.4 us (53%)
  starting transfers between devices  19.4 us (21%)
  waiting for transfers between devices  17.1 us (18%)
  local copies, waits for them, and re-layouts  3.8 us (4%)
  other arithmetic  2.28 us (2%)
    pallas_call x1, Pallas kernels, local_steps(): pl.pallas_call(states_kernel, grid=(steps,), in_specs=[columns_of(length,...  18.3 us
    pallas_call x2, Pallas kernels, project(): pl.pallas_call(project_kernel, grid_spec=pltpu.PrefetchScalarGridSpec(num...  15.1 us
    ppermute x2, starting transfers between devices, shifted(): return lax.ppermute(value, axis, [(i, i + by) for i in range(count - by)])  10.1 us
    pallas_call x1, Pallas kernels, local(): pl.pallas_call(local_kernel, grid=(steps,), in_specs=[columns_of(length,...  9.02 us
    all_to_all x1, waiting for transfers between devices, starts_of(): lax.all_to_all(starts.reshape(heads, DK, DV), axis, 0, 0, axis_index_grou...  8.77 us
    all_to_all x1, starting transfers between devices, starts_of(): lax.all_to_all(pairs, axis, 0, 0, axis_index_groups=groups, tiled=True)  5.47 us
    all_to_all x1, waiting for transfers between devices, starts_of(): lax.all_to_all(pairs, axis, 0, 0, axis_index_groups=groups, tiled=True)  4.55 us
    ppermute x2, waiting for transfers between devices, shifted(): return lax.ppermute(value, axis, [(i, i + by) for i in range(count - by)])  3.78 us
  transfers between devices with their start and end apart: 5, of which 4 were waited for; matrix products, arithmetic and copies ran while one was open for 0% of the time, Pallas kernels for 18%

commit v1 on v0

v1 whole, which is shorter than its diff:
```python
import math

import jax
import jax.numpy as jnp
from jax import lax
from jax.experimental import pallas as pl
from jax.experimental.pallas import tpu as pltpu
from jax.sharding import PartitionSpec as P

DK = 128
DV = 128
CHUNK = 128
SMALL = 32
GROUP = 8
HEADS_AT_ONCE = 4
EPSILON = 1e-06
F32 = jnp.float32
BF16 = jnp.bfloat16


def mul(left, right):
    return jnp.dot(left.astype(BF16), right.astype(BF16), preferred_element_type=F32)


def sigmoid(x):
    return 0.5 + 0.5 * jnp.tanh(0.5 * x)


def conv_silu(padded, first, rows, taps_ref):
    summed = taps_ref[0:1, :] * padded[first : first + rows, :]
    for offset in range(1, 4):
        summed = summed + taps_ref[offset : offset + 1, :] * padded[first + offset : first + offset + rows, :]
    return summed * sigmoid(summed)


def unit_rows(key):
    return key * lax.rsqrt(jnp.sum(key * key, -1, keepdims=True) + EPSILON)


def part_of(chunk):
    return slice(chunk * CHUNK, (chunk + 1) * CHUNK)


def head_of(head):
    return slice(head * DK, (head + 1) * DK)


def chunk_rows(ref, heads, chunks):
    held = ref.shape[0]
    first = (pl.program_id(0) * heads) % held
    rows = ref[:heads, :]
    for at in range(heads, held, heads):
        rows = jnp.where(first == at, ref[at : at + heads, :], rows)
    return jnp.concatenate([rows[:, part_of(c)] for c in chunks], 0)


def square_iotas(rows=CHUNK):
    return (
        lax.broadcasted_iota(jnp.int32, (rows, CHUNK), 0),
        lax.broadcasted_iota(jnp.int32, (rows, CHUNK), 1),
    )


def log_fades(logit):
    rows, cols = square_iotas()
    decay = -(jnp.maximum(logit, 0.0) + jnp.log(1.0 + jnp.exp(-jnp.abs(logit))))
    return jnp.dot(
        decay, (rows <= cols).astype(F32), precision=lax.Precision.HIGHEST, preferred_element_type=F32
    )


def as_columns(blocks):
    rows = sum(block.shape[0] for block in blocks)
    return jnp.concatenate(list(blocks) + [jnp.zeros((CHUNK - rows, CHUNK), F32)], 0).T


def solved_packs(fade, beta, keys, key_cols, values):
    count = len(keys)
    rows, cols = square_iotas()
    strict = rows > cols
    differ = rows ^ cols
    columns = as_columns((fade, beta, beta * jnp.exp(fade)))
    inner = {id(key): mul(key, turned) for key, turned in zip(keys, key_cols)}
    lower = []
    for p in range(count):
        gap = columns[:, p : p + 1] - fade[p : p + 1, :]
        ratio = jnp.exp(jnp.where(strict, gap, -1e30))
        lower.append(columns[:, count + p : count + p + 1] * ratio * inner[id(keys[p])])

    small_rows, small_cols = square_iotas(SMALL)
    small_differ = small_rows ^ (small_cols % SMALL)
    place = small_cols // SMALL
    blocks = jnp.where(rows // SMALL == cols // SMALL, 1.0, 0.0)
    blocks16 = blocks.astype(BF16)

    def spread(small):
        return jnp.concatenate([small] * (CHUNK // SMALL), 0) * (blocks16 if small.dtype == BF16 else blocks)

    small = []
    for low in lower:
        held = low[:SMALL]
        for at in range(1, CHUNK // SMALL):
            held = jnp.where(place == at, low[at * SMALL : (at + 1) * SMALL], held)
        small.append(held)
    inverse = [
        jnp.where(small_differ == 0, 1.0, jnp.where(small_differ == 1, -one, 0.0)) for one in small
    ]
    size = 2
    while size < CHUNK:
        last = size == SMALL
        if last:
            band = (differ >= size) & (differ < 4 * size)
            inside = [jnp.where(band, low, 0.0).astype(BF16) for low in lower]
            inverse16 = [spread(one.astype(BF16)) for one in inverse]
            inverse = [spread(one) for one in inverse]
            wide16 = inverse16
        else:
            band = (small_differ >= size) & (small_differ < 4 * size)
            inside = [spread(jnp.where(band, one, 0.0).astype(BF16)) for one in small]
            inverse16 = [one.astype(BF16) for one in inverse]
            wide16 = [spread(one) for one in inverse16]
        step = [mul(inverse16[p], inside[p]).astype(BF16) for p in range(count)]
        both = [
            mul(step[p], jnp.concatenate([step[p] if last else spread(step[p]), wide16[p]], 1))
            for p in range(count)
        ]
        inverse = [inverse[p] - both[p][:, CHUNK:] for p in range(count)]
        partial = [inverse[p].astype(BF16) for p in range(count)]
        inverse = [
            inverse[p] + mul(both[p][:, :CHUNK], partial[p] if last else spread(partial[p]))
            for p in range(count)
        ]
        size *= 4

    solved = []
    for p in range(count):
        right = jnp.concatenate(
            [
                columns[:, count + p : count + p + 1] * values[p],
                columns[:, 2 * count + p : 2 * count + p + 1] * keys[p],
            ],
            1,
        )
        solved.append(mul(inverse[p], right))
    return solved


def later_kernel(
    key_ref, value_ref, key_taps, value_taps, beta_ref, decay_ref,
    solved_ref, unit_ref, turned_ref, key_padded, value_padded,
):
    length, width = key_ref.shape
    chunks = range(1, length // CHUNK)
    key_heads = width // DK
    heads = value_ref.shape[1] // DV
    repeat_by = heads // key_heads
    packs = [(chunk, head) for chunk in chunks for head in range(heads)]
    skip = CHUNK - 16
    count = length - CHUNK
    key_padded[...] = key_ref[skip:, :].astype(F32)
    value_padded[...] = value_ref[skip:, :].astype(F32)
    key_conv = conv_silu(key_padded, 13, count, key_taps)
    key, turned = {}, {}
    for j in range(key_heads):
        unit = unit_rows(key_conv[:, head_of(j)])
        unit_ref[:, head_of(j)] = unit.astype(BF16)
        for chunk in chunks:
            key[chunk, j] = unit[part_of(chunk - 1)]
            turned[chunk, j] = key[chunk, j].T
            turned_ref[j, chunk - 1] = turned[chunk, j].astype(BF16)
    value = conv_silu(value_padded, 13, count, value_taps)
    solved = solved_packs(
        log_fades(chunk_rows(decay_ref, heads, chunks)),
        sigmoid(chunk_rows(beta_ref, heads, chunks)),
        [key[chunk, head // repeat_by] for chunk, head in packs],
        [turned[chunk, head // repeat_by] for chunk, head in packs],
        [value[part_of(chunk - 1), head_of(head)] for chunk, head in packs],
    )
    for (chunk, head), one in zip(packs, solved):
        solved_ref[head, part_of(chunk - 1), :] = one.astype(BF16)


def states_kernel(
    key_ref, value_ref, key_before, value_before, key_taps, value_taps, beta_ref, decay_ref,
    solved_hbm, turned_hbm,
    pairs_ref, unit_ref, fresh_hbm, starts_hbm,
    key_padded, value_padded, solved_ref, turned_ref, fresh_ref, starts_ref, in_sem, out_sem,
):
    heads, length = decay_ref.shape
    chunks = length // CHUNK
    key_heads = key_ref.shape[1] // DK
    repeat_by = heads // key_heads
    incoming = [
        pltpu.make_async_copy(solved_hbm, solved_ref, in_sem.at[0]),
        pltpu.make_async_copy(turned_hbm, turned_ref, in_sem.at[1]),
    ]
    for copy in incoming:
        copy.start()

    key_padded[5:8, :] = key_before[...].astype(F32)
    key_padded[8 : 8 + CHUNK, :] = key_ref[...].astype(F32)
    value_padded[5:8, :] = value_before[...].astype(F32)
    value_padded[8 : 8 + CHUNK, :] = value_ref[...].astype(F32)
    key_conv = conv_silu(key_padded, 5, CHUNK, key_taps)
    key, first_turned = [], []
    for j in range(key_heads):
        key.append(unit_rows(key_conv[:, head_of(j)]))
        unit_ref[:, head_of(j)] = key[j].astype(BF16)
        first_turned.append(key[j].T)
    value = conv_silu(value_padded, 5, CHUNK, value_taps)
    fade = log_fades(chunk_rows(decay_ref, heads, range(chunks)))
    solved = solved_packs(
        fade[:heads],
        sigmoid(beta_ref[:, :CHUNK]),
        [key[head // repeat_by] for head in range(heads)],
        [first_turned[head // repeat_by] for head in range(heads)],
        [value[:, head_of(head)] for head in range(heads)],
    )
    last = jnp.exp(fade[:, CHUNK - 1 : CHUNK])
    tail = jnp.exp(fade[:, CHUNK - 1 : CHUNK] - fade)
    rows, cols = square_iotas()
    identity = jnp.where(rows == cols, 1.0, 0.0)

    state = [None] * heads
    outgoing = []
    for chunk in range(chunks):
        if chunk == 1:
            for copy in incoming:
                copy.wait()
        for head in range(heads):
            pack = chunk * heads + head
            if chunk == 0:
                updates, wide = solved[head][:, :DV], solved[head][:, DV:]
                fresh = jnp.concatenate([updates, -wide], 1).astype(BF16)
                faded = jnp.concatenate(
                    [jnp.zeros((DK, DV), F32), last[pack : pack + 1, :] * identity], 1
                )
                turned = first_turned[head // repeat_by]
            else:
                held = solved_ref[head, part_of(chunk - 1), :]
                start = state[head].astype(BF16)
                starts_ref[head, chunk - 1] = start
                taken = mul(held[:, DV:], start)
                fresh = jnp.concatenate(
                    [held[:, :DV].astype(F32) - taken[:, :DV], -taken[:, DV:]], 1
                ).astype(BF16)
                faded = last[pack : pack + 1, :] * state[head]
                turned = turned_ref[head // repeat_by, chunk - 1].astype(F32)
            fresh_ref[head, part_of(chunk), :] = fresh
            state[head] = faded + mul(turned * tail[pack : pack + 1, :], fresh)
        outgoing.append(
            pltpu.make_async_copy(
                fresh_ref.at[:, pl.ds(chunk * CHUNK, CHUNK)],
                fresh_hbm.at[:, pl.ds(chunk * CHUNK, CHUNK)],
                out_sem.at[chunk],
            )
        )
        outgoing[-1].start()
    outgoing.append(pltpu.make_async_copy(starts_ref, starts_hbm, out_sem.at[chunks]))
    outgoing[-1].start()
    for head in range(heads):
        pairs_ref[head] = state[head].astype(BF16)
    for copy in outgoing:
        copy.wait()


def local_kernel(
    query_ref, query_before, query_taps, first_unit, later_unit, decay_ref, fresh_ref, starts_ref,
    gate_ref, gain_ref, parts_ref, gated_ref, padded,
):
    length, width = query_ref.shape
    chunks = length // CHUNK
    key_heads = width // DK
    heads = fresh_ref.shape[0]
    repeat_by = heads // key_heads

    rows, cols = square_iotas()
    within = rows >= cols
    fade = log_fades(chunk_rows(decay_ref, heads, range(chunks)))
    columns = as_columns((fade, jnp.exp(fade)))
    padded[5:8, :] = query_before[...].astype(F32)
    padded[8 : 8 + length, :] = query_ref[...].astype(F32)
    query = conv_silu(padded, 5, length, query_taps).astype(BF16)
    for head in range(heads):
        gate = gate_ref[:, head_of(head)].astype(F32)
        gated_ref[:, head_of(head)] = (gate * sigmoid(gate) * gain_ref[...]).astype(BF16)
    for chunk in range(chunks):
        part = part_of(chunk)
        for j in range(key_heads):
            own = head_of(j)
            unit = first_unit[:, own] if chunk == 0 else later_unit[part_of(chunk - 1), own]
            inner = lax.dot_general(
                query[part, own], unit, (((1,), (1,)), ((), ())), preferred_element_type=F32
            )
            for head in range(j * repeat_by, (j + 1) * repeat_by):
                pack = chunk * heads + head
                gap = columns[:, pack : pack + 1] - fade[pack : pack + 1, :]
                scores = inner * jnp.exp(jnp.where(within, gap, -1e30))
                grown = columns[:, chunks * heads + pack : chunks * heads + pack + 1]
                if chunk == 0:
                    carried = jnp.concatenate(
                        [jnp.zeros((CHUNK, DV), F32), grown * query[part, own].astype(F32)], 1
                    )
                else:
                    carried = grown * mul(query[part, own], starts_ref[head, chunk - 1])
                parts_ref[head, part, :] = (carried + mul(scores, fresh_ref[head, part, :])).astype(BF16)


def columns_of(rows, width, first=0):
    return pl.BlockSpec((rows, width), lambda step: (0, step + first))


def in_vmem(mib):
    return pltpu.CompilerParams(vmem_limit_bytes=mib * 1024 * 1024)


def local_steps(raws, before, taps, beta_logit, decay_logit, gate_raw, norm_gain):
    length = raws[0].shape[0]
    key_heads = raws[0].shape[1] // DK
    value_heads = raws[2].shape[1] // DV
    repeat_by = value_heads // key_heads
    chunks = length // CHUNK
    beta, decay = beta_logit.T, decay_logit.T
    work = CHUNK * length * DV * value_heads
    hbm = pl.BlockSpec(memory_space=pltpu.HBM)

    def split(each):
        heads = each * repeat_by
        held = max(heads, math.gcd(8, value_heads))
        of_heads = lambda *shape: pl.BlockSpec((heads,) + shape, lambda step: (step,) + (0,) * len(shape))
        logits = pl.BlockSpec((held, length), lambda step: (step * heads // held, 0))
        return key_heads // each, each * DK, heads * DV, of_heads, logits

    each = math.gcd(4, key_heads)
    steps, narrow, wide, of_heads, logits = split(each)
    later = length - CHUNK
    solved, later_unit, turned = pl.pallas_call(
        later_kernel,
        grid=(steps,),
        in_specs=[
            columns_of(length, narrow), columns_of(length, wide),
            columns_of(4, narrow), columns_of(4, wide), logits, logits,
        ],
        out_specs=[
            of_heads(later, DV + DK), columns_of(later, narrow),
            pl.BlockSpec((each, chunks - 1, DK, CHUNK), lambda step: (step, 0, 0, 0)),
        ],
        out_shape=[
            jax.ShapeDtypeStruct((value_heads, later, DV + DK), BF16),
            jax.ShapeDtypeStruct((later, key_heads * DK), BF16),
            jax.ShapeDtypeStruct((key_heads, chunks - 1, DK, CHUNK), BF16),
        ],
        scratch_shapes=[pltpu.VMEM((later + 16, narrow), F32), pltpu.VMEM((later + 16, wide), F32)],
        compiler_params=in_vmem(60),
        cost_estimate=pl.CostEstimate(flops=30 * work, bytes_accessed=0, transcendentals=0),
        name="later",
    )(raws[1], raws[2], taps[1], taps[2], beta, decay)

    narrow, wide = key_heads * DK, value_heads * DV
    whole = lambda shape, *at: pl.BlockSpec(shape, lambda step: at or (0,) * len(shape))
    pairs, first_unit, fresh, starts = pl.pallas_call(
        states_kernel,
        grid=(1,),
        in_specs=[
            whole((CHUNK, narrow)), whole((CHUNK, wide)),
            whole((3, narrow), 0, repeat_by + 1), whole((3, wide)),
            whole(taps[1].shape), whole(taps[2].shape), whole(beta.shape), whole(decay.shape),
            hbm, hbm,
        ],
        out_specs=[whole((value_heads, DK, DV + DK)), whole((CHUNK, narrow)), hbm, hbm],
        out_shape=[
            jax.ShapeDtypeStruct((value_heads, DK, DV + DK), BF16),
            jax.ShapeDtypeStruct((CHUNK, narrow), BF16),
            jax.ShapeDtypeStruct((value_heads, length, DV + DK), BF16),
            jax.ShapeDtypeStruct((value_heads, chunks - 1, DK, DV + DK), BF16),
        ],
        scratch_shapes=[
            pltpu.VMEM((8 + CHUNK, narrow), F32),
            pltpu.VMEM((8 + CHUNK, wide), F32),
            pltpu.VMEM(solved.shape, BF16),
            pltpu.VMEM(turned.shape, BF16),
            pltpu.VMEM((value_heads, length, DV + DK), BF16),
            pltpu.VMEM((value_heads, chunks - 1, DK, DV + DK), BF16),
            pltpu.SemaphoreType.DMA((2,)),
            pltpu.SemaphoreType.DMA((chunks + 1,)),
        ],
        compiler_params=in_vmem(54),
        cost_estimate=pl.CostEstimate(flops=20 * work, bytes_accessed=0, transcendentals=0),
        name="states",
    )(raws[1], raws[2], before, before, taps[1], taps[2], beta, decay, solved, turned)
    gain = norm_gain.reshape(1, DV)

    def local():
        steps, narrow, wide, of_heads, logits = split(math.gcd(2, key_heads))
        return pl.pallas_call(
            local_kernel,
            grid=(steps,),
            in_specs=[
                columns_of(length, narrow), columns_of(3, narrow, repeat_by * steps), columns_of(4, narrow),
                columns_of(CHUNK, narrow), columns_of(later, narrow), logits,
                of_heads(length, DV + DK), of_heads(chunks - 1, DK, DV + DK),
                columns_of(length, wide), whole(gain.shape),
            ],
            out_specs=[of_heads(length, DV + DK), columns_of(length, wide)],
            out_shape=[
                jax.ShapeDtypeStruct((value_heads, length, DV + DK), BF16),
                jax.ShapeDtypeStruct(gate_raw.shape, BF16),
            ],
            scratch_shapes=[pltpu.VMEM((8 + length, narrow), F32)],
            compiler_params=in_vmem(40),
            cost_estimate=pl.CostEstimate(flops=12 * work, bytes_accessed=0, transcendentals=0),
            name="local",
        )(raws[0], before, taps[0], first_unit, later_unit, decay, fresh, starts, gate_raw, gain)

    return pairs, local


def prefix_kernel(pairs_ref, prefix_ref, total_ref):
    count, heads = pairs_ref.shape[:2]
    running = [None] * heads
    for hop in range(count):
        for head in range(heads):
            now = pairs_ref[hop, head]
            if hop == 0:
                rows = lax.broadcasted_iota(jnp.int32, (DK, DV + DK), 0)
                cols = lax.broadcasted_iota(jnp.int32, (DK, DV + DK), 1)
                prefix_ref[hop, head] = jnp.where(cols == rows + DV, 1.0, 0.0).astype(BF16)
                running[head] = now.astype(F32)
            else:
                before = running[head].astype(BF16)
                prefix_ref[hop, head] = before
                own = jnp.concatenate([now[:, :DV].astype(F32), jnp.zeros((DK, DK), F32)], 1)
                running[head] = own + mul(now[:, DV:], before)
    for head in range(heads):
        total_ref[head] = running[head][:, : total_ref.shape[2]].astype(BF16)


def apply_kernel(prefix_ref, start_ref, starts_ref):
    count, heads = prefix_ref.shape[:2]
    for hop in range(count):
        for head in range(heads):
            starts_ref[hop, head] = (
                prefix_ref[hop, head, :, :DV].astype(F32)
                + mul(prefix_ref[hop, head, :, DV:], start_ref[head])
            ).astype(BF16)


def shifted(value, axis, by):
    count = lax.axis_size(axis)
    return lax.ppermute(value, axis, [(i, i + by) for i in range(count - by)])


def group_start(total, axis, group):
    groups = lax.axis_size(axis) // group
    running = shifted(total, axis, group)
    by = 1
    while by < groups - 1:
        earlier = shifted(running, axis, by * group)
        product = jnp.einsum("bkl,blv->bkv", running[..., DV:], earlier, preferred_element_type=F32)
        own = jnp.pad(running[..., :DV], ((0, 0), (0, 0), (0, DK)))
        running = (product + own.astype(F32)).astype(BF16)
        by *= 2
    return running[..., :DV]


def starts_of(pairs, axis, beside):
    size = lax.axis_size(axis)
    heads = pairs.shape[0]
    group = math.gcd(math.gcd(size, heads), GROUP)
    groups = [[g * group + i for i in range(group)] for g in range(size // group)]
    each = heads // group
    wide = DV if size // group == 2 else DV + DK
    by_head = lax.all_to_all(pairs, axis, 0, 0, axis_index_groups=groups, tiled=True)
    by_head, done = lax.optimization_barrier((by_head, beside()))
    prefix, total = pl.pallas_call(
        prefix_kernel,
        out_shape=[
            jax.ShapeDtypeStruct((group, each, DK, DV + DK), BF16),
            jax.ShapeDtypeStruct((each, DK, wide), BF16),
        ],
        compiler_params=in_vmem(16),
        name="prefix",
    )(by_head.reshape(group, each, DK, DV + DK))
    starts = pl.pallas_call(
        apply_kernel,
        out_shape=jax.ShapeDtypeStruct((group, each, DK, DV), BF16),
        compiler_params=in_vmem(16),
        name="apply",
    )(prefix, group_start(total, axis, group))
    starts = lax.all_to_all(
        starts.reshape(heads, DK, DV), axis, 0, 0, axis_index_groups=groups, tiled=True
    )
    return starts, done


def project_kernel(
    place_ref, starts_ref, parts_hbm, gated_hbm, weight_hbm, away_ref, own_ref,
    parts_ref, gated_ref, weight_ref, total, in_sem,
):
    heads, length = parts_ref.shape[:2]
    depth, width = weight_ref.shape
    each = min(HEADS_AT_ONCE, heads)
    block = min(512, width)
    groups = heads // each
    copies = []
    for g in range(groups):
        here, lanes = pl.ds(g * each, each), pl.ds(g * each * DV, each * DV)
        copies.append(
            [
                pltpu.make_async_copy(parts_hbm.at[here], parts_ref.at[here], in_sem.at[0, g]),
                pltpu.make_async_copy(gated_hbm.at[:, lanes], gated_ref.at[:, lanes], in_sem.at[1, g]),
                pltpu.make_async_copy(weight_hbm.at[lanes], weight_ref.at[lanes], in_sem.at[2, g]),
            ]
        )
        for copy in copies[g]:
            copy.start()
    for g in range(groups):
        copies[g][0].wait()
        copies[g][1].wait()
        normed = []
        for head in range(g * each, (g + 1) * each):
            core = parts_ref[head, :, :DV].astype(F32) + mul(
                parts_ref[head, :, DV:], starts_ref[head]
            )
            scale = lax.rsqrt(jnp.mean(core * core, -1, keepdims=True) + EPSILON)
            normed.append((core * scale * gated_ref[:, head_of(head)].astype(F32)).astype(BF16))
        normed = jnp.concatenate(normed, 1)
        copies[g][2].wait()
        for at in range(0, width, block):
            added = jnp.dot(
                normed, weight_ref[g * each * DV : (g + 1) * each * DV, at : at + block],
                preferred_element_type=F32,
            )
            if g > 0:
                added = added + total[:, at : at + block]
            if g < groups - 1:
                total[:, at : at + block] = added
            elif own_ref is None:
                away_ref[:, at : at + block] = added.astype(BF16)
            else:
                first = place_ref[0] == 0
                low, high = added[: length // 2], added[length // 2 :]
                own_ref[:, at : at + block] = jnp.where(first, low, high).astype(BF16)
                away_ref[:, at : at + block] = jnp.where(first, high, low).astype(BF16)


def whole_kernel(place_ref, starts_ref, parts_hbm, gated_hbm, weight_hbm, out_ref, *scratch):
    project_kernel(place_ref, starts_ref, parts_hbm, gated_hbm, weight_hbm, out_ref, None, *scratch)


def projected(parts, starts, gated, out_weight, axis):
    heads, length = parts.shape[:2]
    depth, width = out_weight.shape
    halves = lax.axis_size(axis) == 2
    hbm = pl.BlockSpec(memory_space=pltpu.HBM)
    vmem = pl.BlockSpec(memory_space=pltpu.VMEM)
    here = lax.axis_index(axis).astype(jnp.int32).reshape(1)
    out = jax.ShapeDtypeStruct((length // 2 if halves else length, width), BF16)
    partial = pl.pallas_call(
        project_kernel if halves else whole_kernel,
        in_specs=[pl.BlockSpec(memory_space=pltpu.SMEM), vmem, hbm, hbm, hbm],
        out_specs=[vmem, vmem] if halves else vmem,
        out_shape=[out, out] if halves else out,
        scratch_shapes=[
            pltpu.VMEM(parts.shape, BF16),
            pltpu.VMEM(gated.shape, BF16),
            pltpu.VMEM(out_weight.shape, BF16),
            pltpu.VMEM((length, width), F32),
            pltpu.SemaphoreType.DMA((3, heads // min(HEADS_AT_ONCE, heads))),
        ],
        compiler_params=in_vmem(40),
        name="project",
    )(here, starts, parts, gated, out_weight)
    if not halves:
        return lax.psum_scatter(partial, axis, scatter_dimension=0, tiled=True)
    away, own = partial
    other = lax.ppermute(away, axis, [(0, 1), (1, 0)])
    return (own.astype(F32) + other.astype(F32)).astype(BF16)


def tails_kernel(value_hbm, query_hbm, key_hbm, out_ref, value_ref, query_ref, key_ref, sem):
    pairs = ((value_hbm, value_ref), (query_hbm, query_ref), (key_hbm, key_ref))
    copies = [
        pltpu.make_async_copy(source.at[pl.ds(source.shape[0] - 16, 16)], held, sem.at[i])
        for i, (source, held) in enumerate(pairs)
    ]
    for copy in copies:
        copy.start()
    at = 0
    for copy, (_, held) in zip(copies, pairs):
        copy.wait()
        width = held.shape[1]
        out_ref[:, at : at + width] = held[...].astype(F32)[13:16].astype(BF16)
        at += width


def tails(raws):
    order = (raws[2], raws[0], raws[1])
    width = sum(raw.shape[1] for raw in order)
    return pl.pallas_call(
        tails_kernel,
        in_specs=[pl.BlockSpec(memory_space=pltpu.HBM)] * 3,
        out_shape=jax.ShapeDtypeStruct((3, width), BF16),
        scratch_shapes=[pltpu.VMEM((16, raw.shape[1]), BF16) for raw in order]
        + [pltpu.SemaphoreType.DMA((3,))],
        compiler_params=in_vmem(60),
        name="tails",
    )(*order)


def shards(
    query_raw, key_raw, value_raw, gate_raw, query_taps, key_taps, value_taps,
    beta_logit, decay_logit, norm_gain, out_weight,
):
    raws = (query_raw, key_raw, value_raw)
    before = shifted(tails(raws), "seq", 1)
    pairs, local = local_steps(
        raws, before, (query_taps, key_taps, value_taps), beta_logit, decay_logit, gate_raw, norm_gain
    )
    starts, (parts, gated) = starts_of(pairs, "seq", local)
    return projected(parts, starts, gated, out_weight, "head")


def solution(mesh):
    placed = (
        P("seq", "head"), P("seq", "head"), P("seq", "head"), P("seq", "head"),
        P(None, "head"), P(None, "head"), P(None, "head"),
        P("seq", "head"), P("seq", "head"), P(), P("head", None),
    )
    return jax.shard_map(
        shards, mesh=mesh, in_specs=placed, out_specs=P(("seq", "head"), None), check_vma=False
    )
```

time: 92.8 us -> 80.8 us (0.87)
  Pallas kernels: 49.4 us -> 37 us
  local copies, waits for them, and re-layouts: 3.8 us -> 10.8 us
  waiting for transfers between devices: 17.1 us -> 11.8 us
  other arithmetic: 2.28 us -> 1.15 us
    unnamed x8 -> x30, local copies, waits for them, and re-layouts: 2.96 us -> 10.8 us
    pallas_call x4, Pallas kernels: 34.8 us -> 28.4 us  [the longest x1 10.1 us: local_steps(): pl.pallas_call(later_kernel, grid=(steps,), in_specs=[columns_of(length,...]
    all_to_all x1, waiting for transfers between devices: 4.55 us -> 0.01 us  [starts_of(): lax.all_to_all(pairs, axis, 0, 0, axis_index_groups=groups, tiled=True)]
    pallas_call x1, Pallas kernels: 9.02 us -> 6.41 us  [local(): pl.pallas_call(local_kernel, grid=(steps,), in_specs=[columns_of(length,...]
    ppermute x1, waiting for transfers between devices: 0.01 us -> 2.27 us  [projected(): other = lax.ppermute(away, axis, [(0, 1), (1, 0)])]
    pallas_call x1, Pallas kernels: 3.24 us -> 1.14 us  [starts_of(): pl.pallas_call(prefix_kernel, out_shape=[jax.ShapeDtypeStruct((group, eac...]
    all_to_all x1, starting transfers between devices: 3.74 us -> 5.67 us  [starts_of(): lax.all_to_all(starts.reshape(heads, DK, DV), axis, 0, 0, axis_index_grou...]
    ppermute x2, waiting for transfers between devices: 3.78 us -> 1.89 us  [shifted(): return lax.ppermute(value, axis, [(i, i + by) for i in range(count - by)])]
  transfers between devices with their start and end apart: 5 -> 5, of which waited for: 4 -> 3; matrix products, arithmetic and copies ran while one was open for 0% -> 0% of each run, Pallas kernels for 18% -> 21%
where the time goes in v1:
time: 80.8 us; the launch traced here: 80.2 us
  Pallas kernels  37 us (46%)
  starting transfers between devices  19.2 us (24%)
  waiting for transfers between devices  11.8 us (15%)
  local copies, waits for them, and re-layouts  10.8 us (13%)
  other arithmetic  1.15 us (1%)
    unnamed x30, local copies, waits for them, and re-layouts  10.8 us
    pallas_call x1, Pallas kernels, local_steps(): pl.pallas_call(later_kernel, grid=(steps,), in_specs=[columns_of(length,...  10.1 us
    pallas_call x1, Pallas kernels, local_steps(): pl.pallas_call(states_kernel, grid=(1,), in_specs=[whole((CHUNK, narrow))...  9.61 us
    ppermute x2, starting transfers between devices, shifted(): return lax.ppermute(value, axis, [(i, i + by) for i in range(count - by)])  8.55 us
    all_to_all x1, waiting for transfers between devices, starts_of(): lax.all_to_all(starts.reshape(heads, DK, DV), axis, 0, 0, axis_index_grou...  7.67 us
    pallas_call x1, Pallas kernels, projected(): pl.pallas_call(project_kernel if halves else whole_kernel, in_specs=[pl.B...  7.2 us
    pallas_call x1, Pallas kernels, local(): pl.pallas_call(local_kernel, grid=(steps,), in_specs=[columns_of(length,...  6.41 us
    all_to_all x1, starting transfers between devices, starts_of(): lax.all_to_all(starts.reshape(heads, DK, DV), axis, 0, 0, axis_index_grou...  5.67 us
  transfers between devices with their start and end apart: 5, of which 3 were waited for; matrix products, arithmetic and copies ran while one was open for 0% of the time, Pallas kernels for 21%

profile of v1, /device:TPU:0, one launch (start us, length us, event | category | flops | bytes accessed | tf_op | source)
XLA Modules:
  0.0 80.2 jit_solution(13036497104612935523)
XLA Ops:
  0.0 1.5 %tails.1 = bf16[3,4096]{1,0:T(4,128)(2,1)} custom-call(bf16[384,2048]{1,0:T(8,128)(2,1)} %value_ref.3, bf16[384,1024]{1,0:T(8,128)(2,1)} %query_ref.1, bf16[384,1024]{1,0:T(8,128)(2,1)} %key_ref.3), custom_call_target="tpu_custom_call" | custom-call | tf_op jit(solution)/shard_map/tails/pallas_call | solution.py:600
  1.5 4.8 %collective-permute-start = (bf16[3,4096]{1,0:T(4,128)(2,1)}, bf16[3,4096]{1,0:T(4,128)(2,1)S(1)}, u32[]{:S(2)}, u32[]{:S(2)}) collective-permute-start(bf16[3,4096]{1,0:T(4,128)(2,1)} %tails.1), channel_id=1, source_target_pairs={{0,2},{2,4},{4,6},{6,8},{8,10},{10,12},{12,14},{14,16},{16,18},{18... | collective-permute-start | bytes 73736 | tf_op jit(solution)/shard_map/ppermute | solution.py:450
  6.4 10.1 %later.1 = (bf16[16,256,256]{2,1,0:T(8,128)(2,1)}, bf16[256,1024]{1,0:T(8,128)(2,1)}, bf16[8,2,128,128]{3,2,1,0:T(8,128)(2,1)}) custom-call(bf16[384,1024]{1,0:T(8,128)(2,1)} %key_ref.3, bf16[384,2048]{1,0:T(8,128)(2,1)} %value_ref.3, f32[4,1024]{1,0:T(4,128)} %key_taps.3, f32[4,2048]{1,0:T(4,128)} %value_taps.3, f32[16,384]{1,0:T(8,128)} %bitcast.11, ...), custom_call_target="tpu_custom_call" | custom-call | flops 3019898880 | tf_op jit(solution)/shard_map/later/pallas_call | solution.py:337
  16.4 0.0 collective-permute-done.key_before.value_before.query_before
  16.5 0.0 copy-start.10
  16.5 0.6 copy-done.10
  17.1 0.0 copy-start.5
  17.1 9.6 %states.1 = (bf16[16,128,256]{2,1,0:T(8,128)(2,1)}, bf16[128,1024]{1,0:T(8,128)(2,1)}, bf16[16,384,256]{2,1,0:T(8,128)(2,1)}, bf16[16,2,128,256]{3,2,1,0:T(8,128)(2,1)}) custom-call(bf16[384,1024]{1,0:T(8,128)(2,1)} %key_ref.3, bf16[384,2048]{1,0:T(8,128)(2,1)} %value_ref.3, bf16[3,4096]{1,0:T(4,128)(2,1)} %copy-done.10, bf16[3,4096]{1,0:T(4,128)(2,1)} %copy-done.10, ...), custom_call_target="tpu_custom_call" | custom-call | flops 2013265920 | tf_op jit(solution)/shard_map/states/pallas_call | solution.py:361
  26.7 0.0 copy-start.1
  26.7 0.0 copy-start.11
  26.7 0.0 copy-start.12
  26.7 0.0 copy-start.13
  26.7 0.0 copy-start.14
  26.7 4.9 %all-to-all-start = ((bf16[16,128,256]{2,1,0:T(8,128)(2,1)}), bf16[16,128,256]{2,1,0:T(8,128)(2,1)S(1)}, u32[]{:S(2)}, u32[]{:S(2)}) async-start(bf16[16,128,256]{2,1,0:T(8,128)(2,1)} %get-tuple-element.23), calls=%async_computation | async-start | bytes 2097152 | tf_op jit(solution)/shard_map/all_to_all | solution.py:473
  31.6 0.0 copy-done.5
  31.6 0.0 copy-done.1
  31.6 0.0 copy-done.11
  31.7 0.0 copy-done.12
  31.7 0.0 copy-done.13
  31.7 0.0 copy-done.14
  31.7 0.0 copy-start
  31.7 1.9 %copy-done = bf16[16,384,256]{2,1,0:T(8,128)(2,1)S(1)} copy-done((bf16[16,384,256]{2,1,0:T(8,128)(2,1)S(1)}, bf16[16,384,256]{2,1,0:T(8,128)(2,1)}, u32[]{:S(2)}) %copy-start) | copy-done | bytes 3145752
  33.6 0.0 copy-start.4
  33.6 1.6 %copy-done.4 = bf16[16,2,128,256]{3,2,1,0:T(8,128)(2,1)S(1)} copy-done((bf16[16,2,128,256]{3,2,1,0:T(8,128)(2,1)S(1)}, bf16[16,2,128,256]{3,2,1,0:T(8,128)(2,1)}, u32[]{:S(2)}) %copy-start.4) | copy-done | bytes 2097176
  35.2 0.0 copy-start.8
  35.2 1.0 %copy-done.8 = bf16[256,1024]{1,0:T(8,128)(2,1)S(1)} copy-done((bf16[256,1024]{1,0:T(8,128)(2,1)S(1)}, bf16[256,1024]{1,0:T(8,128)(2,1)}, u32[]{:S(2)}) %copy-start.8) | copy-done | bytes 524312
  36.2 0.0 copy-start.9
  36.2 0.9 %copy-done.9 = bf16[128,1024]{1,0:T(8,128)(2,1)S(1)} copy-done((bf16[128,1024]{1,0:T(8,128)(2,1)S(1)}, bf16[128,1024]{1,0:T(8,128)(2,1)}, u32[]{:S(2)}) %copy-start.9) | copy-done | bytes 262168
  37.2 6.4 %local.1 = (bf16[16,384,256]{2,1,0:T(8,128)(2,1)S(1)}, bf16[384,2048]{1,0:T(8,128)(2,1)S(1)}) custom-call(bf16[384,1024]{1,0:T(8,128)(2,1)S(1)} %copy-done.1, bf16[3,4096]{1,0:T(4,128)(2,1)S(1)} %copy-done.11, f32[4,1024]{1,0:T(4,128)S(1)} %copy-done.13, bf16[128,1024]{1,0:T(8,128)(2,1)S(1)} %copy-done.9, bf16[256,1024]{1,0:T(8,128)(2,1)S(1)} %copy-done.8, ...), custom_call_target="tpu_custom_call" | custom-call | flops 1207959552 | tf_op jit(solution)/shard_map/local/pallas_call | solution.py:395
  43.6 0.0 copy-start.2
  43.6 1.6 %copy-done.2 = bf16[16,384,256]{2,1,0:T(8,128)(2,1)} copy-done((bf16[16,384,256]{2,1,0:T(8,128)(2,1)}, bf16[16,384,256]{2,1,0:T(8,128)(2,1)S(1)}, u32[]{:S(2)}) %copy-start.2) | copy-done | bytes 3145752
  45.2 0.0 copy-start.6
  45.2 1.2 %copy-done.6 = bf16[384,2048]{1,0:T(8,128)(2,1)} copy-done((bf16[384,2048]{1,0:T(8,128)(2,1)}, bf16[384,2048]{1,0:T(8,128)(2,1)S(1)}, u32[]{:S(2)}) %copy-start.6) | copy-done | bytes 1572888
  46.4 0.0 all-to-all-done
  46.4 1.1 %prefix.1 = (bf16[8,2,128,256]{3,2,1,0:T(8,128)(2,1)S(1)}, bf16[2,128,128]{2,1,0:T(8,128)(2,1)S(1)}) custom-call(bf16[8,2,128,256]{3,2,1,0:T(8,128)(2,1)S(1)} %bitcast.6), custom_call_target="tpu_custom_call" | custom-call | tf_op jit(solution)/shard_map/prefix/pallas_call | solution.py:475
  47.5 0.0 copy-start.7
  47.5 3.7 %collective-permute-start.1 = (bf16[2,128,128]{2,1,0:T(8,128)(2,1)S(1)}, bf16[2,128,128]{2,1,0:T(8,128)(2,1)S(1)}, u32[]{:S(2)}, u32[]{:S(2)}) collective-permute-start(bf16[2,128,128]{2,1,0:T(8,128)(2,1)S(1)} %get-tuple-element.32), channel_id=1, source_target_pairs={{0,16},{2,18},{4,20},{6,22},{8,24},{10,26},{12,28},{14,30},{1,17},... | collective-permute-start | bytes 196616 | tf_op jit(solution)/shard_map/ppermute | solution.py:450
  51.3 1.9 %collective-permute-done.1.start_ref = bf16[2,128,128]{2,1,0:T(8,128)(2,1)S(1)} collective-permute-done((bf16[2,128,128]{2,1,0:T(8,128)(2,1)S(1)}, bf16[2,128,128]{2,1,0:T(8,128)(2,1)S(1)}, u32[]{:S(2)}, u32[]{:S(2)}) %collective-permute-start.1) | collective-permute-done | bytes 65568 | tf_op jit(solution)/shard_map/ppermute | solution.py:450
  53.1 1.1 %apply.1 = bf16[8,2,128,128]{3,2,1,0:T(8,128)(2,1)} custom-call(bf16[8,2,128,256]{3,2,1,0:T(8,128)(2,1)S(1)} %get-tuple-element.31.prefix_ref, bf16[2,128,128]{2,1,0:T(8,128)(2,1)S(1)} %collective-permute-done.1.start_ref), custom_call_target="tpu_custom_call" | custom-call | tf_op jit(solution)/shard_map/apply/pallas_call | solution.py:484
  54.2 5.7 %all-to-all-start.1 = ((bf16[16,128,128]{2,1,0:T(8,128)(2,1)}), bf16[16,128,128]{2,1,0:T(8,128)(2,1)S(1)}, u32[]{:S(2)}, u32[]{:S(2)}) async-start(bf16[16,128,128]{2,1,0:T(8,128)(2,1)} %bitcast.5), calls=%async_computation.1 | async-start | bytes 1048576 | tf_op jit(solution)/shard_map/all_to_all | solution.py:490
  59.9 7.7 %all-to-all-done.1.starts_ref = bf16[16,128,128]{2,1,0:T(8,128)(2,1)S(1)} async-done(((bf16[16,128,128]{2,1,0:T(8,128)(2,1)}), bf16[16,128,128]{2,1,0:T(8,128)(2,1)S(1)}, u32[]{:S(2)}, u32[]{:S(2)}) %all-to-all-start.1) | async-done | bytes 524320 | tf_op jit(solution)/shard_map/all_to_all | solution.py:490
  67.6 0.0 copy-done.7
  67.6 0.0 copy-start.3
  67.6 1.9 %copy-done.3 = bf16[16,384,256]{2,1,0:T(8,128)(2,1)S(1)} copy-done((bf16[16,384,256]{2,1,0:T(8,128)(2,1)S(1)}, bf16[16,384,256]{2,1,0:T(8,128)(2,1)}, u32[]{:S(2)}) %copy-start.3) | copy-done | bytes 3145752
  69.5 7.2 %project.1 = (bf16[192,2048]{1,0:T(8,128)(2,1)S(1)}, bf16[192,2048]{1,0:T(8,128)(2,1)S(1)}) custom-call(s32[1]{0:T(128)} %bitcast.place_ref, bf16[16,128,128]{2,1,0:T(8,128)(2,1)S(1)} %all-to-all-done.1.starts_ref, bf16[16,384,256]{2,1,0:T(8,128)(2,1)S(1)} %copy-done.3, bf16[384,2048]{1,0:T(8,128)(2,1)S(1)} %copy-done.7, bf16[2048,2048]{1,0:T(8,128)(2,1)} %weight_hbm.1), custom_call_target="tpu_custom_call" | custom-call | tf_op jit(solution)/shard_map/project/pallas_call | solution.py:559
  76.7 0.1 collective-permute-start.2
  76.8 2.3 %collective-permute-done.2 = bf16[192,2048]{1,0:T(8,128)(2,1)S(1)} collective-permute-done((bf16[192,2048]{1,0:T(8,128)(2,1)S(1)}, bf16[192,2048]{1,0:T(8,128)(2,1)S(1)}, u32[]{:S(2)}, u32[]{:S(2)}) %collective-permute-start.2) | collective-permute-done | bytes 786464 | tf_op jit(solution)/shard_map/ppermute | solution.py:577
  79.0 1.2 %add_convert_fusion = bf16[192,2048]{1,0:T(8,128)(2,1)} fusion(bf16[192,2048]{1,0:T(8,128)(2,1)S(1)} %collective-permute-done.2, bf16[192,2048]{1,0:T(8,128)(2,1)S(1)} %get-tuple-element.35), kind=kLoop, calls=%fused_computation | loop fusion | flops 1572864 | bytes 2359296 | tf_op jit(solution)/shard_map/convert_element_type | solution.py:578
Async XLA Ops:
  1.5 14.9 %collective-permute-start = (bf16[3,4096]{1,0:T(4,128)(2,1)}, bf16[3,4096]{1,0:T(4,128)(2,1)S(1)}, u32[]{:S(2)}, u32[]{:S(2)}) collective-permute-start(bf16[3,4096]{1,0:T(4,128)(2,1)} %tails.1), channel_id=1, source_target_pairs={{0,2},{2,4},{4,6},{6,8},{8,10},{10,12},{12,14},{14,16},{16,18},{18... | collective-permute-start | bytes 73736 | tf_op jit(solution)/shard_map/ppermute | solution.py:450
  16.5 0.6 copy-start.10
  17.1 14.6 %copy-start.5 = (bf16[384,2048]{1,0:T(8,128)(2,1)S(1)}, bf16[384,2048]{1,0:T(8,128)(2,1)}, u32[]{:S(2)}) copy-start(bf16[384,2048]{1,0:T(8,128)(2,1)} %gate_ref.1) | copy-start | bytes 4718596
  26.7 4.9 %copy-start.1 = (bf16[384,1024]{1,0:T(8,128)(2,1)S(1)}, bf16[384,1024]{1,0:T(8,128)(2,1)}, u32[]{:S(2)}) copy-start(bf16[384,1024]{1,0:T(8,128)(2,1)} %query_ref.1) | copy-start | bytes 2359300
  26.7 4.9 %copy-start.11 = (bf16[3,4096]{1,0:T(4,128)(2,1)S(1)}, bf16[3,4096]{1,0:T(4,128)(2,1)}, u32[]{:S(2)}) copy-start(bf16[3,4096]{1,0:T(4,128)(2,1)} %copy-done.10) | copy-start | bytes 73732
  26.7 4.9 %copy-start.12 = (f32[384,16]{0,1:T(8,128)S(1)}, f32[384,16]{0,1:T(8,128)}, u32[]{:S(2)}) copy-start(f32[384,16]{0,1:T(8,128)} %param.19) | copy-start | bytes 73732
  26.7 4.9 %copy-start.13 = (f32[4,1024]{1,0:T(4,128)S(1)}, f32[4,1024]{1,0:T(4,128)}, u32[]{:S(2)}) copy-start(f32[4,1024]{1,0:T(4,128)} %query_taps.1) | copy-start | bytes 49156
  26.7 4.9 %copy-start.14 = (f32[128]{0:T(128)S(1)}, f32[128]{0:T(128)}, u32[]{:S(2)}) copy-start(f32[128]{0:T(128)} %param.20) | copy-start | bytes 1540
  26.7 19.6 %all-to-all-start = ((bf16[16,128,256]{2,1,0:T(8,128)(2,1)}), bf16[16,128,256]{2,1,0:T(8,128)(2,1)S(1)}, u32[]{:S(2)}, u32[]{:S(2)}) async-start(bf16[16,128,256]{2,1,0:T(8,128)(2,1)} %get-tuple-element.23), calls=%async_computation | async-start | bytes 2097152 | tf_op jit(solution)/shard_map/all_to_all | solution.py:473
  31.7 1.9 %copy-start = (bf16[16,384,256]{2,1,0:T(8,128)(2,1)S(1)}, bf16[16,384,256]{2,1,0:T(8,128)(2,1)}, u32[]{:S(2)}) copy-start(bf16[16,384,256]{2,1,0:T(8,128)(2,1)} %get-tuple-element.26.fresh_ref) | copy-start | bytes 9437188
  33.6 1.6 %copy-start.4 = (bf16[16,2,128,256]{3,2,1,0:T(8,128)(2,1)S(1)}, bf16[16,2,128,256]{3,2,1,0:T(8,128)(2,1)}, u32[]{:S(2)}) copy-start(bf16[16,2,128,256]{3,2,1,0:T(8,128)(2,1)} %get-tuple-element.27.starts_ref) | copy-start | bytes 6291460
  35.2 1.0 %copy-start.8 = (bf16[256,1024]{1,0:T(8,128)(2,1)S(1)}, bf16[256,1024]{1,0:T(8,128)(2,1)}, u32[]{:S(2)}) copy-start(bf16[256,1024]{1,0:T(8,128)(2,1)} %get-tuple-element.25.later_unit) | copy-start | bytes 1572868
  36.2 0.9 %copy-start.9 = (bf16[128,1024]{1,0:T(8,128)(2,1)S(1)}, bf16[128,1024]{1,0:T(8,128)(2,1)}, u32[]{:S(2)}) copy-start(bf16[128,1024]{1,0:T(8,128)(2,1)} %get-tuple-element.24.first_unit) | copy-start | bytes 786436
  43.6 1.6 %copy-start.2 = (bf16[16,384,256]{2,1,0:T(8,128)(2,1)}, bf16[16,384,256]{2,1,0:T(8,128)(2,1)S(1)}, u32[]{:S(2)}) copy-start(bf16[16,384,256]{2,1,0:T(8,128)(2,1)S(1)} %get-tuple-element.33.parts_hbm) | copy-start | bytes 9437188
  45.2 1.2 %copy-start.6 = (bf16[384,2048]{1,0:T(8,128)(2,1)}, bf16[384,2048]{1,0:T(8,128)(2,1)S(1)}, u32[]{:S(2)}) copy-start(bf16[384,2048]{1,0:T(8,128)(2,1)S(1)} %get-tuple-element.34.gated_hbm) | copy-start | bytes 4718596
  47.5 20.0 %copy-start.7 = (bf16[384,2048]{1,0:T(8,128)(2,1)S(1)}, bf16[384,2048]{1,0:T(8,128)(2,1)}, u32[]{:S(2)}) copy-start(bf16[384,2048]{1,0:T(8,128)(2,1)} %copy-done.6) | copy-start | bytes 4718596
  47.5 5.6 %collective-permute-start.1 = (bf16[2,128,128]{2,1,0:T(8,128)(2,1)S(1)}, bf16[2,128,128]{2,1,0:T(8,128)(2,1)S(1)}, u32[]{:S(2)}, u32[]{:S(2)}) collective-permute-start(bf16[2,128,128]{2,1,0:T(8,128)(2,1)S(1)} %get-tuple-element.32), channel_id=1, source_target_pairs={{0,16},{2,18},{4,20},{6,22},{8,24},{10,26},{12,28},{14,30},{1,17},... | collective-permute-start | bytes 196616 | tf_op jit(solution)/shard_map/ppermute | solution.py:450
  54.2 13.3 %all-to-all-start.1 = ((bf16[16,128,128]{2,1,0:T(8,128)(2,1)}), bf16[16,128,128]{2,1,0:T(8,128)(2,1)S(1)}, u32[]{:S(2)}, u32[]{:S(2)}) async-start(bf16[16,128,128]{2,1,0:T(8,128)(2,1)} %bitcast.5), calls=%async_computation.1 | async-start | bytes 1048576 | tf_op jit(solution)/shard_map/all_to_all | solution.py:490
  67.6 1.9 %copy-start.3 = (bf16[16,384,256]{2,1,0:T(8,128)(2,1)S(1)}, bf16[16,384,256]{2,1,0:T(8,128)(2,1)}, u32[]{:S(2)}) copy-start(bf16[16,384,256]{2,1,0:T(8,128)(2,1)} %copy-done.2) | copy-start | bytes 9437188
  76.7 2.4 %collective-permute-start.2 = (bf16[192,2048]{1,0:T(8,128)(2,1)S(1)}, bf16[192,2048]{1,0:T(8,128)(2,1)S(1)}, u32[]{:S(2)}, u32[]{:S(2)}) collective-permute-start(bf16[192,2048]{1,0:T(8,128)(2,1)S(1)} %get-tuple-element.36), channel_id=1, source_target_pairs={{0,1},{1,0},{2,3},{3,2},{4,5},{5,4},{6,7},{7,6},{8,9},{9,8},{10,11... | collective-permute-start | bytes 2359304 | tf_op jit(solution)/shard_map/ppermute | solution.py:577

commit v2 on v1

--- a/solution.py
+++ b/solution.py
@@ -183,8 +183,8 @@
 def states_kernel(
     key_ref, value_ref, key_before, value_before, key_taps, value_taps, beta_ref, decay_ref,
     solved_hbm, turned_hbm,
-    pairs_ref, unit_ref, fresh_hbm, starts_hbm,
-    key_padded, value_padded, solved_ref, turned_ref, fresh_ref, starts_ref, in_sem, out_sem,
+    pairs_ref, unit_ref, fresh_ref, starts_ref,
+    key_padded, value_padded, solved_ref, turned_ref, in_sem,
 ):
     heads, length = decay_ref.shape
     chunks = length // CHUNK
@@ -222,7 +222,6 @@
     identity = jnp.where(rows == cols, 1.0, 0.0)
 
     state = [None] * heads
-    outgoing = []
     for chunk in range(chunks):
         if chunk == 1:
             for copy in incoming:
@@ -248,20 +247,8 @@
                 turned = turned_ref[head // repeat_by, chunk - 1].astype(F32)
             fresh_ref[head, part_of(chunk), :] = fresh
             state[head] = faded + mul(turned * tail[pack : pack + 1, :], fresh)
-        outgoing.append(
-            pltpu.make_async_copy(
-                fresh_ref.at[:, pl.ds(chunk * CHUNK, CHUNK)],
-                fresh_hbm.at[:, pl.ds(chunk * CHUNK, CHUNK)],
-                out_sem.at[chunk],
-            )
-        )
-        outgoing[-1].start()
-    outgoing.append(pltpu.make_async_copy(starts_ref, starts_hbm, out_sem.at[chunks]))
-    outgoing[-1].start()
     for head in range(heads):
         pairs_ref[head] = state[head].astype(BF16)
-    for copy in outgoing:
-        copy.wait()
 
 
 def local_kernel(
@@ -323,6 +310,7 @@
     beta, decay = beta_logit.T, decay_logit.T
     work = CHUNK * length * DV * value_heads
     hbm = pl.BlockSpec(memory_space=pltpu.HBM)
+    vmem = pl.BlockSpec(memory_space=pltpu.VMEM)
 
     def split(each):
         heads = each * repeat_by
@@ -367,7 +355,7 @@
             whole(taps[1].shape), whole(taps[2].shape), whole(beta.shape), whole(decay.shape),
             hbm, hbm,
         ],
-        out_specs=[whole((value_heads, DK, DV + DK)), whole((CHUNK, narrow)), hbm, hbm],
+        out_specs=[vmem] * 4,
         out_shape=[
             jax.ShapeDtypeStruct((value_heads, DK, DV + DK), BF16),
             jax.ShapeDtypeStruct((CHUNK, narrow), BF16),
@@ -379,12 +367,9 @@
             pltpu.VMEM((8 + CHUNK, wide), F32),
             pltpu.VMEM(solved.shape, BF16),
             pltpu.VMEM(turned.shape, BF16),
-            pltpu.VMEM((value_heads, length, DV + DK), BF16),
-            pltpu.VMEM((value_heads, chunks - 1, DK, DV + DK), BF16),
             pltpu.SemaphoreType.DMA((2,)),
-            pltpu.SemaphoreType.DMA((chunks + 1,)),
-        ],
-        compiler_params=in_vmem(54),
+        ],
+        compiler_params=in_vmem(52),
         cost_estimate=pl.CostEstimate(flops=20 * work, bytes_accessed=0, transcendentals=0),
         name="states",
     )(raws[1], raws[2], before, before, taps[1], taps[2], beta, decay, solved, turned)
@@ -407,7 +392,7 @@
                 jax.ShapeDtypeStruct(gate_raw.shape, BF16),
             ],
             scratch_shapes=[pltpu.VMEM((8 + length, narrow), F32)],
-            compiler_params=in_vmem(40),
+            compiler_params=in_vmem(24),
             cost_estimate=pl.CostEstimate(flops=12 * work, bytes_accessed=0, transcendentals=0),
             name="local",
         )(raws[0], before, taps[0], first_unit, later_unit, decay, fresh, starts, gate_raw, gain)
@@ -493,30 +478,13 @@
     return starts, done
 
 
-def project_kernel(
-    place_ref, starts_ref, parts_hbm, gated_hbm, weight_hbm, away_ref, own_ref,
-    parts_ref, gated_ref, weight_ref, total, in_sem,
-):
+def project_kernel(place_ref, starts_ref, parts_ref, gated_ref, weight_ref, away_ref, own_ref, total):
     heads, length = parts_ref.shape[:2]
-    depth, width = weight_ref.shape
+    width = weight_ref.shape[1]
     each = min(HEADS_AT_ONCE, heads)
     block = min(512, width)
     groups = heads // each
-    copies = []
     for g in range(groups):
-        here, lanes = pl.ds(g * each, each), pl.ds(g * each * DV, each * DV)
-        copies.append(
-            [
-                pltpu.make_async_copy(parts_hbm.at[here], parts_ref.at[here], in_sem.at[0, g]),
-                pltpu.make_async_copy(gated_hbm.at[:, lanes], gated_ref.at[:, lanes], in_sem.at[1, g]),
-                pltpu.make_async_copy(weight_hbm.at[lanes], weight_ref.at[lanes], in_sem.at[2, g]),
-            ]
-        )
-        for copy in copies[g]:
-            copy.start()
-    for g in range(groups):
-        copies[g][0].wait()
-        copies[g][1].wait()
         normed = []
         for head in range(g * each, (g + 1) * each):
             core = parts_ref[head, :, :DV].astype(F32) + mul(
@@ -525,7 +493,6 @@
             scale = lax.rsqrt(jnp.mean(core * core, -1, keepdims=True) + EPSILON)
             normed.append((core * scale * gated_ref[:, head_of(head)].astype(F32)).astype(BF16))
         normed = jnp.concatenate(normed, 1)
-        copies[g][2].wait()
         for at in range(0, width, block):
             added = jnp.dot(
                 normed, weight_ref[g * each * DV : (g + 1) * each * DV, at : at + block],
@@ -544,31 +511,24 @@
                 away_ref[:, at : at + block] = jnp.where(first, high, low).astype(BF16)
 
 
-def whole_kernel(place_ref, starts_ref, parts_hbm, gated_hbm, weight_hbm, out_ref, *scratch):
-    project_kernel(place_ref, starts_ref, parts_hbm, gated_hbm, weight_hbm, out_ref, None, *scratch)
+def whole_kernel(place_ref, starts_ref, parts_ref, gated_ref, weight_ref, out_ref, total):
+    project_kernel(place_ref, starts_ref, parts_ref, gated_ref, weight_ref, out_ref, None, total)
 
 
 def projected(parts, starts, gated, out_weight, axis):
-    heads, length = parts.shape[:2]
-    depth, width = out_weight.shape
+    length = parts.shape[1]
+    width = out_weight.shape[1]
     halves = lax.axis_size(axis) == 2
-    hbm = pl.BlockSpec(memory_space=pltpu.HBM)
     vmem = pl.BlockSpec(memory_space=pltpu.VMEM)
     here = lax.axis_index(axis).astype(jnp.int32).reshape(1)
     out = jax.ShapeDtypeStruct((length // 2 if halves else length, width), BF16)
     partial = pl.pallas_call(
         project_kernel if halves else whole_kernel,
-        in_specs=[pl.BlockSpec(memory_space=pltpu.SMEM), vmem, hbm, hbm, hbm],
+        in_specs=[pl.BlockSpec(memory_space=pltpu.SMEM)] + [vmem] * 4,
         out_specs=[vmem, vmem] if halves else vmem,
         out_shape=[out, out] if halves else out,
-        scratch_shapes=[
-            pltpu.VMEM(parts.shape, BF16),
-            pltpu.VMEM(gated.shape, BF16),
-            pltpu.VMEM(out_weight.shape, BF16),
-            pltpu.VMEM((length, width), F32),
-            pltpu.SemaphoreType.DMA((3, heads // min(HEADS_AT_ONCE, heads))),
-        ],
-        compiler_params=in_vmem(40),
+        scratch_shapes=[pltpu.VMEM((length, width), F32)],
+        compiler_params=in_vmem(24),
         name="project",
     )(here, starts, parts, gated, out_weight)
     if not halves:

time: 80.8 us -> 82.6 us (1.022)
  local copies, waits for them, and re-layouts: 10.8 us -> 15.3 us
  Pallas kernels: 37 us -> 34.2 us
    unnamed x30 -> x40, local copies, waits for them, and re-layouts: 10.8 us -> 15.3 us
    pallas_call x1, Pallas kernels: 7.2 us -> 4.6 us  [projected(): pl.pallas_call(project_kernel if halves else whole_kernel, in_specs=[pl.B...]
  transfers between devices with their start and end apart: 5 -> 5, of which waited for: 3 -> 3; matrix products, arithmetic and copies ran while one was open for 0% -> 0% of each run, Pallas kernels for 21% -> 20%
where the time goes in v2:
time: 82.6 us; the launch traced here: 81.9 us
  Pallas kernels  34.2 us (41%)
  starting transfers between devices  19.2 us (23%)
  local copies, waits for them, and re-layouts  15.3 us (19%)
  waiting for transfers between devices  11.8 us (14%)
  other arithmetic  1.15 us (1%)
    unnamed x40, local copies, waits for them, and re-layouts  15.3 us
    pallas_call x1, Pallas kernels, local_steps(): pl.pallas_call(later_kernel, grid=(steps,), in_specs=[columns_of(length,...  10.1 us
    pallas_call x1, Pallas kernels, local_steps(): pl.pallas_call(states_kernel, grid=(1,), in_specs=[whole((CHUNK, narrow))...  9.36 us
    ppermute x2, starting transfers between devices, shifted(): return lax.ppermute(value, axis, [(i, i + by) for i in range(count - by)])  8.55 us
    all_to_all x1, waiting for transfers between devices, starts_of(): lax.all_to_all(starts.reshape(heads, DK, DV), axis, 0, 0, axis_index_grou...  7.67 us
    pallas_call x1, Pallas kernels, local(): pl.pallas_call(local_kernel, grid=(steps,), in_specs=[columns_of(length,...  6.41 us
    all_to_all x1, starting transfers between devices, starts_of(): lax.all_to_all(starts.reshape(heads, DK, DV), axis, 0, 0, axis_index_grou...  5.67 us
    all_to_all x1, starting transfers between devices, starts_of(): lax.all_to_all(pairs, axis, 0, 0, axis_index_groups=groups, tiled=True)  4.87 us
  transfers between devices with their start and end apart: 5, of which 3 were waited for; matrix products, arithmetic and copies ran while one was open for 0% of the time, Pallas kernels for 20%

profile of v2, /device:TPU:0, one launch (start us, length us, event | category | flops | bytes accessed | tf_op | source)
XLA Modules:
  0.0 81.9 jit_solution(14335747148201973036)
XLA Ops:
  0.0 1.5 %tails.1 = bf16[3,4096]{1,0:T(4,128)(2,1)} custom-call(bf16[384,2048]{1,0:T(8,128)(2,1)} %value_ref.3, bf16[384,1024]{1,0:T(8,128)(2,1)} %query_ref.1, bf16[384,1024]{1,0:T(8,128)(2,1)} %key_ref.3), custom_call_target="tpu_custom_call" | custom-call | tf_op jit(solution)/shard_map/tails/pallas_call | solution.py:560
  1.5 4.8 %collective-permute-start = (bf16[3,4096]{1,0:T(4,128)(2,1)}, bf16[3,4096]{1,0:T(4,128)(2,1)S(1)}, u32[]{:S(2)}, u32[]{:S(2)}) collective-permute-start(bf16[3,4096]{1,0:T(4,128)(2,1)} %tails.1), channel_id=1, source_target_pairs={{0,2},{2,4},{4,6},{6,8},{8,10},{10,12},{12,14},{14,16},{16,18},{18... | collective-permute-start | bytes 73736 | tf_op jit(solution)/shard_map/ppermute | solution.py:435
  6.4 0.0 copy-start.9
  6.4 0.0 copy-start.13
  6.4 0.0 copy-start.16
  6.4 0.0 copy-start.17
  6.4 0.0 copy-start.18
  6.4 10.1 %later.1 = (bf16[16,256,256]{2,1,0:T(8,128)(2,1)}, bf16[256,1024]{1,0:T(8,128)(2,1)}, bf16[8,2,128,128]{3,2,1,0:T(8,128)(2,1)}) custom-call(bf16[384,1024]{1,0:T(8,128)(2,1)} %key_ref.3, bf16[384,2048]{1,0:T(8,128)(2,1)} %value_ref.3, f32[4,1024]{1,0:T(4,128)} %key_taps.3, f32[4,2048]{1,0:T(4,128)} %value_taps.3, f32[16,384]{1,0:T(8,128)} %bitcast.11, ...), custom_call_target="tpu_custom_call" | custom-call | flops 3019898880 | tf_op jit(solution)/shard_map/later/pallas_call | solution.py:325
  16.6 0.0 collective-permute-done.key_before.value_before.query_before
  16.6 0.0 copy-done.9
  16.6 0.0 copy-done.13
  16.6 0.0 copy-done.16
  16.6 0.0 copy-done.17
  16.6 0.0 copy-done.18
  16.6 0.0 copy-start.19
  16.6 1.0 %copy-done.19 = bf16[8,2,128,128]{3,2,1,0:T(8,128)(2,1)S(1)} copy-done((bf16[8,2,128,128]{3,2,1,0:T(8,128)(2,1)S(1)}, bf16[8,2,128,128]{3,2,1,0:T(8,128)(2,1)}, u32[]{:S(2)}) %copy-start.19) | copy-done | bytes 524312
  17.7 0.0 copy-start.6
  17.7 9.4 %states.1 = (bf16[16,128,256]{2,1,0:T(8,128)(2,1)}, bf16[128,1024]{1,0:T(8,128)(2,1)S(1)}, bf16[16,384,256]{2,1,0:T(8,128)(2,1)}, bf16[16,2,128,256]{3,2,1,0:T(8,128)(2,1)}) custom-call(bf16[384,1024]{1,0:T(8,128)(2,1)S(1)} %copy-done.9, bf16[384,2048]{1,0:T(8,128)(2,1)} %value_ref.3, ...), custom_call_target="tpu_custom_call" | custom-call | flops 2013265920 | tf_op jit(solution)/shard_map/states/pallas_call | solution.py:349
  27.0 0.0 copy-start.11
  27.0 0.7 copy-done.11
  27.7 0.0 copy-start.2
  27.7 0.0 copy-start.14
  27.7 0.0 copy-start.15
  27.7 4.9 %all-to-all-start = ((bf16[16,128,256]{2,1,0:T(8,128)(2,1)}), bf16[16,128,256]{2,1,0:T(8,128)(2,1)S(1)}, u32[]{:S(2)}, u32[]{:S(2)}) async-start(bf16[16,128,256]{2,1,0:T(8,128)(2,1)} %get-tuple-element.23), calls=%async_computation | async-start | bytes 2097152 | tf_op jit(solution)/shard_map/all_to_all | solution.py:458
  32.6 0.0 copy-done.6
  32.6 0.0 copy-done.2
  32.6 0.0 copy-done.14
  32.6 0.0 copy-done.15
  32.6 0.0 copy-start.1
  32.6 1.9 %copy-done.1 = bf16[16,384,256]{2,1,0:T(8,128)(2,1)S(1)} copy-done((bf16[16,384,256]{2,1,0:T(8,128)(2,1)S(1)}, bf16[16,384,256]{2,1,0:T(8,128)(2,1)}, u32[]{:S(2)}) %copy-start.1) | copy-done | bytes 3145752
  34.5 0.0 copy-start.5
  34.5 1.6 %copy-done.5 = bf16[16,2,128,256]{3,2,1,0:T(8,128)(2,1)S(1)} copy-done((bf16[16,2,128,256]{3,2,1,0:T(8,128)(2,1)S(1)}, bf16[16,2,128,256]{3,2,1,0:T(8,128)(2,1)}, u32[]{:S(2)}) %copy-start.5) | copy-done | bytes 2097176
  36.1 0.0 copy-start.10
  36.1 1.0 %copy-done.10 = bf16[256,1024]{1,0:T(8,128)(2,1)S(1)} copy-done((bf16[256,1024]{1,0:T(8,128)(2,1)S(1)}, bf16[256,1024]{1,0:T(8,128)(2,1)}, u32[]{:S(2)}) %copy-start.10) | copy-done | bytes 524312
  37.2 0.0 copy-start.12
  37.2 0.9 %copy-done.12 = bf16[128,1024]{1,0:T(8,128)(2,1)S(1)} copy-done((bf16[128,1024]{1,0:T(8,128)(2,1)S(1)}, bf16[128,1024]{1,0:T(8,128)(2,1)}, u32[]{:S(2)}) %copy-start.12) | copy-done | bytes 262168
  38.1 6.4 %local.1 = (bf16[16,384,256]{2,1,0:T(8,128)(2,1)S(1)}, bf16[384,2048]{1,0:T(8,128)(2,1)S(1)}) custom-call(bf16[384,1024]{1,0:T(8,128)(2,1)S(1)} %copy-done.2, bf16[3,4096]{1,0:T(4,128)(2,1)S(1)} %collective-permute-done.key_before.value_before.query_before, f32[4,1024]{1,0:T(4,128)S(1)} %copy-done.14, bf16[128,1024]{1,0:T(8,128)(2,1)S(1)} %copy-done.12, ...), custom_call_target="tpu_custom_call" | custom-call | flops 1207959552 | tf_op jit(solution)/shard_map/local/pallas_call | solution.py:380
  44.5 0.0 copy-start.3
  44.5 1.6 %copy-done.3 = bf16[16,384,256]{2,1,0:T(8,128)(2,1)} copy-done((bf16[16,384,256]{2,1,0:T(8,128)(2,1)}, bf16[16,384,256]{2,1,0:T(8,128)(2,1)S(1)}, u32[]{:S(2)}) %copy-start.3) | copy-done | bytes 3145752
  46.2 0.0 copy-start.7
  46.2 1.2 %copy-done.7 = bf16[384,2048]{1,0:T(8,128)(2,1)} copy-done((bf16[384,2048]{1,0:T(8,128)(2,1)}, bf16[384,2048]{1,0:T(8,128)(2,1)S(1)}, u32[]{:S(2)}) %copy-start.7) | copy-done | bytes 1572888
  47.3 0.0 all-to-all-done
  47.4 1.1 %prefix.1 = (bf16[8,2,128,256]{3,2,1,0:T(8,128)(2,1)S(1)}, bf16[2,128,128]{2,1,0:T(8,128)(2,1)S(1)}) custom-call(bf16[8,2,128,256]{3,2,1,0:T(8,128)(2,1)S(1)} %bitcast.6), custom_call_target="tpu_custom_call" | custom-call | tf_op jit(solution)/shard_map/prefix/pallas_call | solution.py:460
  48.5 0.0 copy-start.8
  48.5 3.7 %collective-permute-start.1 = (bf16[2,128,128]{2,1,0:T(8,128)(2,1)S(1)}, bf16[2,128,128]{2,1,0:T(8,128)(2,1)S(1)}, u32[]{:S(2)}, u32[]{:S(2)}) collective-permute-start(bf16[2,128,128]{2,1,0:T(8,128)(2,1)S(1)} %get-tuple-element.32), channel_id=1, source_target_pairs={{0,16},{2,18},{4,20},{6,22},{8,24},{10,26},{12,28},{14,30},{1,17},... | collective-permute-start | bytes 196616 | tf_op jit(solution)/shard_map/ppermute | solution.py:435
  52.2 1.9 %collective-permute-done.1.start_ref = bf16[2,128,128]{2,1,0:T(8,128)(2,1)S(1)} collective-permute-done((bf16[2,128,128]{2,1,0:T(8,128)(2,1)S(1)}, bf16[2,128,128]{2,1,0:T(8,128)(2,1)S(1)}, u32[]{:S(2)}, u32[]{:S(2)}) %collective-permute-start.1) | collective-permute-done | bytes 65568 | tf_op jit(solution)/shard_map/ppermute | solution.py:435
  54.1 1.1 %apply.1 = bf16[8,2,128,128]{3,2,1,0:T(8,128)(2,1)} custom-call(bf16[8,2,128,256]{3,2,1,0:T(8,128)(2,1)S(1)} %get-tuple-element.31.prefix_ref, bf16[2,128,128]{2,1,0:T(8,128)(2,1)S(1)} %collective-permute-done.1.start_ref), custom_call_target="tpu_custom_call" | custom-call | tf_op jit(solution)/shard_map/apply/pallas_call | solution.py:469
  55.2 5.7 %all-to-all-start.1 = ((bf16[16,128,128]{2,1,0:T(8,128)(2,1)}), bf16[16,128,128]{2,1,0:T(8,128)(2,1)S(1)}, u32[]{:S(2)}, u32[]{:S(2)}) async-start(bf16[16,128,128]{2,1,0:T(8,128)(2,1)} %bitcast.5), calls=%async_computation.1 | async-start | bytes 1048576 | tf_op jit(solution)/shard_map/all_to_all | solution.py:475
  60.9 7.7 %all-to-all-done.1.starts_ref = bf16[16,128,128]{2,1,0:T(8,128)(2,1)S(1)} async-done(((bf16[16,128,128]{2,1,0:T(8,128)(2,1)}), bf16[16,128,128]{2,1,0:T(8,128)(2,1)S(1)}, u32[]{:S(2)}, u32[]{:S(2)}) %all-to-all-start.1) | async-done | bytes 524320 | tf_op jit(solution)/shard_map/all_to_all | solution.py:475
  68.5 0.0 copy-done.8
  68.5 0.0 copy-start
  68.5 3.4 %copy-done = bf16[2048,2048]{1,0:T(8,128)(2,1)S(1)} copy-done((bf16[2048,2048]{1,0:T(8,128)(2,1)S(1)}, bf16[2048,2048]{1,0:T(8,128)(2,1)}, u32[]{:S(2)}) %copy-start) | copy-done | bytes 8388632
  71.9 0.0 copy-start.4
  71.9 1.9 %copy-done.4 = bf16[16,384,256]{2,1,0:T(8,128)(2,1)S(1)} copy-done((bf16[16,384,256]{2,1,0:T(8,128)(2,1)S(1)}, bf16[16,384,256]{2,1,0:T(8,128)(2,1)}, u32[]{:S(2)}) %copy-start.4) | copy-done | bytes 3145752
  73.8 4.6 %project.1 = (bf16[192,2048]{1,0:T(8,128)(2,1)S(1)}, bf16[192,2048]{1,0:T(8,128)(2,1)S(1)}) custom-call(s32[1]{0:T(128)} %bitcast.place_ref, bf16[16,128,128]{2,1,0:T(8,128)(2,1)S(1)} %all-to-all-done.1.starts_ref, bf16[16,384,256]{2,1,0:T(8,128)(2,1)S(1)} %copy-done.4, bf16[384,2048]{1,0:T(8,128)(2,1)S(1)} %copy-done.8, bf16[2048,2048]{1,0:T(8,128)(2,1)S(1)} %copy-done), custom_call_target="tpu_custom_call" | custom-call | tf_op jit(solution)/shard_map/project/pallas_call | solution.py:525
  78.4 0.1 collective-permute-start.2
  78.5 2.3 %collective-permute-done.2 = bf16[192,2048]{1,0:T(8,128)(2,1)S(1)} collective-permute-done((bf16[192,2048]{1,0:T(8,128)(2,1)S(1)}, bf16[192,2048]{1,0:T(8,128)(2,1)S(1)}, u32[]{:S(2)}, u32[]{:S(2)}) %collective-permute-start.2) | collective-permute-done | bytes 786464 | tf_op jit(solution)/shard_map/ppermute | solution.py:537
  80.8 1.2 %add_convert_fusion = bf16[192,2048]{1,0:T(8,128)(2,1)} fusion(bf16[192,2048]{1,0:T(8,128)(2,1)S(1)} %collective-permute-done.2, bf16[192,2048]{1,0:T(8,128)(2,1)S(1)} %get-tuple-element.35), kind=kLoop, calls=%fused_computation | loop fusion | flops 1572864 | bytes 2359296 | tf_op jit(solution)/shard_map/convert_element_type | solution.py:538
Async XLA Ops:
  1.5 15.1 %collective-permute-start = (bf16[3,4096]{1,0:T(4,128)(2,1)}, bf16[3,4096]{1,0:T(4,128)(2,1)S(1)}, u32[]{:S(2)}, u32[]{:S(2)}) collective-permute-start(bf16[3,4096]{1,0:T(4,128)(2,1)} %tails.1), channel_id=1, source_target_pairs={{0,2},{2,4},{4,6},{6,8},{8,10},{10,12},{12,14},{14,16},{16,18},{18... | collective-permute-start | bytes 73736 | tf_op jit(solution)/shard_map/ppermute | solution.py:435
  6.4 10.2 %copy-start.9 = (bf16[384,1024]{1,0:T(8,128)(2,1)S(1)}, bf16[384,1024]{1,0:T(8,128)(2,1)}, u32[]{:S(2)}) copy-start(bf16[384,1024]{1,0:T(8,128)(2,1)} %key_ref.3) | copy-start | bytes 2359300
  6.4 10.2 %copy-start.13 = (f32[384,16]{0,1:T(8,128)S(1)}, f32[384,16]{0,1:T(8,128)}, u32[]{:S(2)}) copy-start(f32[384,16]{0,1:T(8,128)} %param.19) | copy-start | bytes 73732
  6.4 10.2 %copy-start.16 = (f32[4,2048]{1,0:T(4,128)S(1)}, f32[4,2048]{1,0:T(4,128)}, u32[]{:S(2)}) copy-start(f32[4,2048]{1,0:T(4,128)} %value_taps.3) | copy-start | bytes 98308
  6.4 10.2 %copy-start.17 = (f32[384,16]{0,1:T(8,128)S(1)}, f32[384,16]{0,1:T(8,128)}, u32[]{:S(2)}) copy-start(f32[384,16]{0,1:T(8,128)} %param.18) | copy-start | bytes 73732
  6.4 10.2 %copy-start.18 = (f32[4,1024]{1,0:T(4,128)S(1)}, f32[4,1024]{1,0:T(4,128)}, u32[]{:S(2)}) copy-start(f32[4,1024]{1,0:T(4,128)} %key_taps.3) | copy-start | bytes 49156
  16.6 1.0 %copy-start.19 = (bf16[8,2,128,128]{3,2,1,0:T(8,128)(2,1)S(1)}, bf16[8,2,128,128]{3,2,1,0:T(8,128)(2,1)}, u32[]{:S(2)}) copy-start(bf16[8,2,128,128]{3,2,1,0:T(8,128)(2,1)} %get-tuple-element.22.turned_hbm) | copy-start | bytes 1572868
  17.7 14.9 %copy-start.6 = (bf16[384,2048]{1,0:T(8,128)(2,1)S(1)}, bf16[384,2048]{1,0:T(8,128)(2,1)}, u32[]{:S(2)}) copy-start(bf16[384,2048]{1,0:T(8,128)(2,1)} %gate_ref.1) | copy-start | bytes 4718596
  27.0 0.7 copy-start.11
  27.7 4.9 %copy-start.2 = (bf16[384,1024]{1,0:T(8,128)(2,1)S(1)}, bf16[384,1024]{1,0:T(8,128)(2,1)}, u32[]{:S(2)}) copy-start(bf16[384,1024]{1,0:T(8,128)(2,1)} %query_ref.1) | copy-start | bytes 2359300
  27.7 4.9 %copy-start.14 = (f32[4,1024]{1,0:T(4,128)S(1)}, f32[4,1024]{1,0:T(4,128)}, u32[]{:S(2)}) copy-start(f32[4,1024]{1,0:T(4,128)} %query_taps.1) | copy-start | bytes 49156
  27.7 4.9 %copy-start.15 = (f32[128]{0:T(128)S(1)}, f32[128]{0:T(128)}, u32[]{:S(2)}) copy-start(f32[128]{0:T(128)} %param.20) | copy-start | bytes 1540
  27.7 19.6 %all-to-all-start = ((bf16[16,128,256]{2,1,0:T(8,128)(2,1)}), bf16[16,128,256]{2,1,0:T(8,128)(2,1)S(1)}, u32[]{:S(2)}, u32[]{:S(2)}) async-start(bf16[16,128,256]{2,1,0:T(8,128)(2,1)} %get-tuple-element.23), calls=%async_computation | async-start | bytes 2097152 | tf_op jit(solution)/shard_map/all_to_all | solution.py:458
  32.6 1.9 %copy-start.1 = (bf16[16,384,256]{2,1,0:T(8,128)(2,1)S(1)}, bf16[16,384,256]{2,1,0:T(8,128)(2,1)}, u32[]{:S(2)}) copy-start(bf16[16,384,256]{2,1,0:T(8,128)(2,1)} %get-tuple-element.26.fresh_ref) | copy-start | bytes 9437188
  34.5 1.6 %copy-start.5 = (bf16[16,2,128,256]{3,2,1,0:T(8,128)(2,1)S(1)}, bf16[16,2,128,256]{3,2,1,0:T(8,128)(2,1)}, u32[]{:S(2)}) copy-start(bf16[16,2,128,256]{3,2,1,0:T(8,128)(2,1)} %get-tuple-element.27.starts_ref) | copy-start | bytes 6291460
  36.1 1.0 %copy-start.10 = (bf16[256,1024]{1,0:T(8,128)(2,1)S(1)}, bf16[256,1024]{1,0:T(8,128)(2,1)}, u32[]{:S(2)}) copy-start(bf16[256,1024]{1,0:T(8,128)(2,1)} %get-tuple-element.25.later_unit) | copy-start | bytes 1572868
  37.2 0.9 %copy-start.12 = (bf16[128,1024]{1,0:T(8,128)(2,1)S(1)}, bf16[128,1024]{1,0:T(8,128)(2,1)}, u32[]{:S(2)}) copy-start(bf16[128,1024]{1,0:T(8,128)(2,1)} %copy-done.11) | copy-start | bytes 786436
  44.5 1.6 %copy-start.3 = (bf16[16,384,256]{2,1,0:T(8,128)(2,1)}, bf16[16,384,256]{2,1,0:T(8,128)(2,1)S(1)}, u32[]{:S(2)}) copy-start(bf16[16,384,256]{2,1,0:T(8,128)(2,1)S(1)} %get-tuple-element.33.parts_ref) | copy-start | bytes 9437188
  46.2 1.2 %copy-start.7 = (bf16[384,2048]{1,0:T(8,128)(2,1)}, bf16[384,2048]{1,0:T(8,128)(2,1)S(1)}, u32[]{:S(2)}) copy-start(bf16[384,2048]{1,0:T(8,128)(2,1)S(1)} %get-tuple-element.34.gated_ref) | copy-start | bytes 4718596
  48.5 20.0 %copy-start.8 = (bf16[384,2048]{1,0:T(8,128)(2,1)S(1)}, bf16[384,2048]{1,0:T(8,128)(2,1)}, u32[]{:S(2)}) copy-start(bf16[384,2048]{1,0:T(8,128)(2,1)} %copy-done.7) | copy-start | bytes 4718596
  48.5 5.6 %collective-permute-start.1 = (bf16[2,128,128]{2,1,0:T(8,128)(2,1)S(1)}, bf16[2,128,128]{2,1,0:T(8,128)(2,1)S(1)}, u32[]{:S(2)}, u32[]{:S(2)}) collective-permute-start(bf16[2,128,128]{2,1,0:T(8,128)(2,1)S(1)} %get-tuple-element.32), channel_id=1, source_target_pairs={{0,16},{2,18},{4,20},{6,22},{8,24},{10,26},{12,28},{14,30},{1,17},... | collective-permute-start | bytes 196616 | tf_op jit(solution)/shard_map/ppermute | solution.py:435
  55.2 13.3 %all-to-all-start.1 = ((bf16[16,128,128]{2,1,0:T(8,128)(2,1)}), bf16[16,128,128]{2,1,0:T(8,128)(2,1)S(1)}, u32[]{:S(2)}, u32[]{:S(2)}) async-start(bf16[16,128,128]{2,1,0:T(8,128)(2,1)} %bitcast.5), calls=%async_computation.1 | async-start | bytes 1048576 | tf_op jit(solution)/shard_map/all_to_all | solution.py:475
  68.5 3.4 %copy-start = (bf16[2048,2048]{1,0:T(8,128)(2,1)S(1)}, bf16[2048,2048]{1,0:T(8,128)(2,1)}, u32[]{:S(2)}) copy-start(bf16[2048,2048]{1,0:T(8,128)(2,1)} %weight_ref.1) | copy-start | bytes 25165828
  71.9 1.9 %copy-start.4 = (bf16[16,384,256]{2,1,0:T(8,128)(2,1)S(1)}, bf16[16,384,256]{2,1,0:T(8,128)(2,1)}, u32[]{:S(2)}) copy-start(bf16[16,384,256]{2,1,0:T(8,128)(2,1)} %copy-done.3) | copy-start | bytes 9437188
  78.4 2.4 %collective-permute-start.2 = (bf16[192,2048]{1,0:T(8,128)(2,1)S(1)}, bf16[192,2048]{1,0:T(8,128)(2,1)S(1)}, u32[]{:S(2)}, u32[]{:S(2)}) collective-permute-start(bf16[192,2048]{1,0:T(8,128)(2,1)S(1)} %get-tuple-element.36), channel_id=1, source_target_pairs={{0,1},{1,0},{2,3},{3,2},{4,5},{5,4},{6,7},{7,6},{8,9},{9,8},{10,11... | collective-permute-start | bytes 2359304 | tf_op jit(solution)/shard_map/ppermute | solution.py:537

commit v3 on v1

--- a/solution.py
+++ b/solution.py
@@ -26,11 +26,17 @@
     return 0.5 + 0.5 * jnp.tanh(0.5 * x)
 
 
-def conv_silu(padded, first, rows, taps_ref):
-    summed = taps_ref[0:1, :] * padded[first : first + rows, :]
+def conv_silu(padded, first, rows, taps_ref, head):
+    taps = taps_ref[:, head_of(head)]
+    summed = taps[0:1] * padded[head, first : first + rows, :]
     for offset in range(1, 4):
-        summed = summed + taps_ref[offset : offset + 1, :] * padded[first + offset : first + offset + rows, :]
+        summed = summed + taps[offset : offset + 1] * padded[head, first + offset : first + offset + rows, :]
     return summed * sigmoid(summed)
+
+
+def widen(padded, first, rows, raw):
+    for head in range(padded.shape[0]):
+        padded[head, first : first + rows, :] = raw[:, head_of(head)].astype(F32)
 
 
 def unit_rows(key):
@@ -147,7 +153,7 @@
 
 def later_kernel(
     key_ref, value_ref, key_taps, value_taps, beta_ref, decay_ref,
-    solved_ref, unit_ref, turned_ref, key_padded, value_padded,
+    solved_ref, moves_ref, unit_ref, key_padded, value_padded,
 ):
     length, width = key_ref.shape
     chunks = range(1, length // CHUNK)
@@ -157,107 +163,92 @@
     packs = [(chunk, head) for chunk in chunks for head in range(heads)]
     skip = CHUNK - 16
     count = length - CHUNK
-    key_padded[...] = key_ref[skip:, :].astype(F32)
-    value_padded[...] = value_ref[skip:, :].astype(F32)
-    key_conv = conv_silu(key_padded, 13, count, key_taps)
+    widen(key_padded, 0, count + 16, key_ref[skip:, :])
+    widen(value_padded, 0, count + 16, value_ref[skip:, :])
     key, turned = {}, {}
     for j in range(key_heads):
-        unit = unit_rows(key_conv[:, head_of(j)])
+        unit = unit_rows(conv_silu(key_padded, 13, count, key_taps, j))
         unit_ref[:, head_of(j)] = unit.astype(BF16)
         for chunk in chunks:
             key[chunk, j] = unit[part_of(chunk - 1)]
             turned[chunk, j] = key[chunk, j].T
-            turned_ref[j, chunk - 1] = turned[chunk, j].astype(BF16)
-    value = conv_silu(value_padded, 13, count, value_taps)
+    value = [conv_silu(value_padded, 13, count, value_taps, head) for head in range(heads)]
+    fade = log_fades(chunk_rows(decay_ref, heads, chunks))
     solved = solved_packs(
-        log_fades(chunk_rows(decay_ref, heads, chunks)),
+        fade,
         sigmoid(chunk_rows(beta_ref, heads, chunks)),
         [key[chunk, head // repeat_by] for chunk, head in packs],
         [turned[chunk, head // repeat_by] for chunk, head in packs],
-        [value[part_of(chunk - 1), head_of(head)] for chunk, head in packs],
-    )
-    for (chunk, head), one in zip(packs, solved):
-        solved_ref[head, part_of(chunk - 1), :] = one.astype(BF16)
+        [value[head][part_of(chunk - 1)] for chunk, head in packs],
+    )
+    tail = jnp.exp(fade[:, CHUNK - 1 : CHUNK] - fade)
+    for pack, (chunk, head) in enumerate(packs):
+        one = solved[pack].astype(BF16)
+        solved_ref[head, part_of(chunk - 1), :] = one
+        moves_ref[head, chunk - 1] = mul(
+            turned[chunk, head // repeat_by] * tail[pack : pack + 1, :], one
+        ).astype(BF16)
 
 
 def states_kernel(
-    key_ref, value_ref, key_before, value_before, key_taps, value_taps, beta_ref, decay_ref,
-    solved_hbm, turned_hbm,
-    pairs_ref, unit_ref, fresh_hbm, starts_hbm,
-    key_padded, value_padded, solved_ref, turned_ref, fresh_ref, starts_ref, in_sem, out_sem,
+    key_ref, value_ref, key_before, value_before, key_taps, value_taps, beta_ref, decay_ref, moves_hbm,
+    pairs_ref, unit_ref, solved_hbm, starts_hbm,
+    key_padded, value_padded, moves_ref, solved_ref, starts_ref, in_sem, out_sem,
 ):
     heads, length = decay_ref.shape
     chunks = length // CHUNK
     key_heads = key_ref.shape[1] // DK
     repeat_by = heads // key_heads
-    incoming = [
-        pltpu.make_async_copy(solved_hbm, solved_ref, in_sem.at[0]),
-        pltpu.make_async_copy(turned_hbm, turned_ref, in_sem.at[1]),
-    ]
-    for copy in incoming:
-        copy.start()
-
-    key_padded[5:8, :] = key_before[...].astype(F32)
-    key_padded[8 : 8 + CHUNK, :] = key_ref[...].astype(F32)
-    value_padded[5:8, :] = value_before[...].astype(F32)
-    value_padded[8 : 8 + CHUNK, :] = value_ref[...].astype(F32)
-    key_conv = conv_silu(key_padded, 5, CHUNK, key_taps)
-    key, first_turned = [], []
+    incoming = pltpu.make_async_copy(moves_hbm, moves_ref, in_sem)
+    incoming.start()
+
+    widen(key_padded, 5, 3, key_before[...])
+    widen(key_padded, 8, CHUNK, key_ref[...])
+    widen(value_padded, 5, 3, value_before[...])
+    widen(value_padded, 8, CHUNK, value_ref[...])
+    key, turned = [], []
     for j in range(key_heads):
-        key.append(unit_rows(key_conv[:, head_of(j)]))
+        key.append(unit_rows(conv_silu(key_padded, 5, CHUNK, key_taps, j)))
         unit_ref[:, head_of(j)] = key[j].astype(BF16)
-        first_turned.append(key[j].T)
-    value = conv_silu(value_padded, 5, CHUNK, value_taps)
+        turned.append(key[j].T)
     fade = log_fades(chunk_rows(decay_ref, heads, range(chunks)))
     solved = solved_packs(
         fade[:heads],
         sigmoid(beta_ref[:, :CHUNK]),
         [key[head // repeat_by] for head in range(heads)],
-        [first_turned[head // repeat_by] for head in range(heads)],
-        [value[:, head_of(head)] for head in range(heads)],
+        [turned[head // repeat_by] for head in range(heads)],
+        [conv_silu(value_padded, 5, CHUNK, value_taps, head) for head in range(heads)],
     )
     last = jnp.exp(fade[:, CHUNK - 1 : CHUNK])
     tail = jnp.exp(fade[:, CHUNK - 1 : CHUNK] - fade)
     rows, cols = square_iotas()
     identity = jnp.where(rows == cols, 1.0, 0.0)
 
-    state = [None] * heads
-    outgoing = []
-    for chunk in range(chunks):
-        if chunk == 1:
-            for copy in incoming:
-                copy.wait()
+    state = []
+    for head in range(heads):
+        one = solved[head].astype(BF16)
+        solved_ref[head] = one
+        moved = mul(turned[head // repeat_by] * tail[head : head + 1, :], one)
+        state.append(
+            jnp.concatenate([moved[:, :DV], last[head : head + 1, :] * identity - moved[:, DV:]], 1)
+        )
+    outgoing = [pltpu.make_async_copy(solved_ref, solved_hbm, out_sem.at[0])]
+    outgoing[0].start()
+    incoming.wait()
+    for chunk in range(1, chunks):
         for head in range(heads):
             pack = chunk * heads + head
-            if chunk == 0:
-                updates, wide = solved[head][:, :DV], solved[head][:, DV:]
-                fresh = jnp.concatenate([updates, -wide], 1).astype(BF16)
-                faded = jnp.concatenate(
-                    [jnp.zeros((DK, DV), F32), last[pack : pack + 1, :] * identity], 1
-                )
-                turned = first_turned[head // repeat_by]
-            else:
-                held = solved_ref[head, part_of(chunk - 1), :]
-                start = state[head].astype(BF16)
-                starts_ref[head, chunk - 1] = start
-                taken = mul(held[:, DV:], start)
-                fresh = jnp.concatenate(
-                    [held[:, :DV].astype(F32) - taken[:, :DV], -taken[:, DV:]], 1
-                ).astype(BF16)
-                faded = last[pack : pack + 1, :] * state[head]
-                turned = turned_ref[head // repeat_by, chunk - 1].astype(F32)
-            fresh_ref[head, part_of(chunk), :] = fresh
-            state[head] = faded + mul(turned * tail[pack : pack + 1, :], fresh)
+            start = state[head].astype(BF16)
+            starts_ref[chunk - 1, head] = start
+            moves = moves_ref[head, chunk - 1]
+            moved = last[pack : pack + 1, :] * state[head] - mul(moves[:, DV:], start)
+            state[head] = jnp.concatenate([moved[:, :DV] + moves[:, :DV].astype(F32), moved[:, DV:]], 1)
         outgoing.append(
             pltpu.make_async_copy(
-                fresh_ref.at[:, pl.ds(chunk * CHUNK, CHUNK)],
-                fresh_hbm.at[:, pl.ds(chunk * CHUNK, CHUNK)],
-                out_sem.at[chunk],
+                starts_ref.at[chunk - 1], starts_hbm.at[chunk - 1], out_sem.at[chunk]
             )
         )
         outgoing[-1].start()
-    outgoing.append(pltpu.make_async_copy(starts_ref, starts_hbm, out_sem.at[chunks]))
-    outgoing[-1].start()
     for head in range(heads):
         pairs_ref[head] = state[head].astype(BF16)
     for copy in outgoing:
@@ -265,32 +256,33 @@
 
 
 def local_kernel(
-    query_ref, query_before, query_taps, first_unit, later_unit, decay_ref, fresh_ref, starts_ref,
-    gate_ref, gain_ref, parts_ref, gated_ref, padded,
+    query_ref, query_before, query_taps, first_unit, later_unit, decay_ref,
+    first_solved, later_solved, starts_ref, gate_ref, gain_ref,
+    parts_ref, gated_ref, padded,
 ):
     length, width = query_ref.shape
     chunks = length // CHUNK
     key_heads = width // DK
-    heads = fresh_ref.shape[0]
+    heads = first_solved.shape[0]
     repeat_by = heads // key_heads
 
     rows, cols = square_iotas()
     within = rows >= cols
     fade = log_fades(chunk_rows(decay_ref, heads, range(chunks)))
     columns = as_columns((fade, jnp.exp(fade)))
-    padded[5:8, :] = query_before[...].astype(F32)
-    padded[8 : 8 + length, :] = query_ref[...].astype(F32)
-    query = conv_silu(padded, 5, length, query_taps).astype(BF16)
+    widen(padded, 5, 3, query_before[...])
+    widen(padded, 8, length, query_ref[...])
+    query = [conv_silu(padded, 5, length, query_taps, j).astype(BF16) for j in range(key_heads)]
     for head in range(heads):
         gate = gate_ref[:, head_of(head)].astype(F32)
         gated_ref[:, head_of(head)] = (gate * sigmoid(gate) * gain_ref[...]).astype(BF16)
     for chunk in range(chunks):
         part = part_of(chunk)
         for j in range(key_heads):
-            own = head_of(j)
-            unit = first_unit[:, own] if chunk == 0 else later_unit[part_of(chunk - 1), own]
+            own = query[j][part]
+            unit = first_unit[:, head_of(j)] if chunk == 0 else later_unit[part_of(chunk - 1), head_of(j)]
             inner = lax.dot_general(
-                query[part, own], unit, (((1,), (1,)), ((), ())), preferred_element_type=F32
+                own, unit, (((1,), (1,)), ((), ())), preferred_element_type=F32
             )
             for head in range(j * repeat_by, (j + 1) * repeat_by):
                 pack = chunk * heads + head
@@ -298,12 +290,20 @@
                 scores = inner * jnp.exp(jnp.where(within, gap, -1e30))
                 grown = columns[:, chunks * heads + pack : chunks * heads + pack + 1]
                 if chunk == 0:
+                    updates, wide = first_solved[head, :, :DV], first_solved[head, :, DV:]
+                    fresh = jnp.concatenate([updates, -wide], 1)
                     carried = jnp.concatenate(
-                        [jnp.zeros((CHUNK, DV), F32), grown * query[part, own].astype(F32)], 1
+                        [jnp.zeros((CHUNK, DV), F32), grown * own.astype(F32)], 1
                     )
                 else:
-                    carried = grown * mul(query[part, own], starts_ref[head, chunk - 1])
-                parts_ref[head, part, :] = (carried + mul(scores, fresh_ref[head, part, :])).astype(BF16)
+                    solved = later_solved[head, part_of(chunk - 1), :]
+                    both = mul(jnp.concatenate([solved[:, DV:], own], 0), starts_ref[chunk - 1, head])
+                    taken = both[:CHUNK]
+                    fresh = jnp.concatenate(
+                        [solved[:, :DV].astype(F32) - taken[:, :DV], -taken[:, DV:]], 1
+                    )
+                    carried = grown * both[CHUNK:]
+                parts_ref[head, part, :] = (carried + mul(scores, fresh)).astype(BF16)
 
 
 def columns_of(rows, width, first=0):
@@ -334,7 +334,7 @@
     each = math.gcd(4, key_heads)
     steps, narrow, wide, of_heads, logits = split(each)
     later = length - CHUNK
-    solved, later_unit, turned = pl.pallas_call(
+    solved, moves, later_unit = pl.pallas_call(
         later_kernel,
         grid=(steps,),
         in_specs=[
@@ -342,15 +342,17 @@
             columns_of(4, narrow), columns_of(4, wide), logits, logits,
         ],
         out_specs=[
-            of_heads(later, DV + DK), columns_of(later, narrow),
-            pl.BlockSpec((each, chunks - 1, DK, CHUNK), lambda step: (step, 0, 0, 0)),
+            of_heads(later, DV + DK), of_heads(chunks - 1, DK, DV + DK), columns_of(later, narrow),
         ],
         out_shape=[
             jax.ShapeDtypeStruct((value_heads, later, DV + DK), BF16),
+            jax.ShapeDtypeStruct((value_heads, chunks - 1, DK, DV + DK), BF16),
             jax.ShapeDtypeStruct((later, key_heads * DK), BF16),
-            jax.ShapeDtypeStruct((key_heads, chunks - 1, DK, CHUNK), BF16),
-        ],
-        scratch_shapes=[pltpu.VMEM((later + 16, narrow), F32), pltpu.VMEM((later + 16, wide), F32)],
+        ],
+        scratch_shapes=[
+            pltpu.VMEM((each, later + 16, DK), F32),
+            pltpu.VMEM((each * repeat_by, later + 16, DV), F32),
+        ],
         compiler_params=in_vmem(60),
         cost_estimate=pl.CostEstimate(flops=30 * work, bytes_accessed=0, transcendentals=0),
         name="later",
@@ -358,47 +360,47 @@
 
     narrow, wide = key_heads * DK, value_heads * DV
     whole = lambda shape, *at: pl.BlockSpec(shape, lambda step: at or (0,) * len(shape))
-    pairs, first_unit, fresh, starts = pl.pallas_call(
+    pairs, first_unit, first_solved, starts = pl.pallas_call(
         states_kernel,
         grid=(1,),
         in_specs=[
             whole((CHUNK, narrow)), whole((CHUNK, wide)),
             whole((3, narrow), 0, repeat_by + 1), whole((3, wide)),
-            whole(taps[1].shape), whole(taps[2].shape), whole(beta.shape), whole(decay.shape),
-            hbm, hbm,
+            whole(taps[1].shape), whole(taps[2].shape), whole(beta.shape), whole(decay.shape), hbm,
         ],
         out_specs=[whole((value_heads, DK, DV + DK)), whole((CHUNK, narrow)), hbm, hbm],
         out_shape=[
             jax.ShapeDtypeStruct((value_heads, DK, DV + DK), BF16),
             jax.ShapeDtypeStruct((CHUNK, narrow), BF16),
-            jax.ShapeDtypeStruct((value_heads, length, DV + DK), BF16),
-            jax.ShapeDtypeStruct((value_heads, chunks - 1, DK, DV + DK), BF16),
+            jax.ShapeDtypeStruct((value_heads, CHUNK, DV + DK), BF16),
+            jax.ShapeDtypeStruct((chunks - 1, value_heads, DK, DV + DK), BF16),
         ],
         scratch_shapes=[
-            pltpu.VMEM((8 + CHUNK, narrow), F32),
-            pltpu.VMEM((8 + CHUNK, wide), F32),
-            pltpu.VMEM(solved.shape, BF16),
-            pltpu.VMEM(turned.shape, BF16),
-            pltpu.VMEM((value_heads, length, DV + DK), BF16),
-            pltpu.VMEM((value_heads, chunks - 1, DK, DV + DK), BF16),
-            pltpu.SemaphoreType.DMA((2,)),
-            pltpu.SemaphoreType.DMA((chunks + 1,)),
+            pltpu.VMEM((key_heads, 8 + CHUNK, DK), F32),
+            pltpu.VMEM((value_heads, 8 + CHUNK, DV), F32),
+            pltpu.VMEM(moves.shape, BF16),
+            pltpu.VMEM((value_heads, CHUNK, DV + DK), BF16),
+            pltpu.VMEM((chunks - 1, value_heads, DK, DV + DK), BF16),
+            pltpu.SemaphoreType.DMA,
+            pltpu.SemaphoreType.DMA((chunks,)),
         ],
         compiler_params=in_vmem(54),
         cost_estimate=pl.CostEstimate(flops=20 * work, bytes_accessed=0, transcendentals=0),
         name="states",
-    )(raws[1], raws[2], before, before, taps[1], taps[2], beta, decay, solved, turned)
+    )(raws[1], raws[2], before, before, taps[1], taps[2], beta, decay, moves)
     gain = norm_gain.reshape(1, DV)
 
     def local():
         steps, narrow, wide, of_heads, logits = split(math.gcd(2, key_heads))
+        heads = wide // DV
         return pl.pallas_call(
             local_kernel,
             grid=(steps,),
             in_specs=[
                 columns_of(length, narrow), columns_of(3, narrow, repeat_by * steps), columns_of(4, narrow),
                 columns_of(CHUNK, narrow), columns_of(later, narrow), logits,
-                of_heads(length, DV + DK), of_heads(chunks - 1, DK, DV + DK),
+                of_heads(CHUNK, DV + DK), of_heads(later, DV + DK),
+                pl.BlockSpec((chunks - 1, heads, DK, DV + DK), lambda step: (0, step, 0, 0)),
                 columns_of(length, wide), whole(gain.shape),
             ],
             out_specs=[of_heads(length, DV + DK), columns_of(length, wide)],
@@ -406,11 +408,14 @@
                 jax.ShapeDtypeStruct((value_heads, length, DV + DK), BF16),
                 jax.ShapeDtypeStruct(gate_raw.shape, BF16),
             ],
-            scratch_shapes=[pltpu.VMEM((8 + length, narrow), F32)],
-            compiler_params=in_vmem(40),
+            scratch_shapes=[pltpu.VMEM((narrow // DK, 8 + length, DK), F32)],
+            compiler_params=in_vmem(60),
             cost_estimate=pl.CostEstimate(flops=12 * work, bytes_accessed=0, transcendentals=0),
             name="local",
-        )(raws[0], before, taps[0], first_unit, later_unit, decay, fresh, starts, gate_raw, gain)
+        )(
+            raws[0], before, taps[0], first_unit, later_unit, decay,
+            first_solved, solved, starts, gate_raw, gain,
+        )
 
     return pairs, local
 
@@ -568,7 +573,7 @@
             pltpu.VMEM((length, width), F32),
             pltpu.SemaphoreType.DMA((3, heads // min(HEADS_AT_ONCE, heads))),
         ],
-        compiler_params=in_vmem(40),
+        compiler_params=in_vmem(60),
         name="project",
     )(here, starts, parts, gated, out_weight)
     if not halves:

time: 80.8 us -> 79.6 us (0.985)
  local copies, waits for them, and re-layouts: 10.8 us -> 1.37 us
  Pallas kernels: 37 us -> 43 us
  waiting for transfers between devices: 11.8 us -> 15.3 us
  starting transfers between devices: 19.2 us -> 17.2 us
  other arithmetic: 1.15 us -> 2.28 us
    unnamed x30 -> x4, local copies, waits for them, and re-layouts: 10.8 us -> 1.37 us
    pallas_call x1, Pallas kernels: 6.41 us -> 12.3 us  [local(): pl.pallas_call(local_kernel, grid=(steps,), in_specs=[columns_of(length,...]
    pallas_call x1, Pallas kernels: 7.2 us -> 9.69 us  [projected(): pl.pallas_call(project_kernel if halves else whole_kernel, in_specs=[pl.B...]
    all_to_all x1, waiting for transfers between devices: 0.01 us -> 2.12 us  [starts_of(): lax.all_to_all(pairs, axis, 0, 0, axis_index_groups=groups, tiled=True)]
    pallas_call x1, Pallas kernels: 9.61 us -> 7.65 us  [local_steps(): pl.pallas_call(states_kernel, grid=(1,), in_specs=[whole((CHUNK, narrow))...]
    all_to_all x1, starting transfers between devices: 5.67 us -> 3.91 us  [starts_of(): lax.all_to_all(starts.reshape(heads, DK, DV), axis, 0, 0, axis_index_grou...]
    all_to_all x1, waiting for transfers between devices: 7.67 us -> 8.8 us  [starts_of(): lax.all_to_all(starts.reshape(heads, DK, DV), axis, 0, 0, axis_index_grou...]
    convert_element_type x1, other arithmetic: 1.15 us -> 2.28 us  [projected(): return (own.astype(F32) + other.astype(F32)).astype(BF16)]
  transfers between devices with their start and end apart: 5 -> 5, of which waited for: 3 -> 4; matrix products, arithmetic and copies ran while one was open for 0% -> 0% of each run, Pallas kernels for 21% -> 28%
where the time goes in v3:
time: 79.6 us; the launch traced here: 79.2 us
  Pallas kernels  43 us (54%)
  starting transfers between devices  17.2 us (22%)
  waiting for transfers between devices  15.3 us (19%)
  other arithmetic  2.28 us (3%)
  local copies, waits for them, and re-layouts  1.37 us (2%)
    pallas_call x1, Pallas kernels, local(): pl.pallas_call(local_kernel, grid=(steps,), in_specs=[columns_of(length,...  12.3 us
    pallas_call x1, Pallas kernels, projected(): pl.pallas_call(project_kernel if halves else whole_kernel, in_specs=[pl.B...  9.69 us
    pallas_call x1, Pallas kernels, local_steps(): pl.pallas_call(later_kernel, grid=(steps,), in_specs=[columns_of(length,...  9.64 us
    all_to_all x1, waiting for transfers between devices, starts_of(): lax.all_to_all(starts.reshape(heads, DK, DV), axis, 0, 0, axis_index_grou...  8.8 us
    ppermute x2, starting transfers between devices, shifted(): return lax.ppermute(value, axis, [(i, i + by) for i in range(count - by)])  8.42 us
    pallas_call x1, Pallas kernels, local_steps(): pl.pallas_call(states_kernel, grid=(1,), in_specs=[whole((CHUNK, narrow))...  7.65 us
    all_to_all x1, starting transfers between devices, starts_of(): lax.all_to_all(pairs, axis, 0, 0, axis_index_groups=groups, tiled=True)  4.75 us
    all_to_all x1, starting transfers between devices, starts_of(): lax.all_to_all(starts.reshape(heads, DK, DV), axis, 0, 0, axis_index_grou...  3.91 us
  transfers between devices with their start and end apart: 5, of which 4 were waited for; matrix products, arithmetic and copies ran while one was open for 0% of the time, Pallas kernels for 28%

profile of v3, /device:TPU:0, one launch (start us, length us, event | category | flops | bytes accessed | tf_op | source)
XLA Modules:
  0.0 79.2 jit_solution(1296494680705217874)
XLA Ops:
  0.0 1.5 %tails.1 = bf16[3,4096]{1,0:T(4,128)(2,1)} custom-call(bf16[384,2048]{1,0:T(8,128)(2,1)} %value_ref.3, bf16[384,1024]{1,0:T(8,128)(2,1)} %query_ref.1, bf16[384,1024]{1,0:T(8,128)(2,1)} %key_ref.3), custom_call_target="tpu_custom_call" | custom-call | tf_op jit(solution)/shard_map/tails/pallas_call | solution.py:605
  1.5 4.8 %collective-permute-start = (bf16[3,4096]{1,0:T(4,128)(2,1)}, bf16[3,4096]{1,0:T(4,128)(2,1)S(1)}, u32[]{:S(2)}, u32[]{:S(2)}) collective-permute-start(bf16[3,4096]{1,0:T(4,128)(2,1)} %tails.1), channel_id=1, source_target_pairs={{0,2},{2,4},{4,6},{6,8},{8,10},{10,12},{12,14},{14,16},{16,18},{18... | collective-permute-start | bytes 73736 | tf_op jit(solution)/shard_map/ppermute | solution.py:455
  6.4 9.6 %later.1 = (bf16[16,256,256]{2,1,0:T(8,128)(2,1)}, bf16[16,2,128,256]{3,2,1,0:T(8,128)(2,1)}, bf16[256,1024]{1,0:T(8,128)(2,1)}) custom-call(bf16[384,1024]{1,0:T(8,128)(2,1)} %key_ref.3, bf16[384,2048]{1,0:T(8,128)(2,1)} %value_ref.3, f32[4,1024]{1,0:T(4,128)} %key_taps.3, f32[4,2048]{1,0:T(4,128)} %value_taps.3, f32[16,384]{1,0:T(8,128)} %bitcast.11, ...), custom_call_target="tpu_custom_call" | custom-call | flops 3019898880 | tf_op jit(solution)/shard_map/later/pallas_call | solution.py:337
  16.0 0.0 collective-permute-done.key_before.value_before.query_before
  16.0 0.0 copy-start.1
  16.0 0.6 copy-done.1
  16.6 7.7 %states.1 = (bf16[16,128,256]{2,1,0:T(8,128)(2,1)}, bf16[128,1024]{1,0:T(8,128)(2,1)}, bf16[16,128,256]{2,1,0:T(8,128)(2,1)}, bf16[2,16,128,256]{3,2,1,0:T(8,128)(2,1)}) custom-call(bf16[384,1024]{1,0:T(8,128)(2,1)} %key_ref.3, bf16[384,2048]{1,0:T(8,128)(2,1)} %value_ref.3, bf16[3,4096]{1,0:T(4,128)(2,1)} %copy-done.1, bf16[3,4096]{1,0:T(4,128)(2,1)} %copy-done.1, ...), custom_call_target="tpu_custom_call" | custom-call | flops 2013265920 | tf_op jit(solution)/shard_map/states/pallas_call | solution.py:363
  24.3 4.8 %all-to-all-start = ((bf16[16,128,256]{2,1,0:T(8,128)(2,1)}), bf16[16,128,256]{2,1,0:T(8,128)(2,1)S(1)}, u32[]{:S(2)}, u32[]{:S(2)}) async-start(bf16[16,128,256]{2,1,0:T(8,128)(2,1)} %get-tuple-element.22), calls=%async_computation | async-start | bytes 2097152 | tf_op jit(solution)/shard_map/all_to_all | solution.py:478
  29.0 12.3 %local.1 = (bf16[16,384,256]{2,1,0:T(8,128)(2,1)}, bf16[384,2048]{1,0:T(8,128)(2,1)}) custom-call(bf16[384,1024]{1,0:T(8,128)(2,1)} %query_ref.1, bf16[3,4096]{1,0:T(4,128)(2,1)} %copy-done.1, f32[4,1024]{1,0:T(4,128)} %query_taps.1, bf16[128,1024]{1,0:T(8,128)(2,1)} %get-tuple-element.23.first_unit, bf16[256,1024]{1,0:T(8,128)(2,1)} %get-tuple-element.24.later_unit, ...), custom_call_target="tpu_custom_call" | custom-call | flops 1207959552 | tf_op jit(solution)/shard_map/local/pallas_call | solution.py:396
  41.3 2.1 %all-to-all-done = bf16[16,128,256]{2,1,0:T(8,128)(2,1)S(1)} async-done(((bf16[16,128,256]{2,1,0:T(8,128)(2,1)}), bf16[16,128,256]{2,1,0:T(8,128)(2,1)S(1)}, u32[]{:S(2)}, u32[]{:S(2)}) %all-to-all-start) | async-done | bytes 1048608 | tf_op jit(solution)/shard_map/all_to_all | solution.py:478
  43.4 1.1 %prefix.1 = (bf16[8,2,128,256]{3,2,1,0:T(8,128)(2,1)S(1)}, bf16[2,128,128]{2,1,0:T(8,128)(2,1)S(1)}) custom-call(bf16[8,2,128,256]{3,2,1,0:T(8,128)(2,1)S(1)} %bitcast.6), custom_call_target="tpu_custom_call" | custom-call | tf_op jit(solution)/shard_map/prefix/pallas_call | solution.py:480
  44.6 3.6 %collective-permute-start.1 = (bf16[2,128,128]{2,1,0:T(8,128)(2,1)S(1)}, bf16[2,128,128]{2,1,0:T(8,128)(2,1)S(1)}, u32[]{:S(2)}, u32[]{:S(2)}) collective-permute-start(bf16[2,128,128]{2,1,0:T(8,128)(2,1)S(1)} %get-tuple-element.32), channel_id=1, source_target_pairs={{0,16},{2,18},{4,20},{6,22},{8,24},{10,26},{12,28},{14,30},{1,17},... | collective-permute-start | bytes 196616 | tf_op jit(solution)/shard_map/ppermute | solution.py:455
  48.1 1.9 %collective-permute-done.1.start_ref = bf16[2,128,128]{2,1,0:T(8,128)(2,1)S(1)} collective-permute-done((bf16[2,128,128]{2,1,0:T(8,128)(2,1)S(1)}, bf16[2,128,128]{2,1,0:T(8,128)(2,1)S(1)}, u32[]{:S(2)}, u32[]{:S(2)}) %collective-permute-start.1) | collective-permute-done | bytes 65568 | tf_op jit(solution)/shard_map/ppermute | solution.py:455
  50.0 1.1 %apply.1 = bf16[8,2,128,128]{3,2,1,0:T(8,128)(2,1)} custom-call(bf16[8,2,128,256]{3,2,1,0:T(8,128)(2,1)S(1)} %get-tuple-element.31.prefix_ref, bf16[2,128,128]{2,1,0:T(8,128)(2,1)S(1)} %collective-permute-done.1.start_ref), custom_call_target="tpu_custom_call" | custom-call | tf_op jit(solution)/shard_map/apply/pallas_call | solution.py:489
  51.1 3.9 %all-to-all-start.1 = ((bf16[16,128,128]{2,1,0:T(8,128)(2,1)}), bf16[16,128,128]{2,1,0:T(8,128)(2,1)S(1)}, u32[]{:S(2)}, u32[]{:S(2)}) async-start(bf16[16,128,128]{2,1,0:T(8,128)(2,1)} %bitcast.5), calls=%async_computation.1 | async-start | bytes 1048576 | tf_op jit(solution)/shard_map/all_to_all | solution.py:495
  55.0 8.8 %all-to-all-done.1.starts_ref = bf16[16,128,128]{2,1,0:T(8,128)(2,1)S(1)} async-done(((bf16[16,128,128]{2,1,0:T(8,128)(2,1)}), bf16[16,128,128]{2,1,0:T(8,128)(2,1)S(1)}, u32[]{:S(2)}, u32[]{:S(2)}) %all-to-all-start.1) | async-done | bytes 524320 | tf_op jit(solution)/shard_map/all_to_all | solution.py:495
  63.8 0.0 copy-start
  63.8 0.8 copy-done
  64.6 9.7 %project.1 = (bf16[192,2048]{1,0:T(8,128)(2,1)}, bf16[192,2048]{1,0:T(8,128)(2,1)}) custom-call(s32[1]{0:T(128)} %bitcast.place_ref, bf16[16,128,128]{2,1,0:T(8,128)(2,1)} %copy-done, bf16[16,384,256]{2,1,0:T(8,128)(2,1)} %get-tuple-element.33.parts_hbm, bf16[384,2048]{1,0:T(8,128)(2,1)} %get-tuple-element.34.gated_hbm, bf16[2048,2048]{1,0:T(8,128)(2,1)} %weight_hbm.1), custom_call_target="tpu_custom_call" | custom-call | tf_op jit(solution)/shard_map/project/pallas_call | solution.py:564
  74.3 0.1 collective-permute-start.2
  74.4 2.5 %collective-permute-done.2 = bf16[192,2048]{1,0:T(8,128)(2,1)S(1)} collective-permute-done((bf16[192,2048]{1,0:T(8,128)(2,1)}, bf16[192,2048]{1,0:T(8,128)(2,1)S(1)}, u32[]{:S(2)}, u32[]{:S(2)}) %collective-permute-start.2) | collective-permute-done | bytes 786464 | tf_op jit(solution)/shard_map/ppermute | solution.py:582
  76.9 2.3 %add_convert_fusion = bf16[192,2048]{1,0:T(8,128)(2,1)} fusion(bf16[192,2048]{1,0:T(8,128)(2,1)S(1)} %collective-permute-done.2, bf16[192,2048]{1,0:T(8,128)(2,1)} %get-tuple-element.35), kind=kLoop, calls=%fused_computation | loop fusion | flops 1572864 | bytes 2359296 | tf_op jit(solution)/shard_map/convert_element_type | solution.py:583
Async XLA Ops:
  1.5 14.5 %collective-permute-start = (bf16[3,4096]{1,0:T(4,128)(2,1)}, bf16[3,4096]{1,0:T(4,128)(2,1)S(1)}, u32[]{:S(2)}, u32[]{:S(2)}) collective-permute-start(bf16[3,4096]{1,0:T(4,128)(2,1)} %tails.1), channel_id=1, source_target_pairs={{0,2},{2,4},{4,6},{6,8},{8,10},{10,12},{12,14},{14,16},{16,18},{18... | collective-permute-start | bytes 73736 | tf_op jit(solution)/shard_map/ppermute | solution.py:455
  16.0 0.6 copy-start.1
  24.3 19.1 %all-to-all-start = ((bf16[16,128,256]{2,1,0:T(8,128)(2,1)}), bf16[16,128,256]{2,1,0:T(8,128)(2,1)S(1)}, u32[]{:S(2)}, u32[]{:S(2)}) async-start(bf16[16,128,256]{2,1,0:T(8,128)(2,1)} %get-tuple-element.22), calls=%async_computation | async-start | bytes 2097152 | tf_op jit(solution)/shard_map/all_to_all | solution.py:478
  44.6 5.5 %collective-permute-start.1 = (bf16[2,128,128]{2,1,0:T(8,128)(2,1)S(1)}, bf16[2,128,128]{2,1,0:T(8,128)(2,1)S(1)}, u32[]{:S(2)}, u32[]{:S(2)}) collective-permute-start(bf16[2,128,128]{2,1,0:T(8,128)(2,1)S(1)} %get-tuple-element.32), channel_id=1, source_target_pairs={{0,16},{2,18},{4,20},{6,22},{8,24},{10,26},{12,28},{14,30},{1,17},... | collective-permute-start | bytes 196616 | tf_op jit(solution)/shard_map/ppermute | solution.py:455
  51.1 12.7 %all-to-all-start.1 = ((bf16[16,128,128]{2,1,0:T(8,128)(2,1)}), bf16[16,128,128]{2,1,0:T(8,128)(2,1)S(1)}, u32[]{:S(2)}, u32[]{:S(2)}) async-start(bf16[16,128,128]{2,1,0:T(8,128)(2,1)} %bitcast.5), calls=%async_computation.1 | async-start | bytes 1048576 | tf_op jit(solution)/shard_map/all_to_all | solution.py:495
  63.8 0.8 copy-start
  74.3 2.6 %collective-permute-start.2 = (bf16[192,2048]{1,0:T(8,128)(2,1)}, bf16[192,2048]{1,0:T(8,128)(2,1)S(1)}, u32[]{:S(2)}, u32[]{:S(2)}) collective-permute-start(bf16[192,2048]{1,0:T(8,128)(2,1)} %get-tuple-element.36), channel_id=1, source_target_pairs={{0,1},{1,0},{2,3},{3,2},{4,5},{5,4},{6,7},{7,6},{8,9},{9,8},{10,11... | collective-permute-start | bytes 2359304 | tf_op jit(solution)/shard_map/ppermute | solution.py:582

commit v4 on v3

--- a/solution.py
+++ b/solution.py
@@ -499,29 +499,24 @@
 
 
 def project_kernel(
-    place_ref, starts_ref, parts_hbm, gated_hbm, weight_hbm, away_ref, own_ref,
-    parts_ref, gated_ref, weight_ref, total, in_sem,
+    place_ref, starts_ref, gated_ref, parts_hbm, weight_hbm, away_ref, own_ref,
+    parts_ref, weight_ref, total, parts_sem, weight_sem,
 ):
     heads, length = parts_ref.shape[:2]
-    depth, width = weight_ref.shape
+    width = weight_ref.shape[1]
     each = min(HEADS_AT_ONCE, heads)
     block = min(512, width)
     groups = heads // each
-    copies = []
-    for g in range(groups):
-        here, lanes = pl.ds(g * each, each), pl.ds(g * each * DV, each * DV)
-        copies.append(
-            [
-                pltpu.make_async_copy(parts_hbm.at[here], parts_ref.at[here], in_sem.at[0, g]),
-                pltpu.make_async_copy(gated_hbm.at[:, lanes], gated_ref.at[:, lanes], in_sem.at[1, g]),
-                pltpu.make_async_copy(weight_hbm.at[lanes], weight_ref.at[lanes], in_sem.at[2, g]),
-            ]
-        )
-        for copy in copies[g]:
-            copy.start()
-    for g in range(groups):
-        copies[g][0].wait()
-        copies[g][1].wait()
+
+    def parts(g):
+        here = pl.ds(g * each, each)
+        return pltpu.make_async_copy(parts_hbm.at[here], parts_ref.at[here], parts_sem.at[g])
+
+    def weights(g):
+        rows = pl.ds(g * each * DV, each * DV)
+        return pltpu.make_async_copy(weight_hbm.at[rows], weight_ref.at[rows], weight_sem.at[g])
+
+    def normed_group(g):
         normed = []
         for head in range(g * each, (g + 1) * each):
             core = parts_ref[head, :, :DV].astype(F32) + mul(
@@ -529,8 +524,24 @@
             )
             scale = lax.rsqrt(jnp.mean(core * core, -1, keepdims=True) + EPSILON)
             normed.append((core * scale * gated_ref[:, head_of(head)].astype(F32)).astype(BF16))
-        normed = jnp.concatenate(normed, 1)
-        copies[g][2].wait()
+        return jnp.concatenate(normed, 1)
+
+    parts(0).start()
+    weights(0).start()
+    parts(0).wait()
+    if groups > 1:
+        parts(1).start()
+    following = normed_group(0)
+    for g in range(groups):
+        weights(g).wait()
+        if g + 1 < groups:
+            weights(g + 1).start()
+            parts(g + 1).wait()
+        if g + 2 < groups:
+            parts(g + 2).start()
+        normed = following
+        if g + 1 < groups:
+            following = normed_group(g + 1)
         for at in range(0, width, block):
             added = jnp.dot(
                 normed, weight_ref[g * each * DV : (g + 1) * each * DV, at : at + block],
@@ -549,33 +560,34 @@
                 away_ref[:, at : at + block] = jnp.where(first, high, low).astype(BF16)
 
 
-def whole_kernel(place_ref, starts_ref, parts_hbm, gated_hbm, weight_hbm, out_ref, *scratch):
-    project_kernel(place_ref, starts_ref, parts_hbm, gated_hbm, weight_hbm, out_ref, None, *scratch)
+def whole_kernel(place_ref, starts_ref, gated_ref, parts_hbm, weight_hbm, out_ref, *scratch):
+    project_kernel(place_ref, starts_ref, gated_ref, parts_hbm, weight_hbm, out_ref, None, *scratch)
 
 
 def projected(parts, starts, gated, out_weight, axis):
     heads, length = parts.shape[:2]
-    depth, width = out_weight.shape
+    width = out_weight.shape[1]
     halves = lax.axis_size(axis) == 2
+    vmem = pl.BlockSpec(memory_space=pltpu.VMEM)
     hbm = pl.BlockSpec(memory_space=pltpu.HBM)
-    vmem = pl.BlockSpec(memory_space=pltpu.VMEM)
+    groups = heads // min(HEADS_AT_ONCE, heads)
     here = lax.axis_index(axis).astype(jnp.int32).reshape(1)
     out = jax.ShapeDtypeStruct((length // 2 if halves else length, width), BF16)
     partial = pl.pallas_call(
         project_kernel if halves else whole_kernel,
-        in_specs=[pl.BlockSpec(memory_space=pltpu.SMEM), vmem, hbm, hbm, hbm],
+        in_specs=[pl.BlockSpec(memory_space=pltpu.SMEM), vmem, vmem, hbm, hbm],
         out_specs=[vmem, vmem] if halves else vmem,
         out_shape=[out, out] if halves else out,
         scratch_shapes=[
             pltpu.VMEM(parts.shape, BF16),
-            pltpu.VMEM(gated.shape, BF16),
             pltpu.VMEM(out_weight.shape, BF16),
             pltpu.VMEM((length, width), F32),
-            pltpu.SemaphoreType.DMA((3, heads // min(HEADS_AT_ONCE, heads))),
-        ],
-        compiler_params=in_vmem(60),
+            pltpu.SemaphoreType.DMA((groups,)),
+            pltpu.SemaphoreType.DMA((groups,)),
+        ],
+        compiler_params=in_vmem(50),
         name="project",
-    )(here, starts, parts, gated, out_weight)
+    )(here, starts, gated, parts, out_weight)
     if not halves:
         return lax.psum_scatter(partial, axis, scatter_dimension=0, tiled=True)
     away, own = partial

time: 79.6 us -> 76 us (0.955)
  Pallas kernels: 43 us -> 41.3 us
  other arithmetic: 2.28 us -> 1.15 us
    pallas_call x1, Pallas kernels: 9.69 us -> 8.02 us  [projected(): pl.pallas_call(project_kernel if halves else whole_kernel, in_specs=[pl.B...]
    convert_element_type x1, other arithmetic: 2.28 us -> 1.15 us  [projected(): return (own.astype(F32) + other.astype(F32)).astype(BF16)]
  transfers between devices with their start and end apart: 5 -> 5, of which waited for: 4 -> 4; matrix products, arithmetic and copies ran while one was open for 0% -> 0% of each run, Pallas kernels for 28% -> 29%
where the time goes in v4:
time: 76 us; the launch traced here: 75.5 us
  Pallas kernels  41.3 us (54%)
  starting transfers between devices  17.3 us (23%)
  waiting for transfers between devices  15.1 us (20%)
  other arithmetic  1.15 us (2%)
    pallas_call x1, Pallas kernels, local(): pl.pallas_call(local_kernel, grid=(steps,), in_specs=[columns_of(length,...  12.3 us
    pallas_call x1, Pallas kernels, local_steps(): pl.pallas_call(later_kernel, grid=(steps,), in_specs=[columns_of(length,...  9.64 us
    all_to_all x1, waiting for transfers between devices, starts_of(): lax.all_to_all(starts.reshape(heads, DK, DV), axis, 0, 0, axis_index_grou...  8.81 us
    ppermute x2, starting transfers between devices, shifted(): return lax.ppermute(value, axis, [(i, i + by) for i in range(count - by)])  8.55 us
    pallas_call x1, Pallas kernels, projected(): pl.pallas_call(project_kernel if halves else whole_kernel, in_specs=[pl.B...  8.02 us
    pallas_call x1, Pallas kernels, local_steps(): pl.pallas_call(states_kernel, grid=(1,), in_specs=[whole((CHUNK, narrow))...  7.65 us
    all_to_all x1, starting transfers between devices, starts_of(): lax.all_to_all(pairs, axis, 0, 0, axis_index_groups=groups, tiled=True)  4.75 us
    all_to_all x1, starting transfers between devices, starts_of(): lax.all_to_all(starts.reshape(heads, DK, DV), axis, 0, 0, axis_index_grou...  3.92 us
  transfers between devices with their start and end apart: 5, of which 4 were waited for; matrix products, arithmetic and copies ran while one was open for 0% of the time, Pallas kernels for 29%

profile of v4, /device:TPU:0, one launch (start us, length us, event | category | flops | bytes accessed | tf_op | source)
XLA Modules:
  0.0 75.5 jit_solution(10198703174550310279)
XLA Ops:
  0.0 1.5 %tails.1 = bf16[3,4096]{1,0:T(4,128)(2,1)} custom-call(bf16[384,2048]{1,0:T(8,128)(2,1)} %value_ref.3, bf16[384,1024]{1,0:T(8,128)(2,1)} %query_ref.1, bf16[384,1024]{1,0:T(8,128)(2,1)} %key_ref.3), custom_call_target="tpu_custom_call" | custom-call | tf_op jit(solution)/shard_map/tails/pallas_call | solution.py:617
  1.5 4.8 %collective-permute-start = (bf16[3,4096]{1,0:T(4,128)(2,1)}, bf16[3,4096]{1,0:T(4,128)(2,1)S(1)}, u32[]{:S(2)}, u32[]{:S(2)}) collective-permute-start(bf16[3,4096]{1,0:T(4,128)(2,1)} %tails.1), channel_id=1, source_target_pairs={{0,2},{2,4},{4,6},{6,8},{8,10},{10,12},{12,14},{14,16},{16,18},{18... | collective-permute-start | bytes 73736 | tf_op jit(solution)/shard_map/ppermute | solution.py:455
  6.4 9.6 %later.1 = (bf16[16,256,256]{2,1,0:T(8,128)(2,1)}, bf16[16,2,128,256]{3,2,1,0:T(8,128)(2,1)}, bf16[256,1024]{1,0:T(8,128)(2,1)}) custom-call(bf16[384,1024]{1,0:T(8,128)(2,1)} %key_ref.3, bf16[384,2048]{1,0:T(8,128)(2,1)} %value_ref.3, f32[4,1024]{1,0:T(4,128)} %key_taps.3, f32[4,2048]{1,0:T(4,128)} %value_taps.3, f32[16,384]{1,0:T(8,128)} %bitcast.11, ...), custom_call_target="tpu_custom_call" | custom-call | flops 3019898880 | tf_op jit(solution)/shard_map/later/pallas_call | solution.py:337
  16.0 0.0 collective-permute-done.key_before.value_before.query_before
  16.0 0.0 copy-start.1
  16.0 0.6 copy-done.1
  16.6 7.7 %states.1 = (bf16[16,128,256]{2,1,0:T(8,128)(2,1)}, bf16[128,1024]{1,0:T(8,128)(2,1)}, bf16[16,128,256]{2,1,0:T(8,128)(2,1)}, bf16[2,16,128,256]{3,2,1,0:T(8,128)(2,1)}) custom-call(bf16[384,1024]{1,0:T(8,128)(2,1)} %key_ref.3, bf16[384,2048]{1,0:T(8,128)(2,1)} %value_ref.3, bf16[3,4096]{1,0:T(4,128)(2,1)} %copy-done.1, bf16[3,4096]{1,0:T(4,128)(2,1)} %copy-done.1, ...), custom_call_target="tpu_custom_call" | custom-call | flops 2013265920 | tf_op jit(solution)/shard_map/states/pallas_call | solution.py:363
  24.3 4.8 %all-to-all-start = ((bf16[16,128,256]{2,1,0:T(8,128)(2,1)}), bf16[16,128,256]{2,1,0:T(8,128)(2,1)S(1)}, u32[]{:S(2)}, u32[]{:S(2)}) async-start(bf16[16,128,256]{2,1,0:T(8,128)(2,1)} %get-tuple-element.22), calls=%async_computation | async-start | bytes 2097152 | tf_op jit(solution)/shard_map/all_to_all | solution.py:478
  29.0 12.3 %local.1 = (bf16[16,384,256]{2,1,0:T(8,128)(2,1)}, bf16[384,2048]{1,0:T(8,128)(2,1)}) custom-call(bf16[384,1024]{1,0:T(8,128)(2,1)} %query_ref.1, bf16[3,4096]{1,0:T(4,128)(2,1)} %copy-done.1, f32[4,1024]{1,0:T(4,128)} %query_taps.1, bf16[128,1024]{1,0:T(8,128)(2,1)} %get-tuple-element.23.first_unit, bf16[256,1024]{1,0:T(8,128)(2,1)} %get-tuple-element.24.later_unit, ...), custom_call_target="tpu_custom_call" | custom-call | flops 1207959552 | tf_op jit(solution)/shard_map/local/pallas_call | solution.py:396
  41.3 2.1 %all-to-all-done = bf16[16,128,256]{2,1,0:T(8,128)(2,1)S(1)} async-done(((bf16[16,128,256]{2,1,0:T(8,128)(2,1)}), bf16[16,128,256]{2,1,0:T(8,128)(2,1)S(1)}, u32[]{:S(2)}, u32[]{:S(2)}) %all-to-all-start) | async-done | bytes 1048608 | tf_op jit(solution)/shard_map/all_to_all | solution.py:478
  43.4 1.1 %prefix.1 = (bf16[8,2,128,256]{3,2,1,0:T(8,128)(2,1)S(1)}, bf16[2,128,128]{2,1,0:T(8,128)(2,1)S(1)}) custom-call(bf16[8,2,128,256]{3,2,1,0:T(8,128)(2,1)S(1)} %bitcast.6), custom_call_target="tpu_custom_call" | custom-call | tf_op jit(solution)/shard_map/prefix/pallas_call | solution.py:480
  44.6 0.0 copy-start
  44.6 3.7 %collective-permute-start.1 = (bf16[2,128,128]{2,1,0:T(8,128)(2,1)S(1)}, bf16[2,128,128]{2,1,0:T(8,128)(2,1)S(1)}, u32[]{:S(2)}, u32[]{:S(2)}) collective-permute-start(bf16[2,128,128]{2,1,0:T(8,128)(2,1)S(1)} %get-tuple-element.32), channel_id=1, source_target_pairs={{0,16},{2,18},{4,20},{6,22},{8,24},{10,26},{12,28},{14,30},{1,17},... | collective-permute-start | bytes 196616 | tf_op jit(solution)/shard_map/ppermute | solution.py:455
  48.3 1.9 %collective-permute-done.1.start_ref = bf16[2,128,128]{2,1,0:T(8,128)(2,1)S(1)} collective-permute-done((bf16[2,128,128]{2,1,0:T(8,128)(2,1)S(1)}, bf16[2,128,128]{2,1,0:T(8,128)(2,1)S(1)}, u32[]{:S(2)}, u32[]{:S(2)}) %collective-permute-start.1) | collective-permute-done | bytes 65568 | tf_op jit(solution)/shard_map/ppermute | solution.py:455
  50.2 1.1 %apply.1 = bf16[8,2,128,128]{3,2,1,0:T(8,128)(2,1)} custom-call(bf16[8,2,128,256]{3,2,1,0:T(8,128)(2,1)S(1)} %get-tuple-element.31.prefix_ref, bf16[2,128,128]{2,1,0:T(8,128)(2,1)S(1)} %collective-permute-done.1.start_ref), custom_call_target="tpu_custom_call" | custom-call | tf_op jit(solution)/shard_map/apply/pallas_call | solution.py:489
  51.3 3.9 %all-to-all-start.1 = ((bf16[16,128,128]{2,1,0:T(8,128)(2,1)}), bf16[16,128,128]{2,1,0:T(8,128)(2,1)S(1)}, u32[]{:S(2)}, u32[]{:S(2)}) async-start(bf16[16,128,128]{2,1,0:T(8,128)(2,1)} %bitcast.5), calls=%async_computation.1 | async-start | bytes 1048576 | tf_op jit(solution)/shard_map/all_to_all | solution.py:495
  55.2 8.8 %all-to-all-done.1.starts_ref = bf16[16,128,128]{2,1,0:T(8,128)(2,1)S(1)} async-done(((bf16[16,128,128]{2,1,0:T(8,128)(2,1)}), bf16[16,128,128]{2,1,0:T(8,128)(2,1)S(1)}, u32[]{:S(2)}, u32[]{:S(2)}) %all-to-all-start.1) | async-done | bytes 524320 | tf_op jit(solution)/shard_map/all_to_all | solution.py:495
  64.0 0.0 copy-done
  64.0 8.0 %project.1 = (bf16[192,2048]{1,0:T(8,128)(2,1)S(1)}, bf16[192,2048]{1,0:T(8,128)(2,1)S(1)}) custom-call(s32[1]{0:T(128)} %bitcast.place_ref, bf16[16,128,128]{2,1,0:T(8,128)(2,1)S(1)} %all-to-all-done.1.starts_ref, bf16[384,2048]{1,0:T(8,128)(2,1)S(1)} %copy-done, bf16[16,384,256]{2,1,0:T(8,128)(2,1)} %get-tuple-element.34.parts_hbm, ...), custom_call_target="tpu_custom_call" | custom-call | tf_op jit(solution)/shard_map/project/pallas_call | solution.py:576
  72.0 0.1 collective-permute-start.2
  72.1 2.3 %collective-permute-done.2 = bf16[192,2048]{1,0:T(8,128)(2,1)S(1)} collective-permute-done((bf16[192,2048]{1,0:T(8,128)(2,1)S(1)}, bf16[192,2048]{1,0:T(8,128)(2,1)S(1)}, u32[]{:S(2)}, u32[]{:S(2)}) %collective-permute-start.2) | collective-permute-done | bytes 786464 | tf_op jit(solution)/shard_map/ppermute | solution.py:594
  74.4 1.2 %add_convert_fusion = bf16[192,2048]{1,0:T(8,128)(2,1)} fusion(bf16[192,2048]{1,0:T(8,128)(2,1)S(1)} %collective-permute-done.2, bf16[192,2048]{1,0:T(8,128)(2,1)S(1)} %get-tuple-element.35), kind=kLoop, calls=%fused_computation | loop fusion | flops 1572864 | bytes 2359296 | tf_op jit(solution)/shard_map/convert_element_type | solution.py:595
Async XLA Ops:
  1.5 14.5 %collective-permute-start = (bf16[3,4096]{1,0:T(4,128)(2,1)}, bf16[3,4096]{1,0:T(4,128)(2,1)S(1)}, u32[]{:S(2)}, u32[]{:S(2)}) collective-permute-start(bf16[3,4096]{1,0:T(4,128)(2,1)} %tails.1), channel_id=1, source_target_pairs={{0,2},{2,4},{4,6},{6,8},{8,10},{10,12},{12,14},{14,16},{16,18},{18... | collective-permute-start | bytes 73736 | tf_op jit(solution)/shard_map/ppermute | solution.py:455
  16.0 0.6 copy-start.1
  24.3 19.1 %all-to-all-start = ((bf16[16,128,256]{2,1,0:T(8,128)(2,1)}), bf16[16,128,256]{2,1,0:T(8,128)(2,1)S(1)}, u32[]{:S(2)}, u32[]{:S(2)}) async-start(bf16[16,128,256]{2,1,0:T(8,128)(2,1)} %get-tuple-element.22), calls=%async_computation | async-start | bytes 2097152 | tf_op jit(solution)/shard_map/all_to_all | solution.py:478
  44.6 19.4 %copy-start = (bf16[384,2048]{1,0:T(8,128)(2,1)S(1)}, bf16[384,2048]{1,0:T(8,128)(2,1)}, u32[]{:S(2)}) copy-start(bf16[384,2048]{1,0:T(8,128)(2,1)} %get-tuple-element.33.gated_ref) | copy-start | bytes 4718596
  44.6 5.6 %collective-permute-start.1 = (bf16[2,128,128]{2,1,0:T(8,128)(2,1)S(1)}, bf16[2,128,128]{2,1,0:T(8,128)(2,1)S(1)}, u32[]{:S(2)}, u32[]{:S(2)}) collective-permute-start(bf16[2,128,128]{2,1,0:T(8,128)(2,1)S(1)} %get-tuple-element.32), channel_id=1, source_target_pairs={{0,16},{2,18},{4,20},{6,22},{8,24},{10,26},{12,28},{14,30},{1,17},... | collective-permute-start | bytes 196616 | tf_op jit(solution)/shard_map/ppermute | solution.py:455
  51.3 12.7 %all-to-all-start.1 = ((bf16[16,128,128]{2,1,0:T(8,128)(2,1)}), bf16[16,128,128]{2,1,0:T(8,128)(2,1)S(1)}, u32[]{:S(2)}, u32[]{:S(2)}) async-start(bf16[16,128,128]{2,1,0:T(8,128)(2,1)} %bitcast.5), calls=%async_computation.1 | async-start | bytes 1048576 | tf_op jit(solution)/shard_map/all_to_all | solution.py:495
  72.0 2.4 %collective-permute-start.2 = (bf16[192,2048]{1,0:T(8,128)(2,1)S(1)}, bf16[192,2048]{1,0:T(8,128)(2,1)S(1)}, u32[]{:S(2)}, u32[]{:S(2)}) collective-permute-start(bf16[192,2048]{1,0:T(8,128)(2,1)S(1)} %get-tuple-element.36), channel_id=1, source_target_pairs={{0,1},{1,0},{2,3},{3,2},{4,5},{5,4},{6,7},{7,6},{8,9},{9,8},{10,11... | collective-permute-start | bytes 2359304 | tf_op jit(solution)/shard_map/ppermute | solution.py:594

commit v5 on v4

--- a/solution.py
+++ b/solution.py
@@ -1,3 +1,4 @@
+import functools
 import math
 
 import jax
@@ -80,8 +81,17 @@
     return jnp.concatenate(list(blocks) + [jnp.zeros((CHUNK - rows, CHUNK), F32)], 0).T
 
 
-def solved_packs(fade, beta, keys, key_cols, values):
+def solved_packs(fade, beta, keys, key_cols, value_work, value_of):
     count = len(keys)
+    stages = 9
+    done = [0, 0]
+
+    def between():
+        done[1] += 1
+        while done[0] < len(value_work) and done[0] * stages < len(value_work) * done[1]:
+            value_work[done[0]]()
+            done[0] += 1
+
     rows, cols = square_iotas()
     strict = rows > cols
     differ = rows ^ cols
@@ -125,11 +135,14 @@
             inside = [spread(jnp.where(band, one, 0.0).astype(BF16)) for one in small]
             inverse16 = [one.astype(BF16) for one in inverse]
             wide16 = [spread(one) for one in inverse16]
+        between()
         step = [mul(inverse16[p], inside[p]).astype(BF16) for p in range(count)]
+        between()
         both = [
             mul(step[p], jnp.concatenate([step[p] if last else spread(step[p]), wide16[p]], 1))
             for p in range(count)
         ]
+        between()
         inverse = [inverse[p] - both[p][:, CHUNK:] for p in range(count)]
         partial = [inverse[p].astype(BF16) for p in range(count)]
         inverse = [
@@ -142,7 +155,7 @@
     for p in range(count):
         right = jnp.concatenate(
             [
-                columns[:, count + p : count + p + 1] * values[p],
+                columns[:, count + p : count + p + 1] * value_of(p),
                 columns[:, 2 * count + p : 2 * count + p + 1] * keys[p],
             ],
             1,
@@ -172,14 +185,23 @@
         for chunk in chunks:
             key[chunk, j] = unit[part_of(chunk - 1)]
             turned[chunk, j] = key[chunk, j].T
-    value = [conv_silu(value_padded, 13, count, value_taps, head) for head in range(heads)]
+    value = {}
+
+    def make_value(head):
+        value[head] = conv_silu(value_padded, 13, count, value_taps, head)
+
+    def value_of(pack):
+        chunk, head = packs[pack]
+        return value[head][part_of(chunk - 1)]
+
     fade = log_fades(chunk_rows(decay_ref, heads, chunks))
     solved = solved_packs(
         fade,
         sigmoid(chunk_rows(beta_ref, heads, chunks)),
         [key[chunk, head // repeat_by] for chunk, head in packs],
         [turned[chunk, head // repeat_by] for chunk, head in packs],
-        [value[head][part_of(chunk - 1)] for chunk, head in packs],
+        [functools.partial(make_value, head) for head in range(heads)],
+        value_of,
     )
     tail = jnp.exp(fade[:, CHUNK - 1 : CHUNK] - fade)
     for pack, (chunk, head) in enumerate(packs):
@@ -212,12 +234,18 @@
         unit_ref[:, head_of(j)] = key[j].astype(BF16)
         turned.append(key[j].T)
     fade = log_fades(chunk_rows(decay_ref, heads, range(chunks)))
+    value = {}
+
+    def make_value(head):
+        value[head] = conv_silu(value_padded, 5, CHUNK, value_taps, head)
+
     solved = solved_packs(
         fade[:heads],
         sigmoid(beta_ref[:, :CHUNK]),
         [key[head // repeat_by] for head in range(heads)],
         [turned[head // repeat_by] for head in range(heads)],
-        [conv_silu(value_padded, 5, CHUNK, value_taps, head) for head in range(heads)],
+        [functools.partial(make_value, head) for head in range(heads)],
+        lambda head: value[head],
     )
     last = jnp.exp(fade[:, CHUNK - 1 : CHUNK])
     tail = jnp.exp(fade[:, CHUNK - 1 : CHUNK] - fade)
@@ -531,11 +559,13 @@
     parts(0).wait()
     if groups > 1:
         parts(1).start()
+        weights(1).start()
     following = normed_group(0)
     for g in range(groups):
         weights(g).wait()
+        if g + 2 < groups:
+            weights(g + 2).start()
         if g + 1 < groups:
-            weights(g + 1).start()
             parts(g + 1).wait()
         if g + 2 < groups:
             parts(g + 2).start()

time: 76 us -> 75.5 us (level)
  no operation moved by 1% of the time
where the time goes in v5:
time: 75.5 us; the launch traced here: 75.1 us
  Pallas kernels  40.9 us (54%)
  starting transfers between devices  17.3 us (23%)
  waiting for transfers between devices  15.1 us (20%)
  other arithmetic  1.15 us (2%)
    pallas_call x1, Pallas kernels, local(): pl.pallas_call(local_kernel, grid=(steps,), in_specs=[columns_of(length,...  12.3 us
    pallas_call x1, Pallas kernels, local_steps(): pl.pallas_call(later_kernel, grid=(steps,), in_specs=[columns_of(length,...  9.63 us
    all_to_all x1, waiting for transfers between devices, starts_of(): lax.all_to_all(starts.reshape(heads, DK, DV), axis, 0, 0, axis_index_grou...  8.81 us
    ppermute x2, starting transfers between devices, shifted(): return lax.ppermute(value, axis, [(i, i + by) for i in range(count - by)])  8.54 us
    pallas_call x1, Pallas kernels, local_steps(): pl.pallas_call(states_kernel, grid=(1,), in_specs=[whole((CHUNK, narrow))...  7.66 us
    pallas_call x1, Pallas kernels, projected(): pl.pallas_call(project_kernel if halves else whole_kernel, in_specs=[pl.B...  7.58 us
    all_to_all x1, starting transfers between devices, starts_of(): lax.all_to_all(pairs, axis, 0, 0, axis_index_groups=groups, tiled=True)  4.75 us
    all_to_all x1, starting transfers between devices, starts_of(): lax.all_to_all(starts.reshape(heads, DK, DV), axis, 0, 0, axis_index_grou...  3.92 us
  transfers between devices with their start and end apart: 5, of which 4 were waited for; matrix products, arithmetic and copies ran while one was open for 0% of the time, Pallas kernels for 29%

profile of v5, /device:TPU:0, one launch (start us, length us, event | category | flops | bytes accessed | tf_op | source)
XLA Modules:
  0.0 75.1 jit_solution(8541293857281130640)
XLA Ops:
  0.0 1.5 %tails.1 = bf16[3,4096]{1,0:T(4,128)(2,1)} custom-call(bf16[384,2048]{1,0:T(8,128)(2,1)} %value_ref.3, bf16[384,1024]{1,0:T(8,128)(2,1)} %query_ref.1, bf16[384,1024]{1,0:T(8,128)(2,1)} %key_ref.3), custom_call_target="tpu_custom_call" | custom-call | tf_op jit(solution)/shard_map/tails/pallas_call | solution.py:647
  1.5 4.8 %collective-permute-start = (bf16[3,4096]{1,0:T(4,128)(2,1)}, bf16[3,4096]{1,0:T(4,128)(2,1)S(1)}, u32[]{:S(2)}, u32[]{:S(2)}) collective-permute-start(bf16[3,4096]{1,0:T(4,128)(2,1)} %tails.1), channel_id=1, source_target_pairs={{0,2},{2,4},{4,6},{6,8},{8,10},{10,12},{12,14},{14,16},{16,18},{18... | collective-permute-start | bytes 73736 | tf_op jit(solution)/shard_map/ppermute | solution.py:483
  6.4 9.6 %later.1 = (bf16[16,256,256]{2,1,0:T(8,128)(2,1)}, bf16[16,2,128,256]{3,2,1,0:T(8,128)(2,1)}, bf16[256,1024]{1,0:T(8,128)(2,1)}) custom-call(bf16[384,1024]{1,0:T(8,128)(2,1)} %key_ref.3, bf16[384,2048]{1,0:T(8,128)(2,1)} %value_ref.3, f32[4,1024]{1,0:T(4,128)} %key_taps.3, f32[4,2048]{1,0:T(4,128)} %value_taps.3, f32[16,384]{1,0:T(8,128)} %bitcast.11, ...), custom_call_target="tpu_custom_call" | custom-call | flops 3019898880 | tf_op jit(solution)/shard_map/later/pallas_call | solution.py:365
  16.0 0.0 collective-permute-done.key_before.value_before.query_before
  16.0 0.0 copy-start.1
  16.0 0.6 copy-done.1
  16.6 7.7 %states.1 = (bf16[16,128,256]{2,1,0:T(8,128)(2,1)}, bf16[128,1024]{1,0:T(8,128)(2,1)}, bf16[16,128,256]{2,1,0:T(8,128)(2,1)}, bf16[2,16,128,256]{3,2,1,0:T(8,128)(2,1)}) custom-call(bf16[384,1024]{1,0:T(8,128)(2,1)} %key_ref.3, bf16[384,2048]{1,0:T(8,128)(2,1)} %value_ref.3, bf16[3,4096]{1,0:T(4,128)(2,1)} %copy-done.1, bf16[3,4096]{1,0:T(4,128)(2,1)} %copy-done.1, ...), custom_call_target="tpu_custom_call" | custom-call | flops 2013265920 | tf_op jit(solution)/shard_map/states/pallas_call | solution.py:391
  24.3 4.8 %all-to-all-start = ((bf16[16,128,256]{2,1,0:T(8,128)(2,1)}), bf16[16,128,256]{2,1,0:T(8,128)(2,1)S(1)}, u32[]{:S(2)}, u32[]{:S(2)}) async-start(bf16[16,128,256]{2,1,0:T(8,128)(2,1)} %get-tuple-element.22), calls=%async_computation | async-start | bytes 2097152 | tf_op jit(solution)/shard_map/all_to_all | solution.py:506
  29.0 12.3 %local.1 = (bf16[16,384,256]{2,1,0:T(8,128)(2,1)}, bf16[384,2048]{1,0:T(8,128)(2,1)}) custom-call(bf16[384,1024]{1,0:T(8,128)(2,1)} %query_ref.1, bf16[3,4096]{1,0:T(4,128)(2,1)} %copy-done.1, f32[4,1024]{1,0:T(4,128)} %query_taps.1, bf16[128,1024]{1,0:T(8,128)(2,1)} %get-tuple-element.23.first_unit, bf16[256,1024]{1,0:T(8,128)(2,1)} %get-tuple-element.24.later_unit, ...), custom_call_target="tpu_custom_call" | custom-call | flops 1207959552 | tf_op jit(solution)/shard_map/local/pallas_call | solution.py:424
  41.3 2.1 %all-to-all-done = bf16[16,128,256]{2,1,0:T(8,128)(2,1)S(1)} async-done(((bf16[16,128,256]{2,1,0:T(8,128)(2,1)}), bf16[16,128,256]{2,1,0:T(8,128)(2,1)S(1)}, u32[]{:S(2)}, u32[]{:S(2)}) %all-to-all-start) | async-done | bytes 1048608 | tf_op jit(solution)/shard_map/all_to_all | solution.py:506
  43.4 1.1 %prefix.1 = (bf16[8,2,128,256]{3,2,1,0:T(8,128)(2,1)S(1)}, bf16[2,128,128]{2,1,0:T(8,128)(2,1)S(1)}) custom-call(bf16[8,2,128,256]{3,2,1,0:T(8,128)(2,1)S(1)} %bitcast.6), custom_call_target="tpu_custom_call" | custom-call | tf_op jit(solution)/shard_map/prefix/pallas_call | solution.py:508
  44.6 0.0 copy-start
  44.6 3.7 %collective-permute-start.1 = (bf16[2,128,128]{2,1,0:T(8,128)(2,1)S(1)}, bf16[2,128,128]{2,1,0:T(8,128)(2,1)S(1)}, u32[]{:S(2)}, u32[]{:S(2)}) collective-permute-start(bf16[2,128,128]{2,1,0:T(8,128)(2,1)S(1)} %get-tuple-element.32), channel_id=1, source_target_pairs={{0,16},{2,18},{4,20},{6,22},{8,24},{10,26},{12,28},{14,30},{1,17},... | collective-permute-start | bytes 196616 | tf_op jit(solution)/shard_map/ppermute | solution.py:483
  48.3 1.9 %collective-permute-done.1.start_ref = bf16[2,128,128]{2,1,0:T(8,128)(2,1)S(1)} collective-permute-done((bf16[2,128,128]{2,1,0:T(8,128)(2,1)S(1)}, bf16[2,128,128]{2,1,0:T(8,128)(2,1)S(1)}, u32[]{:S(2)}, u32[]{:S(2)}) %collective-permute-start.1) | collective-permute-done | bytes 65568 | tf_op jit(solution)/shard_map/ppermute | solution.py:483
  50.2 1.1 %apply.1 = bf16[8,2,128,128]{3,2,1,0:T(8,128)(2,1)} custom-call(bf16[8,2,128,256]{3,2,1,0:T(8,128)(2,1)S(1)} %get-tuple-element.31.prefix_ref, bf16[2,128,128]{2,1,0:T(8,128)(2,1)S(1)} %collective-permute-done.1.start_ref), custom_call_target="tpu_custom_call" | custom-call | tf_op jit(solution)/shard_map/apply/pallas_call | solution.py:517
  51.3 3.9 %all-to-all-start.1 = ((bf16[16,128,128]{2,1,0:T(8,128)(2,1)}), bf16[16,128,128]{2,1,0:T(8,128)(2,1)S(1)}, u32[]{:S(2)}, u32[]{:S(2)}) async-start(bf16[16,128,128]{2,1,0:T(8,128)(2,1)} %bitcast.5), calls=%async_computation.1 | async-start | bytes 1048576 | tf_op jit(solution)/shard_map/all_to_all | solution.py:523
  55.2 8.8 %all-to-all-done.1.starts_ref = bf16[16,128,128]{2,1,0:T(8,128)(2,1)S(1)} async-done(((bf16[16,128,128]{2,1,0:T(8,128)(2,1)}), bf16[16,128,128]{2,1,0:T(8,128)(2,1)S(1)}, u32[]{:S(2)}, u32[]{:S(2)}) %all-to-all-start.1) | async-done | bytes 524320 | tf_op jit(solution)/shard_map/all_to_all | solution.py:523
  64.0 0.0 copy-done
  64.0 7.6 %project.1 = (bf16[192,2048]{1,0:T(8,128)(2,1)S(1)}, bf16[192,2048]{1,0:T(8,128)(2,1)S(1)}) custom-call(s32[1]{0:T(128)} %bitcast.place_ref, bf16[16,128,128]{2,1,0:T(8,128)(2,1)S(1)} %all-to-all-done.1.starts_ref, bf16[384,2048]{1,0:T(8,128)(2,1)S(1)} %copy-done, bf16[16,384,256]{2,1,0:T(8,128)(2,1)} %get-tuple-element.34.parts_hbm, ...), custom_call_target="tpu_custom_call" | custom-call | tf_op jit(solution)/shard_map/project/pallas_call | solution.py:606
  71.6 0.1 collective-permute-start.2
  71.6 2.3 %collective-permute-done.2 = bf16[192,2048]{1,0:T(8,128)(2,1)S(1)} collective-permute-done((bf16[192,2048]{1,0:T(8,128)(2,1)S(1)}, bf16[192,2048]{1,0:T(8,128)(2,1)S(1)}, u32[]{:S(2)}, u32[]{:S(2)}) %collective-permute-start.2) | collective-permute-done | bytes 786464 | tf_op jit(solution)/shard_map/ppermute | solution.py:624
  73.9 1.2 %add_convert_fusion = bf16[192,2048]{1,0:T(8,128)(2,1)} fusion(bf16[192,2048]{1,0:T(8,128)(2,1)S(1)} %collective-permute-done.2, bf16[192,2048]{1,0:T(8,128)(2,1)S(1)} %get-tuple-element.35), kind=kLoop, calls=%fused_computation | loop fusion | flops 1572864 | bytes 2359296 | tf_op jit(solution)/shard_map/convert_element_type | solution.py:625
Async XLA Ops:
  1.5 14.5 %collective-permute-start = (bf16[3,4096]{1,0:T(4,128)(2,1)}, bf16[3,4096]{1,0:T(4,128)(2,1)S(1)}, u32[]{:S(2)}, u32[]{:S(2)}) collective-permute-start(bf16[3,4096]{1,0:T(4,128)(2,1)} %tails.1), channel_id=1, source_target_pairs={{0,2},{2,4},{4,6},{6,8},{8,10},{10,12},{12,14},{14,16},{16,18},{18... | collective-permute-start | bytes 73736 | tf_op jit(solution)/shard_map/ppermute | solution.py:483
  16.0 0.6 copy-start.1
  24.3 19.2 %all-to-all-start = ((bf16[16,128,256]{2,1,0:T(8,128)(2,1)}), bf16[16,128,256]{2,1,0:T(8,128)(2,1)S(1)}, u32[]{:S(2)}, u32[]{:S(2)}) async-start(bf16[16,128,256]{2,1,0:T(8,128)(2,1)} %get-tuple-element.22), calls=%async_computation | async-start | bytes 2097152 | tf_op jit(solution)/shard_map/all_to_all | solution.py:506
  44.6 19.4 %copy-start = (bf16[384,2048]{1,0:T(8,128)(2,1)S(1)}, bf16[384,2048]{1,0:T(8,128)(2,1)}, u32[]{:S(2)}) copy-start(bf16[384,2048]{1,0:T(8,128)(2,1)} %get-tuple-element.33.gated_ref) | copy-start | bytes 4718596
  44.6 5.6 %collective-permute-start.1 = (bf16[2,128,128]{2,1,0:T(8,128)(2,1)S(1)}, bf16[2,128,128]{2,1,0:T(8,128)(2,1)S(1)}, u32[]{:S(2)}, u32[]{:S(2)}) collective-permute-start(bf16[2,128,128]{2,1,0:T(8,128)(2,1)S(1)} %get-tuple-element.32), channel_id=1, source_target_pairs={{0,16},{2,18},{4,20},{6,22},{8,24},{10,26},{12,28},{14,30},{1,17},... | collective-permute-start | bytes 196616 | tf_op jit(solution)/shard_map/ppermute | solution.py:483
  51.3 12.7 %all-to-all-start.1 = ((bf16[16,128,128]{2,1,0:T(8,128)(2,1)}), bf16[16,128,128]{2,1,0:T(8,128)(2,1)S(1)}, u32[]{:S(2)}, u32[]{:S(2)}) async-start(bf16[16,128,128]{2,1,0:T(8,128)(2,1)} %bitcast.5), calls=%async_computation.1 | async-start | bytes 1048576 | tf_op jit(solution)/shard_map/all_to_all | solution.py:523
  71.6 2.4 %collective-permute-start.2 = (bf16[192,2048]{1,0:T(8,128)(2,1)S(1)}, bf16[192,2048]{1,0:T(8,128)(2,1)S(1)}, u32[]{:S(2)}, u32[]{:S(2)}) collective-permute-start(bf16[192,2048]{1,0:T(8,128)(2,1)S(1)} %get-tuple-element.36), channel_id=1, source_target_pairs={{0,1},{1,0},{2,3},{3,2},{4,5},{5,4},{6,7},{7,6},{8,9},{9,8},{10,11... | collective-permute-start | bytes 2359304 | tf_op jit(solution)/shard_map/ppermute | solution.py:624

commit v6 on v5

--- a/solution.py
+++ b/solution.py
@@ -79,6 +79,23 @@
 def as_columns(blocks):
     rows = sum(block.shape[0] for block in blocks)
     return jnp.concatenate(list(blocks) + [jnp.zeros((CHUNK - rows, CHUNK), F32)], 0).T
+
+
+def each_mul(lefts, rights):
+    return [mul(left, right) for left, right in zip(lefts, rights)]
+
+
+def paired_mul(lefts, rights):
+    products = []
+    for p in range(0, len(lefts), 2):
+        if p + 1 == len(lefts):
+            return products + [mul(lefts[p], rights[p])]
+        rows = lefts[p].shape[0]
+        both = mul(
+            jnp.concatenate([lefts[p], lefts[p + 1]], 0), jnp.concatenate([rights[p], rights[p + 1]], 1)
+        )
+        products += [both[:rows, :CHUNK], both[rows:, CHUNK:]]
+    return products
 
 
 def solved_packs(fade, beta, keys, key_cols, value_work, value_of):
@@ -136,7 +153,7 @@
             inverse16 = [one.astype(BF16) for one in inverse]
             wide16 = [spread(one) for one in inverse16]
         between()
-        step = [mul(inverse16[p], inside[p]).astype(BF16) for p in range(count)]
+        step = [one.astype(BF16) for one in (each_mul if last else paired_mul)(inverse16, inside)]
         between()
         both = [
             mul(step[p], jnp.concatenate([step[p] if last else spread(step[p]), wide16[p]], 1))
@@ -145,10 +162,12 @@
         between()
         inverse = [inverse[p] - both[p][:, CHUNK:] for p in range(count)]
         partial = [inverse[p].astype(BF16) for p in range(count)]
-        inverse = [
-            inverse[p] + mul(both[p][:, :CHUNK], partial[p] if last else spread(partial[p]))
-            for p in range(count)
-        ]
+        squared = [one[:, :CHUNK] for one in both]
+        if last:
+            added = each_mul(squared, partial)
+        else:
+            added = paired_mul(squared, [spread(one) for one in partial])
+        inverse = [inverse[p] + added[p] for p in range(count)]
         size *= 4
 
     solved = []
@@ -166,8 +185,9 @@
 
 def later_kernel(
     key_ref, value_ref, key_taps, value_taps, beta_ref, decay_ref,
-    solved_ref, moves_ref, unit_ref, key_padded, value_padded,
+    solved_hbm, moves_hbm, unit_ref, key_padded, value_padded, solved_ref, moves_ref, sem,
 ):
+    step, steps = pl.program_id(0), pl.num_programs(0)
     length, width = key_ref.shape
     chunks = range(1, length // CHUNK)
     key_heads = width // DK
@@ -184,7 +204,7 @@
         unit_ref[:, head_of(j)] = unit.astype(BF16)
         for chunk in chunks:
             key[chunk, j] = unit[part_of(chunk - 1)]
-            turned[chunk, j] = key[chunk, j].T
+            turned[chunk, j] = key[chunk, j].astype(BF16).T
     value = {}
 
     def make_value(head):
@@ -204,18 +224,31 @@
         value_of,
     )
     tail = jnp.exp(fade[:, CHUNK - 1 : CHUNK] - fade)
+
+    def leaving(held, out, at_step, kind):
+        here = pl.ds(at_step * heads, heads)
+        return pltpu.make_async_copy(held.at[here], out.at[here], sem.at[kind, at_step])
+
     for pack, (chunk, head) in enumerate(packs):
-        one = solved[pack].astype(BF16)
-        solved_ref[head, part_of(chunk - 1), :] = one
-        moves_ref[head, chunk - 1] = mul(
-            turned[chunk, head // repeat_by] * tail[pack : pack + 1, :], one
+        solved_ref[step * heads + head, part_of(chunk - 1), :] = solved[pack].astype(BF16)
+    leaving(solved_ref, solved_hbm, step, 0).start()
+    for pack, (chunk, head) in enumerate(packs):
+        moves_ref[step * heads + head, chunk - 1] = mul(
+            turned[chunk, head // repeat_by].astype(F32) * tail[pack : pack + 1, :], solved[pack]
         ).astype(BF16)
+    leaving(moves_ref, moves_hbm, step, 1).start()
+
+    @pl.when(step == steps - 1)
+    def _():
+        for at_step in range(sem.shape[1]):
+            leaving(solved_ref, solved_hbm, at_step, 0).wait()
+            leaving(moves_ref, moves_hbm, at_step, 1).wait()
 
 
 def states_kernel(
     key_ref, value_ref, key_before, value_before, key_taps, value_taps, beta_ref, decay_ref, moves_hbm,
-    pairs_ref, unit_ref, solved_hbm, starts_hbm,
-    key_padded, value_padded, moves_ref, solved_ref, starts_ref, in_sem, out_sem,
+    pairs_hbm, unit_ref, solved_hbm, starts_hbm,
+    key_padded, value_padded, moves_ref, solved_ref, starts_ref, pairs_ref, in_sem, out_sem, pairs_sem,
 ):
     heads, length = decay_ref.shape
     chunks = length // CHUNK
@@ -232,7 +265,7 @@
     for j in range(key_heads):
         key.append(unit_rows(conv_silu(key_padded, 5, CHUNK, key_taps, j)))
         unit_ref[:, head_of(j)] = key[j].astype(BF16)
-        turned.append(key[j].T)
+        turned.append(key[j].astype(BF16).T)
     fade = log_fades(chunk_rows(decay_ref, heads, range(chunks)))
     value = {}
 
@@ -256,10 +289,11 @@
     for head in range(heads):
         one = solved[head].astype(BF16)
         solved_ref[head] = one
-        moved = mul(turned[head // repeat_by] * tail[head : head + 1, :], one)
+        moved = mul(turned[head // repeat_by].astype(F32) * tail[head : head + 1, :], one)
         state.append(
             jnp.concatenate([moved[:, :DV], last[head : head + 1, :] * identity - moved[:, DV:]], 1)
         )
+    each = min(HEADS_AT_ONCE, heads)
     outgoing = [pltpu.make_async_copy(solved_ref, solved_hbm, out_sem.at[0])]
     outgoing[0].start()
     incoming.wait()
@@ -271,14 +305,22 @@
             moves = moves_ref[head, chunk - 1]
             moved = last[pack : pack + 1, :] * state[head] - mul(moves[:, DV:], start)
             state[head] = jnp.concatenate([moved[:, :DV] + moves[:, :DV].astype(F32), moved[:, DV:]], 1)
+            if chunk == chunks - 1:
+                pairs_ref[head] = state[head].astype(BF16)
+                if (head + 1) % each == 0:
+                    done = pl.ds(head + 1 - each, each)
+                    outgoing.append(
+                        pltpu.make_async_copy(
+                            pairs_ref.at[done], pairs_hbm.at[done], pairs_sem.at[head // each]
+                        )
+                    )
+                    outgoing[-1].start()
         outgoing.append(
             pltpu.make_async_copy(
                 starts_ref.at[chunk - 1], starts_hbm.at[chunk - 1], out_sem.at[chunk]
             )
         )
         outgoing[-1].start()
-    for head in range(heads):
-        pairs_ref[head] = state[head].astype(BF16)
     for copy in outgoing:
         copy.wait()
 
@@ -369,9 +411,7 @@
             columns_of(length, narrow), columns_of(length, wide),
             columns_of(4, narrow), columns_of(4, wide), logits, logits,
         ],
-        out_specs=[
-            of_heads(later, DV + DK), of_heads(chunks - 1, DK, DV + DK), columns_of(later, narrow),
-        ],
+        out_specs=[hbm, hbm, columns_of(later, narrow)],
         out_shape=[
             jax.ShapeDtypeStruct((value_heads, later, DV + DK), BF16),
             jax.ShapeDtypeStruct((value_heads, chunks - 1, DK, DV + DK), BF16),
@@ -380,6 +420,9 @@
         scratch_shapes=[
             pltpu.VMEM((each, later + 16, DK), F32),
             pltpu.VMEM((each * repeat_by, later + 16, DV), F32),
+            pltpu.VMEM((value_heads, later, DV + DK), BF16),
+            pltpu.VMEM((value_heads, chunks - 1, DK, DV + DK), BF16),
+            pltpu.SemaphoreType.DMA((2, steps)),
         ],
         compiler_params=in_vmem(60),
         cost_estimate=pl.CostEstimate(flops=30 * work, bytes_accessed=0, transcendentals=0),
@@ -396,7 +439,7 @@
             whole((3, narrow), 0, repeat_by + 1), whole((3, wide)),
             whole(taps[1].shape), whole(taps[2].shape), whole(beta.shape), whole(decay.shape), hbm,
         ],
-        out_specs=[whole((value_heads, DK, DV + DK)), whole((CHUNK, narrow)), hbm, hbm],
+        out_specs=[hbm, whole((CHUNK, narrow)), hbm, hbm],
         out_shape=[
             jax.ShapeDtypeStruct((value_heads, DK, DV + DK), BF16),
             jax.ShapeDtypeStruct((CHUNK, narrow), BF16),
@@ -409,8 +452,10 @@
             pltpu.VMEM(moves.shape, BF16),
             pltpu.VMEM((value_heads, CHUNK, DV + DK), BF16),
             pltpu.VMEM((chunks - 1, value_heads, DK, DV + DK), BF16),
+            pltpu.VMEM((value_heads, DK, DV + DK), BF16),
             pltpu.SemaphoreType.DMA,
             pltpu.SemaphoreType.DMA((chunks,)),
+            pltpu.SemaphoreType.DMA((value_heads // min(HEADS_AT_ONCE, value_heads),)),
         ],
         compiler_params=in_vmem(54),
         cost_estimate=pl.CostEstimate(flops=20 * work, bytes_accessed=0, transcendentals=0),

time: 75.5 us -> 76.1 us (level)
  transfers between devices with their start and end apart: 5 -> 5, of which waited for: 4 -> 4; matrix products, arithmetic and copies ran while one was open for 0% -> 0% of each run, Pallas kernels for 29% -> 30%
where the time goes in v6:
time: 76.1 us; the launch traced here: 75.6 us
  Pallas kernels  41.4 us (54%)
  starting transfers between devices  17.3 us (23%)
  waiting for transfers between devices  15.1 us (20%)
  other arithmetic  1.15 us (2%)
    pallas_call x1, Pallas kernels, local(): pl.pallas_call(local_kernel, grid=(steps,), in_specs=[columns_of(length,...  12.3 us
    pallas_call x1, Pallas kernels, local_steps(): pl.pallas_call(later_kernel, grid=(steps,), in_specs=[columns_of(length,...  10.2 us
    all_to_all x1, waiting for transfers between devices, starts_of(): lax.all_to_all(starts.reshape(heads, DK, DV), axis, 0, 0, axis_index_grou...  8.8 us
    ppermute x2, starting transfers between devices, shifted(): return lax.ppermute(value, axis, [(i, i + by) for i in range(count - by)])  8.54 us
    pallas_call x1, Pallas kernels, local_steps(): pl.pallas_call(states_kernel, grid=(1,), in_specs=[whole((CHUNK, narrow))...  7.6 us
    pallas_call x1, Pallas kernels, projected(): pl.pallas_call(project_kernel if halves else whole_kernel, in_specs=[pl.B...  7.59 us
    all_to_all x1, starting transfers between devices, starts_of(): lax.all_to_all(pairs, axis, 0, 0, axis_index_groups=groups, tiled=True)  4.75 us
    all_to_all x1, starting transfers between devices, starts_of(): lax.all_to_all(starts.reshape(heads, DK, DV), axis, 0, 0, axis_index_grou...  3.92 us
  transfers between devices with their start and end apart: 5, of which 4 were waited for; matrix products, arithmetic and copies ran while one was open for 0% of the time, Pallas kernels for 30%

profile of v6, /device:TPU:0, one launch (start us, length us, event | category | flops | bytes accessed | tf_op | source)
XLA Modules:
  0.0 75.6 jit_solution(17045204597163305898)
XLA Ops:
  0.0 1.5 %tails.1 = bf16[3,4096]{1,0:T(4,128)(2,1)} custom-call(bf16[384,2048]{1,0:T(8,128)(2,1)} %value_ref.3, bf16[384,1024]{1,0:T(8,128)(2,1)} %query_ref.1, bf16[384,1024]{1,0:T(8,128)(2,1)} %key_ref.3), custom_call_target="tpu_custom_call" | custom-call | tf_op jit(solution)/shard_map/tails/pallas_call | solution.py:692
  1.5 4.8 %collective-permute-start = (bf16[3,4096]{1,0:T(4,128)(2,1)}, bf16[3,4096]{1,0:T(4,128)(2,1)S(1)}, u32[]{:S(2)}, u32[]{:S(2)}) collective-permute-start(bf16[3,4096]{1,0:T(4,128)(2,1)} %tails.1), channel_id=1, source_target_pairs={{0,2},{2,4},{4,6},{6,8},{8,10},{10,12},{12,14},{14,16},{16,18},{18... | collective-permute-start | bytes 73736 | tf_op jit(solution)/shard_map/ppermute | solution.py:528
  6.4 10.2 %later.1 = (bf16[16,256,256]{2,1,0:T(8,128)(2,1)}, bf16[16,2,128,256]{3,2,1,0:T(8,128)(2,1)}, bf16[256,1024]{1,0:T(8,128)(2,1)}) custom-call(bf16[384,1024]{1,0:T(8,128)(2,1)} %key_ref.3, bf16[384,2048]{1,0:T(8,128)(2,1)} %value_ref.3, f32[4,1024]{1,0:T(4,128)} %key_taps.3, f32[4,2048]{1,0:T(4,128)} %value_taps.3, f32[16,384]{1,0:T(8,128)} %bitcast.11, ...), custom_call_target="tpu_custom_call" | custom-call | flops 3019898880 | tf_op jit(solution)/shard_map/later/pallas_call | solution.py:407
  16.6 0.0 collective-permute-done.key_before.value_before.query_before
  16.6 0.0 copy-start.1
  16.6 0.6 copy-done.1
  17.2 7.6 %states.1 = (bf16[16,128,256]{2,1,0:T(8,128)(2,1)}, bf16[128,1024]{1,0:T(8,128)(2,1)}, bf16[16,128,256]{2,1,0:T(8,128)(2,1)}, bf16[2,16,128,256]{3,2,1,0:T(8,128)(2,1)}) custom-call(bf16[384,1024]{1,0:T(8,128)(2,1)} %key_ref.3, bf16[384,2048]{1,0:T(8,128)(2,1)} %value_ref.3, bf16[3,4096]{1,0:T(4,128)(2,1)} %copy-done.1, bf16[3,4096]{1,0:T(4,128)(2,1)} %copy-done.1, ...), custom_call_target="tpu_custom_call" | custom-call | flops 2013265920 | tf_op jit(solution)/shard_map/states/pallas_call | solution.py:434
  24.8 4.7 %all-to-all-start = ((bf16[16,128,256]{2,1,0:T(8,128)(2,1)}), bf16[16,128,256]{2,1,0:T(8,128)(2,1)S(1)}, u32[]{:S(2)}, u32[]{:S(2)}) async-start(bf16[16,128,256]{2,1,0:T(8,128)(2,1)} %get-tuple-element.22), calls=%async_computation | async-start | bytes 2097152 | tf_op jit(solution)/shard_map/all_to_all | solution.py:551
  29.6 12.3 %local.1 = (bf16[16,384,256]{2,1,0:T(8,128)(2,1)}, bf16[384,2048]{1,0:T(8,128)(2,1)}) custom-call(bf16[384,1024]{1,0:T(8,128)(2,1)} %query_ref.1, bf16[3,4096]{1,0:T(4,128)(2,1)} %copy-done.1, f32[4,1024]{1,0:T(4,128)} %query_taps.1, bf16[128,1024]{1,0:T(8,128)(2,1)} %get-tuple-element.23.first_unit, bf16[256,1024]{1,0:T(8,128)(2,1)} %get-tuple-element.24.later_unit, ...), custom_call_target="tpu_custom_call" | custom-call | flops 1207959552 | tf_op jit(solution)/shard_map/local/pallas_call | solution.py:469
  41.8 2.1 %all-to-all-done = bf16[16,128,256]{2,1,0:T(8,128)(2,1)S(1)} async-done(((bf16[16,128,256]{2,1,0:T(8,128)(2,1)}), bf16[16,128,256]{2,1,0:T(8,128)(2,1)S(1)}, u32[]{:S(2)}, u32[]{:S(2)}) %all-to-all-start) | async-done | bytes 1048608 | tf_op jit(solution)/shard_map/all_to_all | solution.py:551
  44.0 1.1 %prefix.1 = (bf16[8,2,128,256]{3,2,1,0:T(8,128)(2,1)S(1)}, bf16[2,128,128]{2,1,0:T(8,128)(2,1)S(1)}) custom-call(bf16[8,2,128,256]{3,2,1,0:T(8,128)(2,1)S(1)} %bitcast.6), custom_call_target="tpu_custom_call" | custom-call | tf_op jit(solution)/shard_map/prefix/pallas_call | solution.py:553
  45.1 0.0 copy-start
  45.1 3.7 %collective-permute-start.1 = (bf16[2,128,128]{2,1,0:T(8,128)(2,1)S(1)}, bf16[2,128,128]{2,1,0:T(8,128)(2,1)S(1)}, u32[]{:S(2)}, u32[]{:S(2)}) collective-permute-start(bf16[2,128,128]{2,1,0:T(8,128)(2,1)S(1)} %get-tuple-element.32), channel_id=1, source_target_pairs={{0,16},{2,18},{4,20},{6,22},{8,24},{10,26},{12,28},{14,30},{1,17},... | collective-permute-start | bytes 196616 | tf_op jit(solution)/shard_map/ppermute | solution.py:528
  48.8 1.9 %collective-permute-done.1.start_ref = bf16[2,128,128]{2,1,0:T(8,128)(2,1)S(1)} collective-permute-done((bf16[2,128,128]{2,1,0:T(8,128)(2,1)S(1)}, bf16[2,128,128]{2,1,0:T(8,128)(2,1)S(1)}, u32[]{:S(2)}, u32[]{:S(2)}) %collective-permute-start.1) | collective-permute-done | bytes 65568 | tf_op jit(solution)/shard_map/ppermute | solution.py:528
  50.7 1.1 %apply.1 = bf16[8,2,128,128]{3,2,1,0:T(8,128)(2,1)} custom-call(bf16[8,2,128,256]{3,2,1,0:T(8,128)(2,1)S(1)} %get-tuple-element.31.prefix_ref, bf16[2,128,128]{2,1,0:T(8,128)(2,1)S(1)} %collective-permute-done.1.start_ref), custom_call_target="tpu_custom_call" | custom-call | tf_op jit(solution)/shard_map/apply/pallas_call | solution.py:562
  51.8 3.9 %all-to-all-start.1 = ((bf16[16,128,128]{2,1,0:T(8,128)(2,1)}), bf16[16,128,128]{2,1,0:T(8,128)(2,1)S(1)}, u32[]{:S(2)}, u32[]{:S(2)}) async-start(bf16[16,128,128]{2,1,0:T(8,128)(2,1)} %bitcast.5), calls=%async_computation.1 | async-start | bytes 1048576 | tf_op jit(solution)/shard_map/all_to_all | solution.py:568
  55.7 8.8 %all-to-all-done.1.starts_ref = bf16[16,128,128]{2,1,0:T(8,128)(2,1)S(1)} async-done(((bf16[16,128,128]{2,1,0:T(8,128)(2,1)}), bf16[16,128,128]{2,1,0:T(8,128)(2,1)S(1)}, u32[]{:S(2)}, u32[]{:S(2)}) %all-to-all-start.1) | async-done | bytes 524320 | tf_op jit(solution)/shard_map/all_to_all | solution.py:568
  64.5 0.0 copy-done
  64.5 7.6 %project.1 = (bf16[192,2048]{1,0:T(8,128)(2,1)S(1)}, bf16[192,2048]{1,0:T(8,128)(2,1)S(1)}) custom-call(s32[1]{0:T(128)} %bitcast.place_ref, bf16[16,128,128]{2,1,0:T(8,128)(2,1)S(1)} %all-to-all-done.1.starts_ref, bf16[384,2048]{1,0:T(8,128)(2,1)S(1)} %copy-done, bf16[16,384,256]{2,1,0:T(8,128)(2,1)} %get-tuple-element.34.parts_hbm, ...), custom_call_target="tpu_custom_call" | custom-call | tf_op jit(solution)/shard_map/project/pallas_call | solution.py:651
  72.1 0.1 collective-permute-start.2
  72.2 2.3 %collective-permute-done.2 = bf16[192,2048]{1,0:T(8,128)(2,1)S(1)} collective-permute-done((bf16[192,2048]{1,0:T(8,128)(2,1)S(1)}, bf16[192,2048]{1,0:T(8,128)(2,1)S(1)}, u32[]{:S(2)}, u32[]{:S(2)}) %collective-permute-start.2) | collective-permute-done | bytes 786464 | tf_op jit(solution)/shard_map/ppermute | solution.py:669
  74.5 1.2 %add_convert_fusion = bf16[192,2048]{1,0:T(8,128)(2,1)} fusion(bf16[192,2048]{1,0:T(8,128)(2,1)S(1)} %collective-permute-done.2, bf16[192,2048]{1,0:T(8,128)(2,1)S(1)} %get-tuple-element.35), kind=kLoop, calls=%fused_computation | loop fusion | flops 1572864 | bytes 2359296 | tf_op jit(solution)/shard_map/convert_element_type | solution.py:670
Async XLA Ops:
  1.5 15.1 %collective-permute-start = (bf16[3,4096]{1,0:T(4,128)(2,1)}, bf16[3,4096]{1,0:T(4,128)(2,1)S(1)}, u32[]{:S(2)}, u32[]{:S(2)}) collective-permute-start(bf16[3,4096]{1,0:T(4,128)(2,1)} %tails.1), channel_id=1, source_target_pairs={{0,2},{2,4},{4,6},{6,8},{8,10},{10,12},{12,14},{14,16},{16,18},{18... | collective-permute-start | bytes 73736 | tf_op jit(solution)/shard_map/ppermute | solution.py:528
  16.6 0.6 copy-start.1
  24.8 19.1 %all-to-all-start = ((bf16[16,128,256]{2,1,0:T(8,128)(2,1)}), bf16[16,128,256]{2,1,0:T(8,128)(2,1)S(1)}, u32[]{:S(2)}, u32[]{:S(2)}) async-start(bf16[16,128,256]{2,1,0:T(8,128)(2,1)} %get-tuple-element.22), calls=%async_computation | async-start | bytes 2097152 | tf_op jit(solution)/shard_map/all_to_all | solution.py:551
  45.1 19.4 %copy-start = (bf16[384,2048]{1,0:T(8,128)(2,1)S(1)}, bf16[384,2048]{1,0:T(8,128)(2,1)}, u32[]{:S(2)}) copy-start(bf16[384,2048]{1,0:T(8,128)(2,1)} %get-tuple-element.33.gated_ref) | copy-start | bytes 4718596
  45.1 5.6 %collective-permute-start.1 = (bf16[2,128,128]{2,1,0:T(8,128)(2,1)S(1)}, bf16[2,128,128]{2,1,0:T(8,128)(2,1)S(1)}, u32[]{:S(2)}, u32[]{:S(2)}) collective-permute-start(bf16[2,128,128]{2,1,0:T(8,128)(2,1)S(1)} %get-tuple-element.32), channel_id=1, source_target_pairs={{0,16},{2,18},{4,20},{6,22},{8,24},{10,26},{12,28},{14,30},{1,17},... | collective-permute-start | bytes 196616 | tf_op jit(solution)/shard_map/ppermute | solution.py:528
  51.8 12.7 %all-to-all-start.1 = ((bf16[16,128,128]{2,1,0:T(8,128)(2,1)}), bf16[16,128,128]{2,1,0:T(8,128)(2,1)S(1)}, u32[]{:S(2)}, u32[]{:S(2)}) async-start(bf16[16,128,128]{2,1,0:T(8,128)(2,1)} %bitcast.5), calls=%async_computation.1 | async-start | bytes 1048576 | tf_op jit(solution)/shard_map/all_to_all | solution.py:568
  72.1 2.4 %collective-permute-start.2 = (bf16[192,2048]{1,0:T(8,128)(2,1)S(1)}, bf16[192,2048]{1,0:T(8,128)(2,1)S(1)}, u32[]{:S(2)}, u32[]{:S(2)}) collective-permute-start(bf16[192,2048]{1,0:T(8,128)(2,1)S(1)} %get-tuple-element.36), channel_id=1, source_target_pairs={{0,1},{1,0},{2,3},{3,2},{4,5},{5,4},{6,7},{7,6},{8,9},{9,8},{10,11... | collective-permute-start | bytes 2359304 | tf_op jit(solution)/shard_map/ppermute | solution.py:669

commit v7 on v5

--- a/solution.py
+++ b/solution.py
@@ -11,6 +11,7 @@
 DK = 128
 DV = 128
 CHUNK = 128
+TINY = 8
 SMALL = 32
 GROUP = 8
 HEADS_AT_ONCE = 4
@@ -81,9 +82,35 @@
     return jnp.concatenate(list(blocks) + [jnp.zeros((CHUNK - rows, CHUNK), F32)], 0).T
 
 
+def tiny_inverses(lower):
+    lanes = lax.broadcasted_iota(jnp.int32, (TINY, CHUNK), 1)
+    rows = lax.broadcasted_iota(jnp.int32, (TINY, CHUNK), 0)
+    blocks = []
+    for low in lower:
+        block = low[:TINY]
+        for at in range(1, CHUNK // TINY):
+            block = jnp.where(lanes // TINY == at, low[at * TINY : (at + 1) * TINY], block)
+        blocks.append(block)
+    stacked = jnp.concatenate(blocks, 0)
+    all_lanes = lax.broadcasted_iota(jnp.int32, stacked.shape, 1)
+    factors = [
+        jnp.take_along_axis(
+            stacked, all_lanes // TINY * TINY + c, axis=1, mode="promise_in_bounds"
+        )
+        for c in range(TINY - 1)
+    ]
+    inverses = []
+    for p in range(len(lower)):
+        inverse = jnp.where(lanes % TINY == rows, 1.0, 0.0)
+        for c in range(TINY - 1):
+            inverse = inverse - factors[c][p * TINY : (p + 1) * TINY] * inverse[c : c + 1]
+        inverses.append(inverse)
+    return inverses
+
+
 def solved_packs(fade, beta, keys, key_cols, value_work, value_of):
     count = len(keys)
-    stages = 9
+    stages = 6
     done = [0, 0]
 
     def between():
@@ -96,7 +123,10 @@
     strict = rows > cols
     differ = rows ^ cols
     columns = as_columns((fade, beta, beta * jnp.exp(fade)))
-    inner = {id(key): mul(key, turned) for key, turned in zip(keys, key_cols)}
+    inner = {}
+    for key, turned in zip(keys, key_cols):
+        if id(key) not in inner:
+            inner[id(key)] = mul(key, turned)
     lower = []
     for p in range(count):
         gap = columns[:, p : p + 1] - fade[p : p + 1, :]
@@ -118,10 +148,12 @@
         for at in range(1, CHUNK // SMALL):
             held = jnp.where(place == at, low[at * SMALL : (at + 1) * SMALL], held)
         small.append(held)
+    tiny_inverse = tiny_inverses(lower)
+    held = (small_cols % SMALL) // TINY == small_rows // TINY
     inverse = [
-        jnp.where(small_differ == 0, 1.0, jnp.where(small_differ == 1, -one, 0.0)) for one in small
+        jnp.where(held, jnp.concatenate([one] * (SMALL // TINY), 0), 0.0) for one in tiny_inverse
     ]
-    size = 2
+    size = TINY
     while size < CHUNK:
         last = size == SMALL
         if last:
@@ -214,8 +246,8 @@
 
 def states_kernel(
     key_ref, value_ref, key_before, value_before, key_taps, value_taps, beta_ref, decay_ref, moves_hbm,
-    pairs_ref, unit_ref, solved_hbm, starts_hbm,
-    key_padded, value_padded, moves_ref, solved_ref, starts_ref, in_sem, out_sem,
+    pairs_hbm, unit_ref, solved_hbm, starts_hbm,
+    key_padded, value_padded, moves_ref, solved_ref, starts_ref, pairs_ref, in_sem, out_sem, pairs_sem,
 ):
     heads, length = decay_ref.shape
     chunks = length // CHUNK
@@ -260,6 +292,7 @@
         state.append(
             jnp.concatenate([moved[:, :DV], last[head : head + 1, :] * identity - moved[:, DV:]], 1)
         )
+    each = min(HEADS_AT_ONCE, heads)
     outgoing = [pltpu.make_async_copy(solved_ref, solved_hbm, out_sem.at[0])]
     outgoing[0].start()
     incoming.wait()
@@ -271,14 +304,22 @@
             moves = moves_ref[head, chunk - 1]
             moved = last[pack : pack + 1, :] * state[head] - mul(moves[:, DV:], start)
             state[head] = jnp.concatenate([moved[:, :DV] + moves[:, :DV].astype(F32), moved[:, DV:]], 1)
+            if chunk == chunks - 1:
+                pairs_ref[head] = state[head].astype(BF16)
+                if (head + 1) % each == 0:
+                    done = pl.ds(head + 1 - each, each)
+                    outgoing.append(
+                        pltpu.make_async_copy(
+                            pairs_ref.at[done], pairs_hbm.at[done], pairs_sem.at[head // each]
+                        )
+                    )
+                    outgoing[-1].start()
         outgoing.append(
             pltpu.make_async_copy(
                 starts_ref.at[chunk - 1], starts_hbm.at[chunk - 1], out_sem.at[chunk]
             )
         )
         outgoing[-1].start()
-    for head in range(heads):
-        pairs_ref[head] = state[head].astype(BF16)
     for copy in outgoing:
         copy.wait()
 
@@ -396,7 +437,7 @@
             whole((3, narrow), 0, repeat_by + 1), whole((3, wide)),
             whole(taps[1].shape), whole(taps[2].shape), whole(beta.shape), whole(decay.shape), hbm,
         ],
-        out_specs=[whole((value_heads, DK, DV + DK)), whole((CHUNK, narrow)), hbm, hbm],
+        out_specs=[hbm, whole((CHUNK, narrow)), hbm, hbm],
         out_shape=[
             jax.ShapeDtypeStruct((value_heads, DK, DV + DK), BF16),
             jax.ShapeDtypeStruct((CHUNK, narrow), BF16),
@@ -409,8 +450,10 @@
             pltpu.VMEM(moves.shape, BF16),
             pltpu.VMEM((value_heads, CHUNK, DV + DK), BF16),
             pltpu.VMEM((chunks - 1, value_heads, DK, DV + DK), BF16),
+            pltpu.VMEM((value_heads, DK, DV + DK), BF16),
             pltpu.SemaphoreType.DMA,
             pltpu.SemaphoreType.DMA((chunks,)),
+            pltpu.SemaphoreType.DMA((value_heads // min(HEADS_AT_ONCE, value_heads),)),
         ],
         compiler_params=in_vmem(54),
         cost_estimate=pl.CostEstimate(flops=20 * work, bytes_accessed=0, transcendentals=0),

time: 75.5 us -> 75.1 us (level)
  no operation moved by 1% of the time
where the time goes in v7:
time: 75.1 us; the launch traced here: 74.7 us
  Pallas kernels  40.5 us (54%)
  starting transfers between devices  17.3 us (23%)
  waiting for transfers between devices  15.1 us (20%)
  other arithmetic  1.15 us (2%)
    pallas_call x1, Pallas kernels, local(): pl.pallas_call(local_kernel, grid=(steps,), in_specs=[columns_of(length,...  12.3 us
    pallas_call x1, Pallas kernels, local_steps(): pl.pallas_call(later_kernel, grid=(steps,), in_specs=[columns_of(length,...  9.41 us
    all_to_all x1, waiting for transfers between devices, starts_of(): lax.all_to_all(starts.reshape(heads, DK, DV), axis, 0, 0, axis_index_grou...  8.8 us
    ppermute x2, starting transfers between devices, shifted(): return lax.ppermute(value, axis, [(i, i + by) for i in range(count - by)])  8.54 us
    pallas_call x1, Pallas kernels, projected(): pl.pallas_call(project_kernel if halves else whole_kernel, in_specs=[pl.B...  7.58 us
    pallas_call x1, Pallas kernels, local_steps(): pl.pallas_call(states_kernel, grid=(1,), in_specs=[whole((CHUNK, narrow))...  7.47 us
    all_to_all x1, starting transfers between devices, starts_of(): lax.all_to_all(pairs, axis, 0, 0, axis_index_groups=groups, tiled=True)  4.75 us
    all_to_all x1, starting transfers between devices, starts_of(): lax.all_to_all(starts.reshape(heads, DK, DV), axis, 0, 0, axis_index_grou...  3.92 us
  transfers between devices with their start and end apart: 5, of which 4 were waited for; matrix products, arithmetic and copies ran while one was open for 0% of the time, Pallas kernels for 29%

profile of v7, /device:TPU:0, one launch (start us, length us, event | category | flops | bytes accessed | tf_op | source)
XLA Modules:
  0.0 74.7 jit_solution(13811690766402692995)
XLA Ops:
  0.0 1.5 %tails.1 = bf16[3,4096]{1,0:T(4,128)(2,1)} custom-call(bf16[384,2048]{1,0:T(8,128)(2,1)} %value_ref.3, bf16[384,1024]{1,0:T(8,128)(2,1)} %query_ref.1, bf16[384,1024]{1,0:T(8,128)(2,1)} %key_ref.3), custom_call_target="tpu_custom_call" | custom-call | tf_op jit(solution)/shard_map/tails/pallas_call | solution.py:690
  1.5 4.8 %collective-permute-start = (bf16[3,4096]{1,0:T(4,128)(2,1)}, bf16[3,4096]{1,0:T(4,128)(2,1)S(1)}, u32[]{:S(2)}, u32[]{:S(2)}) collective-permute-start(bf16[3,4096]{1,0:T(4,128)(2,1)} %tails.1), channel_id=1, source_target_pairs={{0,2},{2,4},{4,6},{6,8},{8,10},{10,12},{12,14},{14,16},{16,18},{18... | collective-permute-start | bytes 73736 | tf_op jit(solution)/shard_map/ppermute | solution.py:526
  6.4 9.4 %later.1 = (bf16[16,256,256]{2,1,0:T(8,128)(2,1)}, bf16[16,2,128,256]{3,2,1,0:T(8,128)(2,1)}, bf16[256,1024]{1,0:T(8,128)(2,1)}) custom-call(bf16[384,1024]{1,0:T(8,128)(2,1)} %key_ref.3, bf16[384,2048]{1,0:T(8,128)(2,1)} %value_ref.3, f32[4,1024]{1,0:T(4,128)} %key_taps.3, f32[4,2048]{1,0:T(4,128)} %value_taps.3, f32[16,384]{1,0:T(8,128)} %bitcast.11, ...), custom_call_target="tpu_custom_call" | custom-call | flops 3019898880 | tf_op jit(solution)/shard_map/later/pallas_call | solution.py:406
  15.8 0.0 collective-permute-done.key_before.value_before.query_before
  15.8 0.0 copy-start.1
  15.8 0.6 copy-done.1
  16.4 7.5 %states.1 = (bf16[16,128,256]{2,1,0:T(8,128)(2,1)}, bf16[128,1024]{1,0:T(8,128)(2,1)}, bf16[16,128,256]{2,1,0:T(8,128)(2,1)}, bf16[2,16,128,256]{3,2,1,0:T(8,128)(2,1)}) custom-call(bf16[384,1024]{1,0:T(8,128)(2,1)} %key_ref.3, bf16[384,2048]{1,0:T(8,128)(2,1)} %value_ref.3, bf16[3,4096]{1,0:T(4,128)(2,1)} %copy-done.1, bf16[3,4096]{1,0:T(4,128)(2,1)} %copy-done.1, ...), custom_call_target="tpu_custom_call" | custom-call | flops 2013265920 | tf_op jit(solution)/shard_map/states/pallas_call | solution.py:432
  23.9 4.8 %all-to-all-start = ((bf16[16,128,256]{2,1,0:T(8,128)(2,1)}), bf16[16,128,256]{2,1,0:T(8,128)(2,1)S(1)}, u32[]{:S(2)}, u32[]{:S(2)}) async-start(bf16[16,128,256]{2,1,0:T(8,128)(2,1)} %get-tuple-element.22), calls=%async_computation | async-start | bytes 2097152 | tf_op jit(solution)/shard_map/all_to_all | solution.py:549
  28.6 12.3 %local.1 = (bf16[16,384,256]{2,1,0:T(8,128)(2,1)}, bf16[384,2048]{1,0:T(8,128)(2,1)}) custom-call(bf16[384,1024]{1,0:T(8,128)(2,1)} %query_ref.1, bf16[3,4096]{1,0:T(4,128)(2,1)} %copy-done.1, f32[4,1024]{1,0:T(4,128)} %query_taps.1, bf16[128,1024]{1,0:T(8,128)(2,1)} %get-tuple-element.23.first_unit, bf16[256,1024]{1,0:T(8,128)(2,1)} %get-tuple-element.24.later_unit, ...), custom_call_target="tpu_custom_call" | custom-call | flops 1207959552 | tf_op jit(solution)/shard_map/local/pallas_call | solution.py:467
  40.9 2.1 %all-to-all-done = bf16[16,128,256]{2,1,0:T(8,128)(2,1)S(1)} async-done(((bf16[16,128,256]{2,1,0:T(8,128)(2,1)}), bf16[16,128,256]{2,1,0:T(8,128)(2,1)S(1)}, u32[]{:S(2)}, u32[]{:S(2)}) %all-to-all-start) | async-done | bytes 1048608 | tf_op jit(solution)/shard_map/all_to_all | solution.py:549
  43.0 1.1 %prefix.1 = (bf16[8,2,128,256]{3,2,1,0:T(8,128)(2,1)S(1)}, bf16[2,128,128]{2,1,0:T(8,128)(2,1)S(1)}) custom-call(bf16[8,2,128,256]{3,2,1,0:T(8,128)(2,1)S(1)} %bitcast.6), custom_call_target="tpu_custom_call" | custom-call | tf_op jit(solution)/shard_map/prefix/pallas_call | solution.py:551
  44.2 0.0 copy-start
  44.2 3.7 %collective-permute-start.1 = (bf16[2,128,128]{2,1,0:T(8,128)(2,1)S(1)}, bf16[2,128,128]{2,1,0:T(8,128)(2,1)S(1)}, u32[]{:S(2)}, u32[]{:S(2)}) collective-permute-start(bf16[2,128,128]{2,1,0:T(8,128)(2,1)S(1)} %get-tuple-element.32), channel_id=1, source_target_pairs={{0,16},{2,18},{4,20},{6,22},{8,24},{10,26},{12,28},{14,30},{1,17},... | collective-permute-start | bytes 196616 | tf_op jit(solution)/shard_map/ppermute | solution.py:526
  47.9 1.9 %collective-permute-done.1.start_ref = bf16[2,128,128]{2,1,0:T(8,128)(2,1)S(1)} collective-permute-done((bf16[2,128,128]{2,1,0:T(8,128)(2,1)S(1)}, bf16[2,128,128]{2,1,0:T(8,128)(2,1)S(1)}, u32[]{:S(2)}, u32[]{:S(2)}) %collective-permute-start.1) | collective-permute-done | bytes 65568 | tf_op jit(solution)/shard_map/ppermute | solution.py:526
  49.8 1.1 %apply.1 = bf16[8,2,128,128]{3,2,1,0:T(8,128)(2,1)} custom-call(bf16[8,2,128,256]{3,2,1,0:T(8,128)(2,1)S(1)} %get-tuple-element.31.prefix_ref, bf16[2,128,128]{2,1,0:T(8,128)(2,1)S(1)} %collective-permute-done.1.start_ref), custom_call_target="tpu_custom_call" | custom-call | tf_op jit(solution)/shard_map/apply/pallas_call | solution.py:560
  50.8 3.9 %all-to-all-start.1 = ((bf16[16,128,128]{2,1,0:T(8,128)(2,1)}), bf16[16,128,128]{2,1,0:T(8,128)(2,1)S(1)}, u32[]{:S(2)}, u32[]{:S(2)}) async-start(bf16[16,128,128]{2,1,0:T(8,128)(2,1)} %bitcast.5), calls=%async_computation.1 | async-start | bytes 1048576 | tf_op jit(solution)/shard_map/all_to_all | solution.py:566
  54.8 8.8 %all-to-all-done.1.starts_ref = bf16[16,128,128]{2,1,0:T(8,128)(2,1)S(1)} async-done(((bf16[16,128,128]{2,1,0:T(8,128)(2,1)}), bf16[16,128,128]{2,1,0:T(8,128)(2,1)S(1)}, u32[]{:S(2)}, u32[]{:S(2)}) %all-to-all-start.1) | async-done | bytes 524320 | tf_op jit(solution)/shard_map/all_to_all | solution.py:566
  63.6 0.0 copy-done
  63.6 7.6 %project.1 = (bf16[192,2048]{1,0:T(8,128)(2,1)S(1)}, bf16[192,2048]{1,0:T(8,128)(2,1)S(1)}) custom-call(s32[1]{0:T(128)} %bitcast.place_ref, bf16[16,128,128]{2,1,0:T(8,128)(2,1)S(1)} %all-to-all-done.1.starts_ref, bf16[384,2048]{1,0:T(8,128)(2,1)S(1)} %copy-done, bf16[16,384,256]{2,1,0:T(8,128)(2,1)} %get-tuple-element.34.parts_hbm, ...), custom_call_target="tpu_custom_call" | custom-call | tf_op jit(solution)/shard_map/project/pallas_call | solution.py:649
  71.2 0.1 collective-permute-start.2
  71.2 2.3 %collective-permute-done.2 = bf16[192,2048]{1,0:T(8,128)(2,1)S(1)} collective-permute-done((bf16[192,2048]{1,0:T(8,128)(2,1)S(1)}, bf16[192,2048]{1,0:T(8,128)(2,1)S(1)}, u32[]{:S(2)}, u32[]{:S(2)}) %collective-permute-start.2) | collective-permute-done | bytes 786464 | tf_op jit(solution)/shard_map/ppermute | solution.py:667
  73.5 1.2 %add_convert_fusion = bf16[192,2048]{1,0:T(8,128)(2,1)} fusion(bf16[192,2048]{1,0:T(8,128)(2,1)S(1)} %collective-permute-done.2, bf16[192,2048]{1,0:T(8,128)(2,1)S(1)} %get-tuple-element.35), kind=kLoop, calls=%fused_computation | loop fusion | flops 1572864 | bytes 2359296 | tf_op jit(solution)/shard_map/convert_element_type | solution.py:668
Async XLA Ops:
  1.5 14.3 %collective-permute-start = (bf16[3,4096]{1,0:T(4,128)(2,1)}, bf16[3,4096]{1,0:T(4,128)(2,1)S(1)}, u32[]{:S(2)}, u32[]{:S(2)}) collective-permute-start(bf16[3,4096]{1,0:T(4,128)(2,1)} %tails.1), channel_id=1, source_target_pairs={{0,2},{2,4},{4,6},{6,8},{8,10},{10,12},{12,14},{14,16},{16,18},{18... | collective-permute-start | bytes 73736 | tf_op jit(solution)/shard_map/ppermute | solution.py:526
  15.8 0.6 copy-start.1
  23.9 19.2 %all-to-all-start = ((bf16[16,128,256]{2,1,0:T(8,128)(2,1)}), bf16[16,128,256]{2,1,0:T(8,128)(2,1)S(1)}, u32[]{:S(2)}, u32[]{:S(2)}) async-start(bf16[16,128,256]{2,1,0:T(8,128)(2,1)} %get-tuple-element.22), calls=%async_computation | async-start | bytes 2097152 | tf_op jit(solution)/shard_map/all_to_all | solution.py:549
  44.2 19.4 %copy-start = (bf16[384,2048]{1,0:T(8,128)(2,1)S(1)}, bf16[384,2048]{1,0:T(8,128)(2,1)}, u32[]{:S(2)}) copy-start(bf16[384,2048]{1,0:T(8,128)(2,1)} %get-tuple-element.33.gated_ref) | copy-start | bytes 4718596
  44.2 5.6 %collective-permute-start.1 = (bf16[2,128,128]{2,1,0:T(8,128)(2,1)S(1)}, bf16[2,128,128]{2,1,0:T(8,128)(2,1)S(1)}, u32[]{:S(2)}, u32[]{:S(2)}) collective-permute-start(bf16[2,128,128]{2,1,0:T(8,128)(2,1)S(1)} %get-tuple-element.32), channel_id=1, source_target_pairs={{0,16},{2,18},{4,20},{6,22},{8,24},{10,26},{12,28},{14,30},{1,17},... | collective-permute-start | bytes 196616 | tf_op jit(solution)/shard_map/ppermute | solution.py:526
  50.8 12.7 %all-to-all-start.1 = ((bf16[16,128,128]{2,1,0:T(8,128)(2,1)}), bf16[16,128,128]{2,1,0:T(8,128)(2,1)S(1)}, u32[]{:S(2)}, u32[]{:S(2)}) async-start(bf16[16,128,128]{2,1,0:T(8,128)(2,1)} %bitcast.5), calls=%async_computation.1 | async-start | bytes 1048576 | tf_op jit(solution)/shard_map/all_to_all | solution.py:566
  71.2 2.4 %collective-permute-start.2 = (bf16[192,2048]{1,0:T(8,128)(2,1)S(1)}, bf16[192,2048]{1,0:T(8,128)(2,1)S(1)}, u32[]{:S(2)}, u32[]{:S(2)}) collective-permute-start(bf16[192,2048]{1,0:T(8,128)(2,1)S(1)} %get-tuple-element.36), channel_id=1, source_target_pairs={{0,1},{1,0},{2,3},{3,2},{4,5},{5,4},{6,7},{7,6},{8,9},{9,8},{10,11... | collective-permute-start | bytes 2359304 | tf_op jit(solution)/shard_map/ppermute | solution.py:667

commit v8 on v7

--- a/solution.py
+++ b/solution.py
@@ -41,8 +41,16 @@
         padded[head, first : first + rows, :] = raw[:, head_of(head)].astype(F32)
 
 
+def row_sums(values, factor):
+    return mul(values, jnp.full((CHUNK, CHUNK), factor, BF16))
+
+
 def unit_rows(key):
-    return key * lax.rsqrt(jnp.sum(key * key, -1, keepdims=True) + EPSILON)
+    return key * lax.rsqrt(row_sums(key * key, 1.0) + EPSILON)
+
+
+def softplus(x):
+    return jnp.maximum(x, 0.0) + jnp.log(1.0 + jnp.exp(-jnp.abs(x)))
 
 
 def part_of(chunk):
@@ -71,9 +79,8 @@
 
 def log_fades(logit):
     rows, cols = square_iotas()
-    decay = -(jnp.maximum(logit, 0.0) + jnp.log(1.0 + jnp.exp(-jnp.abs(logit))))
     return jnp.dot(
-        decay, (rows <= cols).astype(F32), precision=lax.Precision.HIGHEST, preferred_element_type=F32
+        -softplus(logit), (rows <= cols).astype(F32), precision=lax.Precision.HIGHEST, preferred_element_type=F32
     )
 
 
@@ -108,7 +115,7 @@
     return inverses
 
 
-def solved_packs(fade, beta, keys, key_cols, value_work, value_of):
+def solved_packs(fade, beta_logit, keys, key_cols, value_work, value_of):
     count = len(keys)
     stages = 6
     done = [0, 0]
@@ -122,7 +129,9 @@
     rows, cols = square_iotas()
     strict = rows > cols
     differ = rows ^ cols
-    columns = as_columns((fade, beta, beta * jnp.exp(fade)))
+    columns = as_columns((fade - softplus(-beta_logit),))
+    beta = sigmoid(beta_logit)
+    beta_grown = beta * jnp.exp(fade)
     inner = {}
     for key, turned in zip(keys, key_cols):
         if id(key) not in inner:
@@ -130,8 +139,7 @@
     lower = []
     for p in range(count):
         gap = columns[:, p : p + 1] - fade[p : p + 1, :]
-        ratio = jnp.exp(jnp.where(strict, gap, -1e30))
-        lower.append(columns[:, count + p : count + p + 1] * ratio * inner[id(keys[p])])
+        lower.append(jnp.exp(jnp.where(strict, gap, -1e30)) * inner[id(keys[p])])
 
     small_rows, small_cols = square_iotas(SMALL)
     small_differ = small_rows ^ (small_cols % SMALL)
@@ -183,17 +191,16 @@
         ]
         size *= 4
 
-    solved = []
-    for p in range(count):
-        right = jnp.concatenate(
+    return [
+        jnp.concatenate(
             [
-                columns[:, count + p : count + p + 1] * value_of(p),
-                columns[:, 2 * count + p : 2 * count + p + 1] * keys[p],
+                mul(inverse[p] * beta[p : p + 1, :], value_of(p)),
+                mul(inverse[p] * beta_grown[p : p + 1, :], keys[p]),
             ],
             1,
         )
-        solved.append(mul(inverse[p], right))
-    return solved
+        for p in range(count)
+    ]
 
 
 def later_kernel(
@@ -229,7 +236,7 @@
     fade = log_fades(chunk_rows(decay_ref, heads, chunks))
     solved = solved_packs(
         fade,
-        sigmoid(chunk_rows(beta_ref, heads, chunks)),
+        chunk_rows(beta_ref, heads, chunks),
         [key[chunk, head // repeat_by] for chunk, head in packs],
         [turned[chunk, head // repeat_by] for chunk, head in packs],
         [functools.partial(make_value, head) for head in range(heads)],
@@ -273,7 +280,7 @@
 
     solved = solved_packs(
         fade[:heads],
-        sigmoid(beta_ref[:, :CHUNK]),
+        beta_ref[:, :CHUNK],
         [key[head // repeat_by] for head in range(heads)],
         [turned[head // repeat_by] for head in range(heads)],
         [functools.partial(make_value, head) for head in range(heads)],
@@ -338,7 +345,7 @@
     rows, cols = square_iotas()
     within = rows >= cols
     fade = log_fades(chunk_rows(decay_ref, heads, range(chunks)))
-    columns = as_columns((fade, jnp.exp(fade)))
+    columns = as_columns((fade,))
     widen(padded, 5, 3, query_before[...])
     widen(padded, 8, length, query_ref[...])
     query = [conv_silu(padded, 5, length, query_taps, j).astype(BF16) for j in range(key_heads)]
@@ -355,9 +362,9 @@
             )
             for head in range(j * repeat_by, (j + 1) * repeat_by):
                 pack = chunk * heads + head
-                gap = columns[:, pack : pack + 1] - fade[pack : pack + 1, :]
-                scores = inner * jnp.exp(jnp.where(within, gap, -1e30))
-                grown = columns[:, chunks * heads + pack : chunks * heads + pack + 1]
+                column = jnp.broadcast_to(columns[:, pack : pack + 1], (CHUNK, CHUNK))
+                scores = inner * jnp.exp(jnp.where(within, column - fade[pack : pack + 1, :], -1e30))
+                grown = jnp.exp(column)
                 if chunk == 0:
                     updates, wide = first_solved[head, :, :DV], first_solved[head, :, DV:]
                     fresh = jnp.concatenate([updates, -wide], 1)
@@ -371,7 +378,9 @@
                     fresh = jnp.concatenate(
                         [solved[:, :DV].astype(F32) - taken[:, :DV], -taken[:, DV:]], 1
                     )
-                    carried = grown * both[CHUNK:]
+                    carried = jnp.concatenate(
+                        [grown * both[CHUNK:, :DV], grown * both[CHUNK:, DV:]], 1
+                    )
                 parts_ref[head, part, :] = (carried + mul(scores, fresh)).astype(BF16)
 
 
@@ -593,7 +602,7 @@
             core = parts_ref[head, :, :DV].astype(F32) + mul(
                 parts_ref[head, :, DV:], starts_ref[head]
             )
-            scale = lax.rsqrt(jnp.mean(core * core, -1, keepdims=True) + EPSILON)
+            scale = lax.rsqrt(row_sums(core * core, 1.0 / DV) + EPSILON)
             normed.append((core * scale * gated_ref[:, head_of(head)].astype(F32)).astype(BF16))
         return jnp.concatenate(normed, 1)
 

time: 75.1 us -> 75.5 us (level)
  no operation moved by 1% of the time
where the time goes in v8:
time: 75.5 us; the launch traced here: 75 us
  Pallas kernels  40.8 us (54%)
  starting transfers between devices  17.3 us (23%)
  waiting for transfers between devices  15.1 us (20%)
  other arithmetic  1.15 us (2%)
    pallas_call x1, Pallas kernels, local(): pl.pallas_call(local_kernel, grid=(steps,), in_specs=[columns_of(length,...  12.2 us
    pallas_call x1, Pallas kernels, local_steps(): pl.pallas_call(later_kernel, grid=(steps,), in_specs=[columns_of(length,...  9.4 us
    all_to_all x1, waiting for transfers between devices, starts_of(): lax.all_to_all(starts.reshape(heads, DK, DV), axis, 0, 0, axis_index_grou...  8.8 us
    ppermute x2, starting transfers between devices, shifted(): return lax.ppermute(value, axis, [(i, i + by) for i in range(count - by)])  8.55 us
    pallas_call x1, Pallas kernels, projected(): pl.pallas_call(project_kernel if halves else whole_kernel, in_specs=[pl.B...  7.93 us
    pallas_call x1, Pallas kernels, local_steps(): pl.pallas_call(states_kernel, grid=(1,), in_specs=[whole((CHUNK, narrow))...  7.5 us
    all_to_all x1, starting transfers between devices, starts_of(): lax.all_to_all(pairs, axis, 0, 0, axis_index_groups=groups, tiled=True)  4.75 us
    all_to_all x1, starting transfers between devices, starts_of(): lax.all_to_all(starts.reshape(heads, DK, DV), axis, 0, 0, axis_index_grou...  3.92 us
  transfers between devices with their start and end apart: 5, of which 4 were waited for; matrix products, arithmetic and copies ran while one was open for 0% of the time, Pallas kernels for 29%

profile of v8, /device:TPU:0, one launch (start us, length us, event | category | flops | bytes accessed | tf_op | source)
XLA Modules:
  0.0 75.0 jit_solution(17170281029895343431)
XLA Ops:
  0.0 1.5 %tails.1 = bf16[3,4096]{1,0:T(4,128)(2,1)} custom-call(bf16[384,2048]{1,0:T(8,128)(2,1)} %value_ref.3, bf16[384,1024]{1,0:T(8,128)(2,1)} %query_ref.1, bf16[384,1024]{1,0:T(8,128)(2,1)} %key_ref.3), custom_call_target="tpu_custom_call" | custom-call | tf_op jit(solution)/shard_map/tails/pallas_call | solution.py:699
  1.5 4.8 %collective-permute-start = (bf16[3,4096]{1,0:T(4,128)(2,1)}, bf16[3,4096]{1,0:T(4,128)(2,1)S(1)}, u32[]{:S(2)}, u32[]{:S(2)}) collective-permute-start(bf16[3,4096]{1,0:T(4,128)(2,1)} %tails.1), channel_id=1, source_target_pairs={{0,2},{2,4},{4,6},{6,8},{8,10},{10,12},{12,14},{14,16},{16,18},{18... | collective-permute-start | bytes 73736 | tf_op jit(solution)/shard_map/ppermute | solution.py:535
  6.4 9.4 %later.1 = (bf16[16,256,256]{2,1,0:T(8,128)(2,1)}, bf16[16,2,128,256]{3,2,1,0:T(8,128)(2,1)}, bf16[256,1024]{1,0:T(8,128)(2,1)}) custom-call(bf16[384,1024]{1,0:T(8,128)(2,1)} %key_ref.3, bf16[384,2048]{1,0:T(8,128)(2,1)} %value_ref.3, f32[4,1024]{1,0:T(4,128)} %key_taps.3, f32[4,2048]{1,0:T(4,128)} %value_taps.3, f32[16,384]{1,0:T(8,128)} %bitcast.11, ...), custom_call_target="tpu_custom_call" | custom-call | flops 3019898880 | tf_op jit(solution)/shard_map/later/pallas_call | solution.py:415
  15.8 0.0 collective-permute-done.key_before.value_before.query_before
  15.8 0.0 copy-start.1
  15.8 0.6 copy-done.1
  16.4 7.5 %states.1 = (bf16[16,128,256]{2,1,0:T(8,128)(2,1)}, bf16[128,1024]{1,0:T(8,128)(2,1)}, bf16[16,128,256]{2,1,0:T(8,128)(2,1)}, bf16[2,16,128,256]{3,2,1,0:T(8,128)(2,1)}) custom-call(bf16[384,1024]{1,0:T(8,128)(2,1)} %key_ref.3, bf16[384,2048]{1,0:T(8,128)(2,1)} %value_ref.3, bf16[3,4096]{1,0:T(4,128)(2,1)} %copy-done.1, bf16[3,4096]{1,0:T(4,128)(2,1)} %copy-done.1, ...), custom_call_target="tpu_custom_call" | custom-call | flops 2013265920 | tf_op jit(solution)/shard_map/states/pallas_call | solution.py:441
  23.9 4.8 %all-to-all-start = ((bf16[16,128,256]{2,1,0:T(8,128)(2,1)}), bf16[16,128,256]{2,1,0:T(8,128)(2,1)S(1)}, u32[]{:S(2)}, u32[]{:S(2)}) async-start(bf16[16,128,256]{2,1,0:T(8,128)(2,1)} %get-tuple-element.22), calls=%async_computation | async-start | bytes 2097152 | tf_op jit(solution)/shard_map/all_to_all | solution.py:558
  28.6 12.2 %local.1 = (bf16[16,384,256]{2,1,0:T(8,128)(2,1)}, bf16[384,2048]{1,0:T(8,128)(2,1)}) custom-call(bf16[384,1024]{1,0:T(8,128)(2,1)} %query_ref.1, bf16[3,4096]{1,0:T(4,128)(2,1)} %copy-done.1, f32[4,1024]{1,0:T(4,128)} %query_taps.1, bf16[128,1024]{1,0:T(8,128)(2,1)} %get-tuple-element.23.first_unit, bf16[256,1024]{1,0:T(8,128)(2,1)} %get-tuple-element.24.later_unit, ...), custom_call_target="tpu_custom_call" | custom-call | flops 1207959552 | tf_op jit(solution)/shard_map/local/pallas_call | solution.py:476
  40.9 2.2 %all-to-all-done = bf16[16,128,256]{2,1,0:T(8,128)(2,1)S(1)} async-done(((bf16[16,128,256]{2,1,0:T(8,128)(2,1)}), bf16[16,128,256]{2,1,0:T(8,128)(2,1)S(1)}, u32[]{:S(2)}, u32[]{:S(2)}) %all-to-all-start) | async-done | bytes 1048608 | tf_op jit(solution)/shard_map/all_to_all | solution.py:558
  43.0 1.1 %prefix.1 = (bf16[8,2,128,256]{3,2,1,0:T(8,128)(2,1)S(1)}, bf16[2,128,128]{2,1,0:T(8,128)(2,1)S(1)}) custom-call(bf16[8,2,128,256]{3,2,1,0:T(8,128)(2,1)S(1)} %bitcast.6), custom_call_target="tpu_custom_call" | custom-call | tf_op jit(solution)/shard_map/prefix/pallas_call | solution.py:560
  44.2 0.0 copy-start
  44.2 3.7 %collective-permute-start.1 = (bf16[2,128,128]{2,1,0:T(8,128)(2,1)S(1)}, bf16[2,128,128]{2,1,0:T(8,128)(2,1)S(1)}, u32[]{:S(2)}, u32[]{:S(2)}) collective-permute-start(bf16[2,128,128]{2,1,0:T(8,128)(2,1)S(1)} %get-tuple-element.32), channel_id=1, source_target_pairs={{0,16},{2,18},{4,20},{6,22},{8,24},{10,26},{12,28},{14,30},{1,17},... | collective-permute-start | bytes 196616 | tf_op jit(solution)/shard_map/ppermute | solution.py:535
  47.9 1.9 %collective-permute-done.1.start_ref = bf16[2,128,128]{2,1,0:T(8,128)(2,1)S(1)} collective-permute-done((bf16[2,128,128]{2,1,0:T(8,128)(2,1)S(1)}, bf16[2,128,128]{2,1,0:T(8,128)(2,1)S(1)}, u32[]{:S(2)}, u32[]{:S(2)}) %collective-permute-start.1) | collective-permute-done | bytes 65568 | tf_op jit(solution)/shard_map/ppermute | solution.py:535
  49.8 1.1 %apply.1 = bf16[8,2,128,128]{3,2,1,0:T(8,128)(2,1)} custom-call(bf16[8,2,128,256]{3,2,1,0:T(8,128)(2,1)S(1)} %get-tuple-element.31.prefix_ref, bf16[2,128,128]{2,1,0:T(8,128)(2,1)S(1)} %collective-permute-done.1.start_ref), custom_call_target="tpu_custom_call" | custom-call | tf_op jit(solution)/shard_map/apply/pallas_call | solution.py:569
  50.8 3.9 %all-to-all-start.1 = ((bf16[16,128,128]{2,1,0:T(8,128)(2,1)}), bf16[16,128,128]{2,1,0:T(8,128)(2,1)S(1)}, u32[]{:S(2)}, u32[]{:S(2)}) async-start(bf16[16,128,128]{2,1,0:T(8,128)(2,1)} %bitcast.5), calls=%async_computation.1 | async-start | bytes 1048576 | tf_op jit(solution)/shard_map/all_to_all | solution.py:575
  54.8 8.8 %all-to-all-done.1.starts_ref = bf16[16,128,128]{2,1,0:T(8,128)(2,1)S(1)} async-done(((bf16[16,128,128]{2,1,0:T(8,128)(2,1)}), bf16[16,128,128]{2,1,0:T(8,128)(2,1)S(1)}, u32[]{:S(2)}, u32[]{:S(2)}) %all-to-all-start.1) | async-done | bytes 524320 | tf_op jit(solution)/shard_map/all_to_all | solution.py:575
  63.6 0.0 copy-done
  63.6 7.9 %project.1 = (bf16[192,2048]{1,0:T(8,128)(2,1)S(1)}, bf16[192,2048]{1,0:T(8,128)(2,1)S(1)}) custom-call(s32[1]{0:T(128)} %bitcast.place_ref, bf16[16,128,128]{2,1,0:T(8,128)(2,1)S(1)} %all-to-all-done.1.starts_ref, bf16[384,2048]{1,0:T(8,128)(2,1)S(1)} %copy-done, bf16[16,384,256]{2,1,0:T(8,128)(2,1)} %get-tuple-element.34.parts_hbm, ...), custom_call_target="tpu_custom_call" | custom-call | tf_op jit(solution)/shard_map/project/pallas_call | solution.py:658
  71.5 0.1 collective-permute-start.2
  71.6 2.3 %collective-permute-done.2 = bf16[192,2048]{1,0:T(8,128)(2,1)S(1)} collective-permute-done((bf16[192,2048]{1,0:T(8,128)(2,1)S(1)}, bf16[192,2048]{1,0:T(8,128)(2,1)S(1)}, u32[]{:S(2)}, u32[]{:S(2)}) %collective-permute-start.2) | collective-permute-done | bytes 786464 | tf_op jit(solution)/shard_map/ppermute | solution.py:676
  73.9 1.2 %add_convert_fusion = bf16[192,2048]{1,0:T(8,128)(2,1)} fusion(bf16[192,2048]{1,0:T(8,128)(2,1)S(1)} %collective-permute-done.2, bf16[192,2048]{1,0:T(8,128)(2,1)S(1)} %get-tuple-element.35), kind=kLoop, calls=%fused_computation | loop fusion | flops 1572864 | bytes 2359296 | tf_op jit(solution)/shard_map/convert_element_type | solution.py:677
Async XLA Ops:
  1.5 14.3 %collective-permute-start = (bf16[3,4096]{1,0:T(4,128)(2,1)}, bf16[3,4096]{1,0:T(4,128)(2,1)S(1)}, u32[]{:S(2)}, u32[]{:S(2)}) collective-permute-start(bf16[3,4096]{1,0:T(4,128)(2,1)} %tails.1), channel_id=1, source_target_pairs={{0,2},{2,4},{4,6},{6,8},{8,10},{10,12},{12,14},{14,16},{16,18},{18... | collective-permute-start | bytes 73736 | tf_op jit(solution)/shard_map/ppermute | solution.py:535
  15.8 0.6 copy-start.1
  23.9 19.1 %all-to-all-start = ((bf16[16,128,256]{2,1,0:T(8,128)(2,1)}), bf16[16,128,256]{2,1,0:T(8,128)(2,1)S(1)}, u32[]{:S(2)}, u32[]{:S(2)}) async-start(bf16[16,128,256]{2,1,0:T(8,128)(2,1)} %get-tuple-element.22), calls=%async_computation | async-start | bytes 2097152 | tf_op jit(solution)/shard_map/all_to_all | solution.py:558
  44.2 19.4 %copy-start = (bf16[384,2048]{1,0:T(8,128)(2,1)S(1)}, bf16[384,2048]{1,0:T(8,128)(2,1)}, u32[]{:S(2)}) copy-start(bf16[384,2048]{1,0:T(8,128)(2,1)} %get-tuple-element.33.gated_ref) | copy-start | bytes 4718596
  44.2 5.6 %collective-permute-start.1 = (bf16[2,128,128]{2,1,0:T(8,128)(2,1)S(1)}, bf16[2,128,128]{2,1,0:T(8,128)(2,1)S(1)}, u32[]{:S(2)}, u32[]{:S(2)}) collective-permute-start(bf16[2,128,128]{2,1,0:T(8,128)(2,1)S(1)} %get-tuple-element.32), channel_id=1, source_target_pairs={{0,16},{2,18},{4,20},{6,22},{8,24},{10,26},{12,28},{14,30},{1,17},... | collective-permute-start | bytes 196616 | tf_op jit(solution)/shard_map/ppermute | solution.py:535
  50.8 12.7 %all-to-all-start.1 = ((bf16[16,128,128]{2,1,0:T(8,128)(2,1)}), bf16[16,128,128]{2,1,0:T(8,128)(2,1)S(1)}, u32[]{:S(2)}, u32[]{:S(2)}) async-start(bf16[16,128,128]{2,1,0:T(8,128)(2,1)} %bitcast.5), calls=%async_computation.1 | async-start | bytes 1048576 | tf_op jit(solution)/shard_map/all_to_all | solution.py:575
  71.5 2.4 %collective-permute-start.2 = (bf16[192,2048]{1,0:T(8,128)(2,1)S(1)}, bf16[192,2048]{1,0:T(8,128)(2,1)S(1)}, u32[]{:S(2)}, u32[]{:S(2)}) collective-permute-start(bf16[192,2048]{1,0:T(8,128)(2,1)S(1)} %get-tuple-element.36), channel_id=1, source_target_pairs={{0,1},{1,0},{2,3},{3,2},{4,5},{5,4},{6,7},{7,6},{8,9},{9,8},{10,11... | collective-permute-start | bytes 2359304 | tf_op jit(solution)/shard_map/ppermute | solution.py:676

commit v9 on v8

--- a/solution.py
+++ b/solution.py
@@ -41,12 +41,12 @@
         padded[head, first : first + rows, :] = raw[:, head_of(head)].astype(F32)
 
 
-def row_sums(values, factor):
-    return mul(values, jnp.full((CHUNK, CHUNK), factor, BF16))
+def row_sums(values):
+    return mul(values, jnp.ones((CHUNK, CHUNK), BF16))
 
 
 def unit_rows(key):
-    return key * lax.rsqrt(row_sums(key * key, 1.0) + EPSILON)
+    return key * lax.rsqrt(row_sums(key * key) + EPSILON)
 
 
 def softplus(x):
@@ -205,7 +205,7 @@
 
 def later_kernel(
     key_ref, value_ref, key_taps, value_taps, beta_ref, decay_ref,
-    solved_ref, moves_ref, unit_ref, key_padded, value_padded,
+    solved_ref, moves_ref, key_padded, value_padded,
 ):
     length, width = key_ref.shape
     chunks = range(1, length // CHUNK)
@@ -220,7 +220,8 @@
     key, turned = {}, {}
     for j in range(key_heads):
         unit = unit_rows(conv_silu(key_padded, 13, count, key_taps, j))
-        unit_ref[:, head_of(j)] = unit.astype(BF16)
+        for head in range(j * repeat_by, (j + 1) * repeat_by):
+            solved_ref[head, :, DV + DK :] = unit.astype(BF16)
         for chunk in chunks:
             key[chunk, j] = unit[part_of(chunk - 1)]
             turned[chunk, j] = key[chunk, j].T
@@ -245,7 +246,7 @@
     tail = jnp.exp(fade[:, CHUNK - 1 : CHUNK] - fade)
     for pack, (chunk, head) in enumerate(packs):
         one = solved[pack].astype(BF16)
-        solved_ref[head, part_of(chunk - 1), :] = one
+        solved_ref[head, part_of(chunk - 1), : DV + DK] = one
         moves_ref[head, chunk - 1] = mul(
             turned[chunk, head // repeat_by] * tail[pack : pack + 1, :], one
         ).astype(BF16)
@@ -253,7 +254,7 @@
 
 def states_kernel(
     key_ref, value_ref, key_before, value_before, key_taps, value_taps, beta_ref, decay_ref, moves_hbm,
-    pairs_hbm, unit_ref, solved_hbm, starts_hbm,
+    pairs_hbm, solved_hbm, starts_hbm,
     key_padded, value_padded, moves_ref, solved_ref, starts_ref, pairs_ref, in_sem, out_sem, pairs_sem,
 ):
     heads, length = decay_ref.shape
@@ -270,7 +271,8 @@
     key, turned = [], []
     for j in range(key_heads):
         key.append(unit_rows(conv_silu(key_padded, 5, CHUNK, key_taps, j)))
-        unit_ref[:, head_of(j)] = key[j].astype(BF16)
+        for head in range(j * repeat_by, (j + 1) * repeat_by):
+            solved_ref[head, :, DV + DK :] = key[j].astype(BF16)
         turned.append(key[j].T)
     fade = log_fades(chunk_rows(decay_ref, heads, range(chunks)))
     value = {}
@@ -294,7 +296,7 @@
     state = []
     for head in range(heads):
         one = solved[head].astype(BF16)
-        solved_ref[head] = one
+        solved_ref[head, :, : DV + DK] = one
         moved = mul(turned[head // repeat_by] * tail[head : head + 1, :], one)
         state.append(
             jnp.concatenate([moved[:, :DV], last[head : head + 1, :] * identity - moved[:, DV:]], 1)
@@ -332,7 +334,7 @@
 
 
 def local_kernel(
-    query_ref, query_before, query_taps, first_unit, later_unit, decay_ref,
+    query_ref, query_before, query_taps, decay_ref,
     first_solved, later_solved, starts_ref, gate_ref, gain_ref,
     parts_ref, gated_ref, padded,
 ):
@@ -356,7 +358,10 @@
         part = part_of(chunk)
         for j in range(key_heads):
             own = query[j][part]
-            unit = first_unit[:, head_of(j)] if chunk == 0 else later_unit[part_of(chunk - 1), head_of(j)]
+            if chunk == 0:
+                unit = first_solved[j * repeat_by, :, DV + DK :]
+            else:
+                unit = later_solved[j * repeat_by, part_of(chunk - 1), DV + DK :]
             inner = lax.dot_general(
                 own, unit, (((1,), (1,)), ((), ())), preferred_element_type=F32
             )
@@ -366,13 +371,13 @@
                 scores = inner * jnp.exp(jnp.where(within, column - fade[pack : pack + 1, :], -1e30))
                 grown = jnp.exp(column)
                 if chunk == 0:
-                    updates, wide = first_solved[head, :, :DV], first_solved[head, :, DV:]
+                    updates, wide = first_solved[head, :, :DV], first_solved[head, :, DV : DV + DK]
                     fresh = jnp.concatenate([updates, -wide], 1)
                     carried = jnp.concatenate(
                         [jnp.zeros((CHUNK, DV), F32), grown * own.astype(F32)], 1
                     )
                 else:
-                    solved = later_solved[head, part_of(chunk - 1), :]
+                    solved = later_solved[head, part_of(chunk - 1), : DV + DK]
                     both = mul(jnp.concatenate([solved[:, DV:], own], 0), starts_ref[chunk - 1, head])
                     taken = both[:CHUNK]
                     fresh = jnp.concatenate(
@@ -412,7 +417,7 @@
     each = math.gcd(4, key_heads)
     steps, narrow, wide, of_heads, logits = split(each)
     later = length - CHUNK
-    solved, moves, later_unit = pl.pallas_call(
+    solved, moves = pl.pallas_call(
         later_kernel,
         grid=(steps,),
         in_specs=[
@@ -420,25 +425,24 @@
             columns_of(4, narrow), columns_of(4, wide), logits, logits,
         ],
         out_specs=[
-            of_heads(later, DV + DK), of_heads(chunks - 1, DK, DV + DK), columns_of(later, narrow),
+            of_heads(later, DV + 2 * DK), of_heads(chunks - 1, DK, DV + DK),
         ],
         out_shape=[
-            jax.ShapeDtypeStruct((value_heads, later, DV + DK), BF16),
+            jax.ShapeDtypeStruct((value_heads, later, DV + 2 * DK), BF16),
             jax.ShapeDtypeStruct((value_heads, chunks - 1, DK, DV + DK), BF16),
-            jax.ShapeDtypeStruct((later, key_heads * DK), BF16),
         ],
         scratch_shapes=[
             pltpu.VMEM((each, later + 16, DK), F32),
             pltpu.VMEM((each * repeat_by, later + 16, DV), F32),
         ],
-        compiler_params=in_vmem(60),
+        compiler_params=in_vmem(50),
         cost_estimate=pl.CostEstimate(flops=30 * work, bytes_accessed=0, transcendentals=0),
         name="later",
     )(raws[1], raws[2], taps[1], taps[2], beta, decay)
 
     narrow, wide = key_heads * DK, value_heads * DV
     whole = lambda shape, *at: pl.BlockSpec(shape, lambda step: at or (0,) * len(shape))
-    pairs, first_unit, first_solved, starts = pl.pallas_call(
+    pairs, first_solved, starts = pl.pallas_call(
         states_kernel,
         grid=(1,),
         in_specs=[
@@ -446,25 +450,24 @@
             whole((3, narrow), 0, repeat_by + 1), whole((3, wide)),
             whole(taps[1].shape), whole(taps[2].shape), whole(beta.shape), whole(decay.shape), hbm,
         ],
-        out_specs=[hbm, whole((CHUNK, narrow)), hbm, hbm],
+        out_specs=[hbm, hbm, hbm],
         out_shape=[
             jax.ShapeDtypeStruct((value_heads, DK, DV + DK), BF16),
-            jax.ShapeDtypeStruct((CHUNK, narrow), BF16),
-            jax.ShapeDtypeStruct((value_heads, CHUNK, DV + DK), BF16),
+            jax.ShapeDtypeStruct((value_heads, CHUNK, DV + 2 * DK), BF16),
             jax.ShapeDtypeStruct((chunks - 1, value_heads, DK, DV + DK), BF16),
         ],
         scratch_shapes=[
             pltpu.VMEM((key_heads, 8 + CHUNK, DK), F32),
             pltpu.VMEM((value_heads, 8 + CHUNK, DV), F32),
             pltpu.VMEM(moves.shape, BF16),
-            pltpu.VMEM((value_heads, CHUNK, DV + DK), BF16),
+            pltpu.VMEM((value_heads, CHUNK, DV + 2 * DK), BF16),
             pltpu.VMEM((chunks - 1, value_heads, DK, DV + DK), BF16),
             pltpu.VMEM((value_heads, DK, DV + DK), BF16),
             pltpu.SemaphoreType.DMA,
             pltpu.SemaphoreType.DMA((chunks,)),
             pltpu.SemaphoreType.DMA((value_heads // min(HEADS_AT_ONCE, value_heads),)),
         ],
-        compiler_params=in_vmem(54),
+        compiler_params=in_vmem(52),
         cost_estimate=pl.CostEstimate(flops=20 * work, bytes_accessed=0, transcendentals=0),
         name="states",
     )(raws[1], raws[2], before, before, taps[1], taps[2], beta, decay, moves)
@@ -478,8 +481,7 @@
             grid=(steps,),
             in_specs=[
                 columns_of(length, narrow), columns_of(3, narrow, repeat_by * steps), columns_of(4, narrow),
-                columns_of(CHUNK, narrow), columns_of(later, narrow), logits,
-                of_heads(CHUNK, DV + DK), of_heads(later, DV + DK),
+                logits, of_heads(CHUNK, DV + 2 * DK), of_heads(later, DV + 2 * DK),
                 pl.BlockSpec((chunks - 1, heads, DK, DV + DK), lambda step: (0, step, 0, 0)),
                 columns_of(length, wide), whole(gain.shape),
             ],
@@ -493,8 +495,7 @@
             cost_estimate=pl.CostEstimate(flops=12 * work, bytes_accessed=0, transcendentals=0),
             name="local",
         )(
-            raws[0], before, taps[0], first_unit, later_unit, decay,
-            first_solved, solved, starts, gate_raw, gain,
+            raws[0], before, taps[0], decay, first_solved, solved, starts, gate_raw, gain,
         )
 
     return pairs, local
@@ -602,7 +603,7 @@
             core = parts_ref[head, :, :DV].astype(F32) + mul(
                 parts_ref[head, :, DV:], starts_ref[head]
             )
-            scale = lax.rsqrt(row_sums(core * core, 1.0 / DV) + EPSILON)
+            scale = lax.rsqrt(jnp.mean(core * core, -1, keepdims=True) + EPSILON)
             normed.append((core * scale * gated_ref[:, head_of(head)].astype(F32)).astype(BF16))
         return jnp.concatenate(normed, 1)
 

time: 75.5 us -> 73.2 us (0.970)
  Pallas kernels: 40.8 us -> 39 us
    pallas_call x1, Pallas kernels: 9.4 us -> 8.4 us  [local_steps(): pl.pallas_call(later_kernel, grid=(steps,), in_specs=[columns_of(length,...]
  transfers between devices with their start and end apart: 5 -> 5, of which waited for: 4 -> 4; matrix products, arithmetic and copies ran while one was open for 0% -> 0% of each run, Pallas kernels for 29% -> 28%
where the time goes in v9:
time: 73.2 us; the launch traced here: 72.8 us
  Pallas kernels  39 us (53%)
  starting transfers between devices  17.3 us (24%)
  waiting for transfers between devices  15.1 us (21%)
  other arithmetic  1.15 us (2%)
    pallas_call x1, Pallas kernels, local(): pl.pallas_call(local_kernel, grid=(steps,), in_specs=[columns_of(length,...  12.2 us
    all_to_all x1, waiting for transfers between devices, starts_of(): lax.all_to_all(starts.reshape(heads, DK, DV), axis, 0, 0, axis_index_grou...  8.81 us
    ppermute x2, starting transfers between devices, shifted(): return lax.ppermute(value, axis, [(i, i + by) for i in range(count - by)])  8.56 us
    pallas_call x1, Pallas kernels, local_steps(): pl.pallas_call(later_kernel, grid=(steps,), in_specs=[columns_of(length,...  8.4 us
    pallas_call x1, Pallas kernels, projected(): pl.pallas_call(project_kernel if halves else whole_kernel, in_specs=[pl.B...  7.58 us
    pallas_call x1, Pallas kernels, local_steps(): pl.pallas_call(states_kernel, grid=(1,), in_specs=[whole((CHUNK, narrow))...  6.93 us
    all_to_all x1, starting transfers between devices, starts_of(): lax.all_to_all(pairs, axis, 0, 0, axis_index_groups=groups, tiled=True)  4.75 us
    all_to_all x1, starting transfers between devices, starts_of(): lax.all_to_all(starts.reshape(heads, DK, DV), axis, 0, 0, axis_index_grou...  3.92 us
  transfers between devices with their start and end apart: 5, of which 4 were waited for; matrix products, arithmetic and copies ran while one was open for 0% of the time, Pallas kernels for 28%

profile of v9, /device:TPU:0, one launch (start us, length us, event | category | flops | bytes accessed | tf_op | source)
XLA Modules:
  0.0 72.8 jit_solution(10499113223326069605)
XLA Ops:
  0.0 0.0 copy-start.2
  0.0 0.0 copy-start
  0.0 0.0 copy-start.4
  0.0 0.0 copy-start.6
  0.0 0.0 copy-start.7
  0.0 0.0 copy-start.5
  0.0 1.7 %tails.1 = bf16[3,4096]{1,0:T(4,128)(2,1)} custom-call(bf16[384,2048]{1,0:T(8,128)(2,1)} %value_ref.3, bf16[384,1024]{1,0:T(8,128)(2,1)} %query_ref.1, bf16[384,1024]{1,0:T(8,128)(2,1)} %key_ref.3), custom_call_target="tpu_custom_call" | custom-call | tf_op jit(solution)/shard_map/tails/pallas_call | solution.py:700
  1.7 4.9 %collective-permute-start = (bf16[3,4096]{1,0:T(4,128)(2,1)}, bf16[3,4096]{1,0:T(4,128)(2,1)S(1)}, u32[]{:S(2)}, u32[]{:S(2)}) collective-permute-start(bf16[3,4096]{1,0:T(4,128)(2,1)} %tails.1), channel_id=1, source_target_pairs={{0,2},{2,4},{4,6},{6,8},{8,10},{10,12},{12,14},{14,16},{16,18},{18... | collective-permute-start | bytes 73736 | tf_op jit(solution)/shard_map/ppermute | solution.py:536
  6.6 0.0 copy-done.2
  6.6 0.0 copy-done
  6.6 0.0 copy-done.4
  6.6 0.0 copy-done.6
  6.6 0.0 copy-done.7
  6.6 0.0 copy-done.5
  6.6 8.4 %later.1 = (bf16[16,256,384]{2,1,0:T(8,128)(2,1)}, bf16[16,2,128,256]{3,2,1,0:T(8,128)(2,1)}) custom-call(bf16[384,1024]{1,0:T(8,128)(2,1)S(1)} %copy-done.2, bf16[384,2048]{1,0:T(8,128)(2,1)S(1)} %copy-done, f32[4,1024]{1,0:T(4,128)S(1)} %copy-done.7, f32[4,2048]{1,0:T(4,128)S(1)} %copy-done.5, f32[16,384]{1,0:T(8,128)S(1)} %bitcast.10, f32[16,384]{1,0:T(8,128)S(1)} %bitcast.8), custom_call_target="tpu_custom_call" | custom-call | flops 3019898880 | tf_op jit(solution)/shard_map/later/pallas_call | solution.py:420
  15.0 0.0 collective-permute-done.key_before.value_before.query_before
  15.0 0.0 copy-start.3
  15.0 6.9 %states.1 = (bf16[16,128,256]{2,1,0:T(8,128)(2,1)}, bf16[16,128,384]{2,1,0:T(8,128)(2,1)}, bf16[2,16,128,256]{3,2,1,0:T(8,128)(2,1)}) custom-call(bf16[384,1024]{1,0:T(8,128)(2,1)S(1)} %copy-done.2, bf16[384,2048]{1,0:T(8,128)(2,1)} %value_ref.3, bf16[3,4096]{1,0:T(4,128)(2,1)S(1)} %collective-permute-done.key_before.value_before.query_before, ...), custom_call_target="tpu_custom_call" | custom-call | flops 2013265920 | tf_op jit(solution)/shard_map/states/pallas_call | solution.py:445
  22.0 0.0 copy-done.3
  22.0 4.8 %all-to-all-start = ((bf16[16,128,256]{2,1,0:T(8,128)(2,1)}), bf16[16,128,256]{2,1,0:T(8,128)(2,1)S(1)}, u32[]{:S(2)}, u32[]{:S(2)}) async-start(bf16[16,128,256]{2,1,0:T(8,128)(2,1)} %get-tuple-element.20), calls=%async_computation | async-start | bytes 2097152 | tf_op jit(solution)/shard_map/all_to_all | solution.py:559
  26.7 12.2 %local.1 = (bf16[16,384,256]{2,1,0:T(8,128)(2,1)}, bf16[384,2048]{1,0:T(8,128)(2,1)}) custom-call(bf16[384,1024]{1,0:T(8,128)(2,1)} %query_ref.1, bf16[3,4096]{1,0:T(4,128)(2,1)} %copy-done.3, f32[4,1024]{1,0:T(4,128)} %query_taps.1, f32[16,384]{1,0:T(8,128)} %bitcast.7, bf16[16,128,384]{2,1,0:T(8,128)(2,1)} %get-tuple-element.21.first_solved, ...), custom_call_target="tpu_custom_call" | custom-call | flops 1207959552 | tf_op jit(solution)/shard_map/local/pallas_call | solution.py:479
  39.0 2.2 %all-to-all-done = bf16[16,128,256]{2,1,0:T(8,128)(2,1)S(1)} async-done(((bf16[16,128,256]{2,1,0:T(8,128)(2,1)}), bf16[16,128,256]{2,1,0:T(8,128)(2,1)S(1)}, u32[]{:S(2)}, u32[]{:S(2)}) %all-to-all-start) | async-done | bytes 1048608 | tf_op jit(solution)/shard_map/all_to_all | solution.py:559
  41.1 1.1 %prefix.1 = (bf16[8,2,128,256]{3,2,1,0:T(8,128)(2,1)S(1)}, bf16[2,128,128]{2,1,0:T(8,128)(2,1)S(1)}) custom-call(bf16[8,2,128,256]{3,2,1,0:T(8,128)(2,1)S(1)} %bitcast.6), custom_call_target="tpu_custom_call" | custom-call | tf_op jit(solution)/shard_map/prefix/pallas_call | solution.py:561
  42.3 0.0 copy-start.1
  42.3 3.7 %collective-permute-start.1 = (bf16[2,128,128]{2,1,0:T(8,128)(2,1)S(1)}, bf16[2,128,128]{2,1,0:T(8,128)(2,1)S(1)}, u32[]{:S(2)}, u32[]{:S(2)}) collective-permute-start(bf16[2,128,128]{2,1,0:T(8,128)(2,1)S(1)} %get-tuple-element.28), channel_id=1, source_target_pairs={{0,16},{2,18},{4,20},{6,22},{8,24},{10,26},{12,28},{14,30},{1,17},... | collective-permute-start | bytes 196616 | tf_op jit(solution)/shard_map/ppermute | solution.py:536
  46.0 1.9 %collective-permute-done.1.start_ref = bf16[2,128,128]{2,1,0:T(8,128)(2,1)S(1)} collective-permute-done((bf16[2,128,128]{2,1,0:T(8,128)(2,1)S(1)}, bf16[2,128,128]{2,1,0:T(8,128)(2,1)S(1)}, u32[]{:S(2)}, u32[]{:S(2)}) %collective-permute-start.1) | collective-permute-done | bytes 65568 | tf_op jit(solution)/shard_map/ppermute | solution.py:536
  47.9 1.1 %apply.1 = bf16[8,2,128,128]{3,2,1,0:T(8,128)(2,1)} custom-call(bf16[8,2,128,256]{3,2,1,0:T(8,128)(2,1)S(1)} %get-tuple-element.27.prefix_ref, bf16[2,128,128]{2,1,0:T(8,128)(2,1)S(1)} %collective-permute-done.1.start_ref), custom_call_target="tpu_custom_call" | custom-call | tf_op jit(solution)/shard_map/apply/pallas_call | solution.py:570
  49.0 3.9 %all-to-all-start.1 = ((bf16[16,128,128]{2,1,0:T(8,128)(2,1)}), bf16[16,128,128]{2,1,0:T(8,128)(2,1)S(1)}, u32[]{:S(2)}, u32[]{:S(2)}) async-start(bf16[16,128,128]{2,1,0:T(8,128)(2,1)} %bitcast.5), calls=%async_computation.1 | async-start | bytes 1048576 | tf_op jit(solution)/shard_map/all_to_all | solution.py:576
  52.9 8.8 %all-to-all-done.1.starts_ref = bf16[16,128,128]{2,1,0:T(8,128)(2,1)S(1)} async-done(((bf16[16,128,128]{2,1,0:T(8,128)(2,1)}), bf16[16,128,128]{2,1,0:T(8,128)(2,1)S(1)}, u32[]{:S(2)}, u32[]{:S(2)}) %all-to-all-start.1) | async-done | bytes 524320 | tf_op jit(solution)/shard_map/all_to_all | solution.py:576
  61.7 0.0 copy-done.1
  61.7 7.6 %project.1 = (bf16[192,2048]{1,0:T(8,128)(2,1)S(1)}, bf16[192,2048]{1,0:T(8,128)(2,1)S(1)}) custom-call(s32[1]{0:T(128)} %bitcast.place_ref, bf16[16,128,128]{2,1,0:T(8,128)(2,1)S(1)} %all-to-all-done.1.starts_ref, bf16[384,2048]{1,0:T(8,128)(2,1)S(1)} %copy-done.1, bf16[16,384,256]{2,1,0:T(8,128)(2,1)} %get-tuple-element.30.parts_hbm, ...), custom_call_target="tpu_custom_call" | custom-call | tf_op jit(solution)/shard_map/project/pallas_call | solution.py:659
  69.3 0.1 collective-permute-start.2
  69.3 2.3 %collective-permute-done.2 = bf16[192,2048]{1,0:T(8,128)(2,1)S(1)} collective-permute-done((bf16[192,2048]{1,0:T(8,128)(2,1)S(1)}, bf16[192,2048]{1,0:T(8,128)(2,1)S(1)}, u32[]{:S(2)}, u32[]{:S(2)}) %collective-permute-start.2) | collective-permute-done | bytes 786464 | tf_op jit(solution)/shard_map/ppermute | solution.py:677
  71.6 1.2 %add_convert_fusion = bf16[192,2048]{1,0:T(8,128)(2,1)} fusion(bf16[192,2048]{1,0:T(8,128)(2,1)S(1)} %collective-permute-done.2, bf16[192,2048]{1,0:T(8,128)(2,1)S(1)} %get-tuple-element.31), kind=kLoop, calls=%fused_computation | loop fusion | flops 1572864 | bytes 2359296 | tf_op jit(solution)/shard_map/convert_element_type | solution.py:678
Async XLA Ops:
  0.0 6.6 %copy-start.2 = (bf16[384,1024]{1,0:T(8,128)(2,1)S(1)}, bf16[384,1024]{1,0:T(8,128)(2,1)}, u32[]{:S(2)}) copy-start(bf16[384,1024]{1,0:T(8,128)(2,1)} %key_ref.3) | copy-start | bytes 2359300
  0.0 6.6 %copy-start = (bf16[384,2048]{1,0:T(8,128)(2,1)S(1)}, bf16[384,2048]{1,0:T(8,128)(2,1)}, u32[]{:S(2)}) copy-start(bf16[384,2048]{1,0:T(8,128)(2,1)} %value_ref.3) | copy-start | bytes 4718596
  0.0 6.6 %copy-start.4 = (f32[384,16]{0,1:T(8,128)S(1)}, f32[384,16]{0,1:T(8,128)}, u32[]{:S(2)}) copy-start(f32[384,16]{0,1:T(8,128)} %param.19) | copy-start | bytes 73732
  0.0 6.6 %copy-start.6 = (f32[384,16]{0,1:T(8,128)S(1)}, f32[384,16]{0,1:T(8,128)}, u32[]{:S(2)}) copy-start(f32[384,16]{0,1:T(8,128)} %param.18) | copy-start | bytes 73732
  0.0 6.6 %copy-start.7 = (f32[4,1024]{1,0:T(4,128)S(1)}, f32[4,1024]{1,0:T(4,128)}, u32[]{:S(2)}) copy-start(f32[4,1024]{1,0:T(4,128)} %key_taps.3) | copy-start | bytes 49156
  0.0 6.6 %copy-start.5 = (f32[4,2048]{1,0:T(4,128)S(1)}, f32[4,2048]{1,0:T(4,128)}, u32[]{:S(2)}) copy-start(f32[4,2048]{1,0:T(4,128)} %value_taps.3) | copy-start | bytes 98308
  1.7 13.3 %collective-permute-start = (bf16[3,4096]{1,0:T(4,128)(2,1)}, bf16[3,4096]{1,0:T(4,128)(2,1)S(1)}, u32[]{:S(2)}, u32[]{:S(2)}) collective-permute-start(bf16[3,4096]{1,0:T(4,128)(2,1)} %tails.1), channel_id=1, source_target_pairs={{0,2},{2,4},{4,6},{6,8},{8,10},{10,12},{12,14},{14,16},{16,18},{18... | collective-permute-start | bytes 73736 | tf_op jit(solution)/shard_map/ppermute | solution.py:536
  15.0 6.9 %copy-start.3 = (bf16[3,4096]{1,0:T(4,128)(2,1)}, bf16[3,4096]{1,0:T(4,128)(2,1)S(1)}, u32[]{:S(2)}) copy-start(bf16[3,4096]{1,0:T(4,128)(2,1)S(1)} %collective-permute-done.key_before.value_before.query_before) | copy-start | bytes 73732
  22.0 19.2 %all-to-all-start = ((bf16[16,128,256]{2,1,0:T(8,128)(2,1)}), bf16[16,128,256]{2,1,0:T(8,128)(2,1)S(1)}, u32[]{:S(2)}, u32[]{:S(2)}) async-start(bf16[16,128,256]{2,1,0:T(8,128)(2,1)} %get-tuple-element.20), calls=%async_computation | async-start | bytes 2097152 | tf_op jit(solution)/shard_map/all_to_all | solution.py:559
  42.3 19.4 %copy-start.1 = (bf16[384,2048]{1,0:T(8,128)(2,1)S(1)}, bf16[384,2048]{1,0:T(8,128)(2,1)}, u32[]{:S(2)}) copy-start(bf16[384,2048]{1,0:T(8,128)(2,1)} %get-tuple-element.29.gated_ref) | copy-start | bytes 4718596
  42.3 5.6 %collective-permute-start.1 = (bf16[2,128,128]{2,1,0:T(8,128)(2,1)S(1)}, bf16[2,128,128]{2,1,0:T(8,128)(2,1)S(1)}, u32[]{:S(2)}, u32[]{:S(2)}) collective-permute-start(bf16[2,128,128]{2,1,0:T(8,128)(2,1)S(1)} %get-tuple-element.28), channel_id=1, source_target_pairs={{0,16},{2,18},{4,20},{6,22},{8,24},{10,26},{12,28},{14,30},{1,17},... | collective-permute-start | bytes 196616 | tf_op jit(solution)/shard_map/ppermute | solution.py:536
  49.0 12.7 %all-to-all-start.1 = ((bf16[16,128,128]{2,1,0:T(8,128)(2,1)}), bf16[16,128,128]{2,1,0:T(8,128)(2,1)S(1)}, u32[]{:S(2)}, u32[]{:S(2)}) async-start(bf16[16,128,128]{2,1,0:T(8,128)(2,1)} %bitcast.5), calls=%async_computation.1 | async-start | bytes 1048576 | tf_op jit(solution)/shard_map/all_to_all | solution.py:576
  69.3 2.4 %collective-permute-start.2 = (bf16[192,2048]{1,0:T(8,128)(2,1)S(1)}, bf16[192,2048]{1,0:T(8,128)(2,1)S(1)}, u32[]{:S(2)}, u32[]{:S(2)}) collective-permute-start(bf16[192,2048]{1,0:T(8,128)(2,1)S(1)} %get-tuple-element.32), channel_id=1, source_target_pairs={{0,1},{1,0},{2,3},{3,2},{4,5},{5,4},{6,7},{7,6},{8,9},{9,8},{10,11... | collective-permute-start | bytes 2359304 | tf_op jit(solution)/shard_map/ppermute | solution.py:677

commit v10 on v9

--- a/solution.py
+++ b/solution.py
@@ -207,16 +207,18 @@
     key_ref, value_ref, key_taps, value_taps, beta_ref, decay_ref,
     solved_ref, moves_ref, key_padded, value_padded,
 ):
-    length, width = key_ref.shape
+    length = key_ref.shape[0]
     chunks = range(1, length // CHUNK)
-    key_heads = width // DK
-    heads = value_ref.shape[1] // DV
+    key_heads, heads = key_padded.shape[0], value_padded.shape[0]
+    step = pl.program_id(0)
     repeat_by = heads // key_heads
     packs = [(chunk, head) for chunk in chunks for head in range(heads)]
     skip = CHUNK - 16
     count = length - CHUNK
-    widen(key_padded, 0, count + 16, key_ref[skip:, :])
-    widen(value_padded, 0, count + 16, value_ref[skip:, :])
+    for padded, raw_ref in ((key_padded, key_ref), (value_padded, value_ref)):
+        for head in range(padded.shape[0]):
+            first = pl.multiple_of((step * padded.shape[0] + head) * DK, DK)
+            padded[head] = raw_ref[skip:, pl.ds(first, DK)].astype(F32)
     key, turned = {}, {}
     for j in range(key_heads):
         unit = unit_rows(conv_silu(key_padded, 13, count, key_taps, j))
@@ -336,8 +338,9 @@
 def local_kernel(
     query_ref, query_before, query_taps, decay_ref,
     first_solved, later_solved, starts_ref, gate_ref, gain_ref,
-    parts_ref, gated_ref, padded,
+    ahead_ref, parts_ref, padded,
 ):
+    step = pl.program_id(0)
     length, width = query_ref.shape
     chunks = length // CHUNK
     key_heads = width // DK
@@ -353,7 +356,9 @@
     query = [conv_silu(padded, 5, length, query_taps, j).astype(BF16) for j in range(key_heads)]
     for head in range(heads):
         gate = gate_ref[:, head_of(head)].astype(F32)
-        gated_ref[:, head_of(head)] = (gate * sigmoid(gate) * gain_ref[...]).astype(BF16)
+        parts_ref[heads + head // 2, :, head_of(head % 2)] = (
+            gate * sigmoid(gate) * gain_ref[...]
+        ).astype(BF16)
     for chunk in range(chunks):
         part = part_of(chunk)
         for j in range(key_heads):
@@ -388,6 +393,10 @@
                     )
                 parts_ref[head, part, :] = (carried + mul(scores, fresh)).astype(BF16)
 
+    @pl.when(step == 0)
+    def _():
+        ahead_ref[...] = parts_ref[...]
+
 
 def columns_of(rows, width, first=0):
     return pl.BlockSpec((rows, width), lambda step: (0, step + first))
@@ -406,6 +415,7 @@
     beta, decay = beta_logit.T, decay_logit.T
     work = CHUNK * length * DV * value_heads
     hbm = pl.BlockSpec(memory_space=pltpu.HBM)
+    vmem = pl.BlockSpec(memory_space=pltpu.VMEM)
 
     def split(each):
         heads = each * repeat_by
@@ -421,8 +431,7 @@
         later_kernel,
         grid=(steps,),
         in_specs=[
-            columns_of(length, narrow), columns_of(length, wide),
-            columns_of(4, narrow), columns_of(4, wide), logits, logits,
+            vmem, vmem, columns_of(4, narrow), columns_of(4, wide), logits, logits,
         ],
         out_specs=[
             of_heads(later, DV + 2 * DK), of_heads(chunks - 1, DK, DV + DK),
@@ -476,6 +485,7 @@
     def local():
         steps, narrow, wide, of_heads, logits = split(math.gcd(2, key_heads))
         heads = wide // DV
+        ahead = (heads + heads // 2, length, DV + DK)
         return pl.pallas_call(
             local_kernel,
             grid=(steps,),
@@ -485,10 +495,13 @@
                 pl.BlockSpec((chunks - 1, heads, DK, DV + DK), lambda step: (0, step, 0, 0)),
                 columns_of(length, wide), whole(gain.shape),
             ],
-            out_specs=[of_heads(length, DV + DK), columns_of(length, wide)],
+            out_specs=[
+                whole(ahead),
+                pl.BlockSpec(ahead, lambda step: (jnp.maximum(step - 1, 0), 0, 0)),
+            ],
             out_shape=[
-                jax.ShapeDtypeStruct((value_heads, length, DV + DK), BF16),
-                jax.ShapeDtypeStruct(gate_raw.shape, BF16),
+                jax.ShapeDtypeStruct(ahead, BF16),
+                jax.ShapeDtypeStruct((max(steps - 1, 1) * ahead[0],) + ahead[1:], BF16),
             ],
             scratch_shapes=[pltpu.VMEM((narrow // DK, 8 + length, DK), F32)],
             compiler_params=in_vmem(60),
@@ -580,17 +593,18 @@
 
 
 def project_kernel(
-    place_ref, starts_ref, gated_ref, parts_hbm, weight_hbm, away_ref, own_ref,
+    place_ref, starts_ref, ahead_ref, parts_hbm, weight_hbm, away_ref, own_ref,
     parts_ref, weight_ref, total, parts_sem, weight_sem,
 ):
-    heads, length = parts_ref.shape[:2]
+    heads = starts_ref.shape[0]
+    entries, length = ahead_ref.shape[:2]
+    each = entries * 2 // 3
     width = weight_ref.shape[1]
-    each = min(HEADS_AT_ONCE, heads)
     block = min(512, width)
     groups = heads // each
 
     def parts(g):
-        here = pl.ds(g * each, each)
+        here = pl.ds((g - 1) * entries, entries)
         return pltpu.make_async_copy(parts_hbm.at[here], parts_ref.at[here], parts_sem.at[g])
 
     def weights(g):
@@ -600,16 +614,14 @@
     def normed_group(g):
         normed = []
         for head in range(g * each, (g + 1) * each):
-            core = parts_ref[head, :, :DV].astype(F32) + mul(
-                parts_ref[head, :, DV:], starts_ref[head]
-            )
+            held, at = (ahead_ref, head) if g == 0 else (parts_ref, (g - 1) * entries + head - g * each)
+            core = held[at, :, :DV].astype(F32) + mul(held[at, :, DV:], starts_ref[head])
             scale = lax.rsqrt(jnp.mean(core * core, -1, keepdims=True) + EPSILON)
-            normed.append((core * scale * gated_ref[:, head_of(head)].astype(F32)).astype(BF16))
+            gated = held[at - head % each + each + head % each // 2, :, head_of(head % 2)]
+            normed.append((core * scale * gated.astype(F32)).astype(BF16))
         return jnp.concatenate(normed, 1)
 
-    parts(0).start()
     weights(0).start()
-    parts(0).wait()
     if groups > 1:
         parts(1).start()
         weights(1).start()
@@ -643,17 +655,18 @@
                 away_ref[:, at : at + block] = jnp.where(first, high, low).astype(BF16)
 
 
-def whole_kernel(place_ref, starts_ref, gated_ref, parts_hbm, weight_hbm, out_ref, *scratch):
-    project_kernel(place_ref, starts_ref, gated_ref, parts_hbm, weight_hbm, out_ref, None, *scratch)
-
-
-def projected(parts, starts, gated, out_weight, axis):
-    heads, length = parts.shape[:2]
+def whole_kernel(place_ref, starts_ref, ahead_ref, parts_hbm, weight_hbm, out_ref, *scratch):
+    project_kernel(place_ref, starts_ref, ahead_ref, parts_hbm, weight_hbm, out_ref, None, *scratch)
+
+
+def projected(ahead, parts, starts, out_weight, axis):
+    length = parts.shape[1]
     width = out_weight.shape[1]
     halves = lax.axis_size(axis) == 2
     vmem = pl.BlockSpec(memory_space=pltpu.VMEM)
     hbm = pl.BlockSpec(memory_space=pltpu.HBM)
-    groups = heads // min(HEADS_AT_ONCE, heads)
+    heads = starts.shape[0]
+    groups = heads // (ahead.shape[0] * 2 // 3)
     here = lax.axis_index(axis).astype(jnp.int32).reshape(1)
     out = jax.ShapeDtypeStruct((length // 2 if halves else length, width), BF16)
     partial = pl.pallas_call(
@@ -670,7 +683,7 @@
         ],
         compiler_params=in_vmem(50),
         name="project",
-    )(here, starts, gated, parts, out_weight)
+    )(here, starts, ahead, parts, out_weight)
     if not halves:
         return lax.psum_scatter(partial, axis, scatter_dimension=0, tiled=True)
     away, own = partial
@@ -717,8 +730,8 @@
     pairs, local = local_steps(
         raws, before, (query_taps, key_taps, value_taps), beta_logit, decay_logit, gate_raw, norm_gain
     )
-    starts, (parts, gated) = starts_of(pairs, "seq", local)
-    return projected(parts, starts, gated, out_weight, "head")
+    starts, (ahead, parts) = starts_of(pairs, "seq", local)
+    return projected(ahead, parts, starts, out_weight, "head")
 
 
 def solution(mesh):

time: 73.2 us -> 72.1 us (0.985)
  waiting for transfers between devices: 15.1 us -> 13.1 us
    all_to_all x1, waiting for transfers between devices: 8.81 us -> 7.67 us  [starts_of(): lax.all_to_all(starts.reshape(heads, DK, DV), axis, 0, 0, axis_index_grou...]
    all_to_all x1, waiting for transfers between devices: 2.15 us -> 1.27 us  [starts_of(): lax.all_to_all(pairs, axis, 0, 0, axis_index_groups=groups, tiled=True)]
    pallas_call x1, Pallas kernels: 12.2 us -> 13.1 us  [local(): pl.pallas_call(local_kernel, grid=(steps,), in_specs=[columns_of(length,...]
  transfers between devices with their start and end apart: 5 -> 5, of which waited for: 4 -> 4; matrix products, arithmetic and copies ran while one was open for 0% -> 0% of each run, Pallas kernels for 28% -> 30%
where the time goes in v10:
time: 72.1 us; the launch traced here: 71.7 us
  Pallas kernels  39.5 us (55%)
  starting transfers between devices  17.8 us (25%)
  waiting for transfers between devices  13.1 us (18%)
  other arithmetic  1.15 us (2%)
    pallas_call x1, Pallas kernels, local(): pl.pallas_call(local_kernel, grid=(steps,), in_specs=[columns_of(length,...  13.1 us
    ppermute x2, starting transfers between devices, shifted(): return lax.ppermute(value, axis, [(i, i + by) for i in range(count - by)])  8.56 us
    pallas_call x1, Pallas kernels, local_steps(): pl.pallas_call(later_kernel, grid=(steps,), in_specs=[vmem, vmem, columns...  8.26 us
    all_to_all x1, waiting for transfers between devices, starts_of(): lax.all_to_all(starts.reshape(heads, DK, DV), axis, 0, 0, axis_index_grou...  7.67 us
    pallas_call x1, Pallas kernels, projected(): pl.pallas_call(project_kernel if halves else whole_kernel, in_specs=[pl.B...  7.26 us
    pallas_call x1, Pallas kernels, local_steps(): pl.pallas_call(states_kernel, grid=(1,), in_specs=[whole((CHUNK, narrow))...  6.94 us
    all_to_all x1, starting transfers between devices, starts_of(): lax.all_to_all(pairs, axis, 0, 0, axis_index_groups=groups, tiled=True)  4.75 us
    all_to_all x1, starting transfers between devices, starts_of(): lax.all_to_all(starts.reshape(heads, DK, DV), axis, 0, 0, axis_index_grou...  4.41 us
  transfers between devices with their start and end apart: 5, of which 4 were waited for; matrix products, arithmetic and copies ran while one was open for 0% of the time, Pallas kernels for 30%

profile of v10, /device:TPU:0, one launch (start us, length us, event | category | flops | bytes accessed | tf_op | source)
XLA Modules:
  0.0 71.7 jit_solution(2508900955998105268)
XLA Ops:
  0.0 0.0 copy-start.2
  0.0 0.0 copy-start
  0.0 0.0 copy-start.4
  0.0 0.0 copy-start.6
  0.0 0.0 copy-start.7
  0.0 0.0 copy-start.5
  0.0 1.7 %tails.1 = bf16[3,4096]{1,0:T(4,128)(2,1)} custom-call(bf16[384,2048]{1,0:T(8,128)(2,1)} %value_ref.3, bf16[384,1024]{1,0:T(8,128)(2,1)} %query_ref.1, bf16[384,1024]{1,0:T(8,128)(2,1)} %key_ref.3), custom_call_target="tpu_custom_call" | custom-call | tf_op jit(solution)/shard_map/tails/pallas_call | solution.py:713
  1.7 4.9 %collective-permute-start = (bf16[3,4096]{1,0:T(4,128)(2,1)}, bf16[3,4096]{1,0:T(4,128)(2,1)S(1)}, u32[]{:S(2)}, u32[]{:S(2)}) collective-permute-start(bf16[3,4096]{1,0:T(4,128)(2,1)} %tails.1), channel_id=1, source_target_pairs={{0,2},{2,4},{4,6},{6,8},{8,10},{10,12},{12,14},{14,16},{16,18},{18... | collective-permute-start | bytes 73736 | tf_op jit(solution)/shard_map/ppermute | solution.py:549
  6.6 0.0 copy-done.2
  6.6 0.0 copy-done
  6.6 0.0 copy-done.4
  6.6 0.0 copy-done.6
  6.6 0.0 copy-done.7
  6.6 0.0 copy-done.5
  6.6 8.3 %later.1 = (bf16[16,256,384]{2,1,0:T(8,128)(2,1)}, bf16[16,2,128,256]{3,2,1,0:T(8,128)(2,1)}) custom-call(bf16[384,1024]{1,0:T(8,128)(2,1)S(1)} %copy-done.2, bf16[384,2048]{1,0:T(8,128)(2,1)S(1)} %copy-done, f32[4,1024]{1,0:T(4,128)S(1)} %copy-done.7, f32[4,2048]{1,0:T(4,128)S(1)} %copy-done.5, f32[16,384]{1,0:T(8,128)S(1)} %bitcast.10, f32[16,384]{1,0:T(8,128)S(1)} %bitcast.8), custom_call_target="tpu_custom_call" | custom-call | flops 3019898880 | tf_op jit(solution)/shard_map/later/pallas_call | solution.py:430
  14.9 0.0 collective-permute-done.key_before.value_before.query_before
  14.9 0.0 copy-start.3
  14.9 6.9 %states.1 = (bf16[16,128,256]{2,1,0:T(8,128)(2,1)}, bf16[16,128,384]{2,1,0:T(8,128)(2,1)}, bf16[2,16,128,256]{3,2,1,0:T(8,128)(2,1)}) custom-call(bf16[384,1024]{1,0:T(8,128)(2,1)S(1)} %copy-done.2, bf16[384,2048]{1,0:T(8,128)(2,1)} %value_ref.3, bf16[3,4096]{1,0:T(4,128)(2,1)S(1)} %collective-permute-done.key_before.value_before.query_before, ...), custom_call_target="tpu_custom_call" | custom-call | flops 2013265920 | tf_op jit(solution)/shard_map/states/pallas_call | solution.py:454
  21.8 0.0 copy-done.3
  21.8 4.7 %all-to-all-start = ((bf16[16,128,256]{2,1,0:T(8,128)(2,1)}), bf16[16,128,256]{2,1,0:T(8,128)(2,1)S(1)}, u32[]{:S(2)}, u32[]{:S(2)}) async-start(bf16[16,128,256]{2,1,0:T(8,128)(2,1)} %get-tuple-element.20), calls=%async_computation | async-start | bytes 2097152 | tf_op jit(solution)/shard_map/all_to_all | solution.py:572
  26.6 13.1 %local.1 = (bf16[6,384,256]{2,1,0:T(8,128)(2,1)}, bf16[18,384,256]{2,1,0:T(8,128)(2,1)}) custom-call(bf16[384,1024]{1,0:T(8,128)(2,1)} %query_ref.1, bf16[3,4096]{1,0:T(4,128)(2,1)} %copy-done.3, f32[4,1024]{1,0:T(4,128)} %query_taps.1, f32[16,384]{1,0:T(8,128)} %bitcast.7, bf16[16,128,384]{2,1,0:T(8,128)(2,1)} %get-tuple-element.21.first_solved, ...), custom_call_target="tpu_custom_call" | custom-call | flops 1207959552 | tf_op jit(solution)/shard_map/local/pallas_call | solution.py:489
  39.7 1.3 %all-to-all-done = bf16[16,128,256]{2,1,0:T(8,128)(2,1)S(1)} async-done(((bf16[16,128,256]{2,1,0:T(8,128)(2,1)}), bf16[16,128,256]{2,1,0:T(8,128)(2,1)S(1)}, u32[]{:S(2)}, u32[]{:S(2)}) %all-to-all-start) | async-done | bytes 1048608 | tf_op jit(solution)/shard_map/all_to_all | solution.py:572
  41.0 1.1 %prefix.1 = (bf16[8,2,128,256]{3,2,1,0:T(8,128)(2,1)S(1)}, bf16[2,128,128]{2,1,0:T(8,128)(2,1)S(1)}) custom-call(bf16[8,2,128,256]{3,2,1,0:T(8,128)(2,1)S(1)} %bitcast.6), custom_call_target="tpu_custom_call" | custom-call | tf_op jit(solution)/shard_map/prefix/pallas_call | solution.py:574
  42.1 0.0 copy-start.1
  42.1 3.7 %collective-permute-start.1 = (bf16[2,128,128]{2,1,0:T(8,128)(2,1)S(1)}, bf16[2,128,128]{2,1,0:T(8,128)(2,1)S(1)}, u32[]{:S(2)}, u32[]{:S(2)}) collective-permute-start(bf16[2,128,128]{2,1,0:T(8,128)(2,1)S(1)} %get-tuple-element.28), channel_id=1, source_target_pairs={{0,16},{2,18},{4,20},{6,22},{8,24},{10,26},{12,28},{14,30},{1,17},... | collective-permute-start | bytes 196616 | tf_op jit(solution)/shard_map/ppermute | solution.py:549
  45.9 1.9 %collective-permute-done.1.start_ref = bf16[2,128,128]{2,1,0:T(8,128)(2,1)S(1)} collective-permute-done((bf16[2,128,128]{2,1,0:T(8,128)(2,1)S(1)}, bf16[2,128,128]{2,1,0:T(8,128)(2,1)S(1)}, u32[]{:S(2)}, u32[]{:S(2)}) %collective-permute-start.1) | collective-permute-done | bytes 65568 | tf_op jit(solution)/shard_map/ppermute | solution.py:549
  47.7 1.1 %apply.1 = bf16[8,2,128,128]{3,2,1,0:T(8,128)(2,1)} custom-call(bf16[8,2,128,256]{3,2,1,0:T(8,128)(2,1)S(1)} %get-tuple-element.27.prefix_ref, bf16[2,128,128]{2,1,0:T(8,128)(2,1)S(1)} %collective-permute-done.1.start_ref), custom_call_target="tpu_custom_call" | custom-call | tf_op jit(solution)/shard_map/apply/pallas_call | solution.py:583
  48.8 4.4 %all-to-all-start.1 = ((bf16[16,128,128]{2,1,0:T(8,128)(2,1)}), bf16[16,128,128]{2,1,0:T(8,128)(2,1)S(1)}, u32[]{:S(2)}, u32[]{:S(2)}) async-start(bf16[16,128,128]{2,1,0:T(8,128)(2,1)} %bitcast.5), calls=%async_computation.1 | async-start | bytes 1048576 | tf_op jit(solution)/shard_map/all_to_all | solution.py:589
  53.2 7.7 %all-to-all-done.1.starts_ref = bf16[16,128,128]{2,1,0:T(8,128)(2,1)S(1)} async-done(((bf16[16,128,128]{2,1,0:T(8,128)(2,1)}), bf16[16,128,128]{2,1,0:T(8,128)(2,1)S(1)}, u32[]{:S(2)}, u32[]{:S(2)}) %all-to-all-start.1) | async-done | bytes 524320 | tf_op jit(solution)/shard_map/all_to_all | solution.py:589
  60.9 0.0 copy-done.1
  60.9 7.3 %project.1 = (bf16[192,2048]{1,0:T(8,128)(2,1)S(1)}, bf16[192,2048]{1,0:T(8,128)(2,1)S(1)}) custom-call(s32[1]{0:T(128)} %bitcast.place_ref, bf16[16,128,128]{2,1,0:T(8,128)(2,1)S(1)} %all-to-all-done.1.starts_ref, bf16[6,384,256]{2,1,0:T(8,128)(2,1)S(1)} %copy-done.1, bf16[18,384,256]{2,1,0:T(8,128)(2,1)} %get-tuple-element.30.parts_hbm, ...), custom_call_target="tpu_custom_call" | custom-call | tf_op jit(solution)/shard_map/project/pallas_call | solution.py:672
  68.2 0.1 collective-permute-start.2
  68.3 2.3 %collective-permute-done.2 = bf16[192,2048]{1,0:T(8,128)(2,1)S(1)} collective-permute-done((bf16[192,2048]{1,0:T(8,128)(2,1)S(1)}, bf16[192,2048]{1,0:T(8,128)(2,1)S(1)}, u32[]{:S(2)}, u32[]{:S(2)}) %collective-permute-start.2) | collective-permute-done | bytes 786464 | tf_op jit(solution)/shard_map/ppermute | solution.py:690
  70.5 1.2 %add_convert_fusion = bf16[192,2048]{1,0:T(8,128)(2,1)} fusion(bf16[192,2048]{1,0:T(8,128)(2,1)S(1)} %collective-permute-done.2, bf16[192,2048]{1,0:T(8,128)(2,1)S(1)} %get-tuple-element.31), kind=kLoop, calls=%fused_computation | loop fusion | flops 1572864 | bytes 2359296 | tf_op jit(solution)/shard_map/convert_element_type | solution.py:691
Async XLA Ops:
  0.0 6.6 %copy-start.2 = (bf16[384,1024]{1,0:T(8,128)(2,1)S(1)}, bf16[384,1024]{1,0:T(8,128)(2,1)}, u32[]{:S(2)}) copy-start(bf16[384,1024]{1,0:T(8,128)(2,1)} %key_ref.3) | copy-start | bytes 2359300
  0.0 6.6 %copy-start = (bf16[384,2048]{1,0:T(8,128)(2,1)S(1)}, bf16[384,2048]{1,0:T(8,128)(2,1)}, u32[]{:S(2)}) copy-start(bf16[384,2048]{1,0:T(8,128)(2,1)} %value_ref.3) | copy-start | bytes 4718596
  0.0 6.6 %copy-start.4 = (f32[384,16]{0,1:T(8,128)S(1)}, f32[384,16]{0,1:T(8,128)}, u32[]{:S(2)}) copy-start(f32[384,16]{0,1:T(8,128)} %param.19) | copy-start | bytes 73732
  0.0 6.6 %copy-start.6 = (f32[384,16]{0,1:T(8,128)S(1)}, f32[384,16]{0,1:T(8,128)}, u32[]{:S(2)}) copy-start(f32[384,16]{0,1:T(8,128)} %param.18) | copy-start | bytes 73732
  0.0 6.6 %copy-start.7 = (f32[4,1024]{1,0:T(4,128)S(1)}, f32[4,1024]{1,0:T(4,128)}, u32[]{:S(2)}) copy-start(f32[4,1024]{1,0:T(4,128)} %key_taps.3) | copy-start | bytes 49156
  0.0 6.6 %copy-start.5 = (f32[4,2048]{1,0:T(4,128)S(1)}, f32[4,2048]{1,0:T(4,128)}, u32[]{:S(2)}) copy-start(f32[4,2048]{1,0:T(4,128)} %value_taps.3) | copy-start | bytes 98308
  1.7 13.2 %collective-permute-start = (bf16[3,4096]{1,0:T(4,128)(2,1)}, bf16[3,4096]{1,0:T(4,128)(2,1)S(1)}, u32[]{:S(2)}, u32[]{:S(2)}) collective-permute-start(bf16[3,4096]{1,0:T(4,128)(2,1)} %tails.1), channel_id=1, source_target_pairs={{0,2},{2,4},{4,6},{6,8},{8,10},{10,12},{12,14},{14,16},{16,18},{18... | collective-permute-start | bytes 73736 | tf_op jit(solution)/shard_map/ppermute | solution.py:549
  14.9 7.0 %copy-start.3 = (bf16[3,4096]{1,0:T(4,128)(2,1)}, bf16[3,4096]{1,0:T(4,128)(2,1)S(1)}, u32[]{:S(2)}) copy-start(bf16[3,4096]{1,0:T(4,128)(2,1)S(1)} %collective-permute-done.key_before.value_before.query_before) | copy-start | bytes 73732
  21.8 19.1 %all-to-all-start = ((bf16[16,128,256]{2,1,0:T(8,128)(2,1)}), bf16[16,128,256]{2,1,0:T(8,128)(2,1)S(1)}, u32[]{:S(2)}, u32[]{:S(2)}) async-start(bf16[16,128,256]{2,1,0:T(8,128)(2,1)} %get-tuple-element.20), calls=%async_computation | async-start | bytes 2097152 | tf_op jit(solution)/shard_map/all_to_all | solution.py:572
  42.1 18.8 %copy-start.1 = (bf16[6,384,256]{2,1,0:T(8,128)(2,1)S(1)}, bf16[6,384,256]{2,1,0:T(8,128)(2,1)}, u32[]{:S(2)}) copy-start(bf16[6,384,256]{2,1,0:T(8,128)(2,1)} %get-tuple-element.29.ahead_ref) | copy-start | bytes 3538948
  42.1 5.6 %collective-permute-start.1 = (bf16[2,128,128]{2,1,0:T(8,128)(2,1)S(1)}, bf16[2,128,128]{2,1,0:T(8,128)(2,1)S(1)}, u32[]{:S(2)}, u32[]{:S(2)}) collective-permute-start(bf16[2,128,128]{2,1,0:T(8,128)(2,1)S(1)} %get-tuple-element.28), channel_id=1, source_target_pairs={{0,16},{2,18},{4,20},{6,22},{8,24},{10,26},{12,28},{14,30},{1,17},... | collective-permute-start | bytes 196616 | tf_op jit(solution)/shard_map/ppermute | solution.py:549
  48.8 12.1 %all-to-all-start.1 = ((bf16[16,128,128]{2,1,0:T(8,128)(2,1)}), bf16[16,128,128]{2,1,0:T(8,128)(2,1)S(1)}, u32[]{:S(2)}, u32[]{:S(2)}) async-start(bf16[16,128,128]{2,1,0:T(8,128)(2,1)} %bitcast.5), calls=%async_computation.1 | async-start | bytes 1048576 | tf_op jit(solution)/shard_map/all_to_all | solution.py:589
  68.2 2.4 %collective-permute-start.2 = (bf16[192,2048]{1,0:T(8,128)(2,1)S(1)}, bf16[192,2048]{1,0:T(8,128)(2,1)S(1)}, u32[]{:S(2)}, u32[]{:S(2)}) collective-permute-start(bf16[192,2048]{1,0:T(8,128)(2,1)S(1)} %get-tuple-element.32), channel_id=1, source_target_pairs={{0,1},{1,0},{2,3},{3,2},{4,5},{5,4},{6,7},{7,6},{8,9},{9,8},{10,11... | collective-permute-start | bytes 2359304 | tf_op jit(solution)/shard_map/ppermute | solution.py:690

commit v11 on v10

--- a/solution.py
+++ b/solution.py
@@ -28,8 +28,8 @@
     return 0.5 + 0.5 * jnp.tanh(0.5 * x)
 
 
-def conv_silu(padded, first, rows, taps_ref, head):
-    taps = taps_ref[:, head_of(head)]
+def conv_silu(padded, first, rows, taps_ref, head, before=0):
+    taps = taps_ref[:, pl.ds(pl.multiple_of((before + head) * DK, DK), DK)]
     summed = taps[0:1] * padded[head, first : first + rows, :]
     for offset in range(1, 4):
         summed = summed + taps[offset : offset + 1] * padded[head, first + offset : first + offset + rows, :]
@@ -205,7 +205,7 @@
 
 def later_kernel(
     key_ref, value_ref, key_taps, value_taps, beta_ref, decay_ref,
-    solved_ref, moves_ref, key_padded, value_padded,
+    solved_hbm, moves_hbm, key_padded, value_padded, solved_ref, moves_ref, sem,
 ):
     length = key_ref.shape[0]
     chunks = range(1, length // CHUNK)
@@ -221,16 +221,16 @@
             padded[head] = raw_ref[skip:, pl.ds(first, DK)].astype(F32)
     key, turned = {}, {}
     for j in range(key_heads):
-        unit = unit_rows(conv_silu(key_padded, 13, count, key_taps, j))
+        unit = unit_rows(conv_silu(key_padded, 13, count, key_taps, j, step * key_heads))
         for head in range(j * repeat_by, (j + 1) * repeat_by):
-            solved_ref[head, :, DV + DK :] = unit.astype(BF16)
+            solved_ref[step * heads + head, :, DV + DK :] = unit.astype(BF16)
         for chunk in chunks:
             key[chunk, j] = unit[part_of(chunk - 1)]
             turned[chunk, j] = key[chunk, j].T
     value = {}
 
     def make_value(head):
-        value[head] = conv_silu(value_padded, 13, count, value_taps, head)
+        value[head] = conv_silu(value_padded, 13, count, value_taps, head, step * heads)
 
     def value_of(pack):
         chunk, head = packs[pack]
@@ -246,30 +246,46 @@
         value_of,
     )
     tail = jnp.exp(fade[:, CHUNK - 1 : CHUNK] - fade)
+
+    def leaving(held, out, at_step, kind):
+        here = pl.ds(at_step * heads, heads)
+        return pltpu.make_async_copy(held.at[here], out.at[here], sem.at[kind, at_step])
+
+    solved = [one.astype(BF16) for one in solved]
     for pack, (chunk, head) in enumerate(packs):
-        one = solved[pack].astype(BF16)
-        solved_ref[head, part_of(chunk - 1), : DV + DK] = one
-        moves_ref[head, chunk - 1] = mul(
-            turned[chunk, head // repeat_by] * tail[pack : pack + 1, :], one
+        solved_ref[step * heads + head, part_of(chunk - 1), : DV + DK] = solved[pack]
+    leaving(solved_ref, solved_hbm, step, 0).start()
+    for pack, (chunk, head) in enumerate(packs):
+        moves_ref[step * heads + head, chunk - 1] = mul(
+            turned[chunk, head // repeat_by] * tail[pack : pack + 1, :], solved[pack]
         ).astype(BF16)
+    leaving(moves_ref, moves_hbm, step, 1).start()
+
+    @pl.when(step == pl.num_programs(0) - 1)
+    def _():
+        for at_step in range(sem.shape[1]):
+            leaving(solved_ref, solved_hbm, at_step, 0).wait()
+            leaving(moves_ref, moves_hbm, at_step, 1).wait()
 
 
 def states_kernel(
-    key_ref, value_ref, key_before, value_before, key_taps, value_taps, beta_ref, decay_ref, moves_hbm,
+    key_ref, value_hbm, before_ref, key_taps, value_taps, beta_ref, decay_ref, moves_hbm,
     pairs_hbm, solved_hbm, starts_hbm,
-    key_padded, value_padded, moves_ref, solved_ref, starts_ref, pairs_ref, in_sem, out_sem, pairs_sem,
+    key_padded, value_padded, value_ref, moves_ref, solved_ref, starts_ref, pairs_ref,
+    value_sem, in_sem, out_sem, pairs_sem,
 ):
     heads, length = decay_ref.shape
     chunks = length // CHUNK
     key_heads = key_ref.shape[1] // DK
     repeat_by = heads // key_heads
+    value_copy = pltpu.make_async_copy(value_hbm.at[pl.ds(0, CHUNK)], value_ref, value_sem)
+    value_copy.start()
     incoming = pltpu.make_async_copy(moves_hbm, moves_ref, in_sem)
     incoming.start()
 
-    widen(key_padded, 5, 3, key_before[...])
-    widen(key_padded, 8, CHUNK, key_ref[...])
-    widen(value_padded, 5, 3, value_before[...])
-    widen(value_padded, 8, CHUNK, value_ref[...])
+    key_at = before_ref.shape[1] - key_ref.shape[1]
+    widen(key_padded, 5, 3, before_ref[:, key_at:])
+    widen(key_padded, 8, CHUNK, key_ref[:CHUNK, :])
     key, turned = [], []
     for j in range(key_heads):
         key.append(unit_rows(conv_silu(key_padded, 5, CHUNK, key_taps, j)))
@@ -279,6 +295,11 @@
     fade = log_fades(chunk_rows(decay_ref, heads, range(chunks)))
     value = {}
 
+    def value_rows():
+        value_copy.wait()
+        widen(value_padded, 5, 3, before_ref[:, : value_ref.shape[1]])
+        widen(value_padded, 8, CHUNK, value_ref[...])
+
     def make_value(head):
         value[head] = conv_silu(value_padded, 5, CHUNK, value_taps, head)
 
@@ -287,7 +308,7 @@
         beta_ref[:, :CHUNK],
         [key[head // repeat_by] for head in range(heads)],
         [turned[head // repeat_by] for head in range(heads)],
-        [functools.partial(make_value, head) for head in range(heads)],
+        [value_rows] + [functools.partial(make_value, head) for head in range(heads)],
         lambda head: value[head],
     )
     last = jnp.exp(fade[:, CHUNK - 1 : CHUNK])
@@ -431,11 +452,9 @@
         later_kernel,
         grid=(steps,),
         in_specs=[
-            vmem, vmem, columns_of(4, narrow), columns_of(4, wide), logits, logits,
+            vmem, vmem, vmem, vmem, vmem, vmem,
         ],
-        out_specs=[
-            of_heads(later, DV + 2 * DK), of_heads(chunks - 1, DK, DV + DK),
-        ],
+        out_specs=[hbm, hbm],
         out_shape=[
             jax.ShapeDtypeStruct((value_heads, later, DV + 2 * DK), BF16),
             jax.ShapeDtypeStruct((value_heads, chunks - 1, DK, DV + DK), BF16),
@@ -443,6 +462,9 @@
         scratch_shapes=[
             pltpu.VMEM((each, later + 16, DK), F32),
             pltpu.VMEM((each * repeat_by, later + 16, DV), F32),
+            pltpu.VMEM((value_heads, later, DV + 2 * DK), BF16),
+            pltpu.VMEM((value_heads, chunks - 1, DK, DV + DK), BF16),
+            pltpu.SemaphoreType.DMA((2, steps)),
         ],
         compiler_params=in_vmem(50),
         cost_estimate=pl.CostEstimate(flops=30 * work, bytes_accessed=0, transcendentals=0),
@@ -455,9 +477,7 @@
         states_kernel,
         grid=(1,),
         in_specs=[
-            whole((CHUNK, narrow)), whole((CHUNK, wide)),
-            whole((3, narrow), 0, repeat_by + 1), whole((3, wide)),
-            whole(taps[1].shape), whole(taps[2].shape), whole(beta.shape), whole(decay.shape), hbm,
+            vmem, hbm, vmem, vmem, vmem, vmem, vmem, hbm,
         ],
         out_specs=[hbm, hbm, hbm],
         out_shape=[
@@ -468,10 +488,12 @@
         scratch_shapes=[
             pltpu.VMEM((key_heads, 8 + CHUNK, DK), F32),
             pltpu.VMEM((value_heads, 8 + CHUNK, DV), F32),
+            pltpu.VMEM((CHUNK, wide), BF16),
             pltpu.VMEM(moves.shape, BF16),
             pltpu.VMEM((value_heads, CHUNK, DV + 2 * DK), BF16),
             pltpu.VMEM((chunks - 1, value_heads, DK, DV + DK), BF16),
             pltpu.VMEM((value_heads, DK, DV + DK), BF16),
+            pltpu.SemaphoreType.DMA,
             pltpu.SemaphoreType.DMA,
             pltpu.SemaphoreType.DMA((chunks,)),
             pltpu.SemaphoreType.DMA((value_heads // min(HEADS_AT_ONCE, value_heads),)),
@@ -479,7 +501,7 @@
         compiler_params=in_vmem(52),
         cost_estimate=pl.CostEstimate(flops=20 * work, bytes_accessed=0, transcendentals=0),
         name="states",
-    )(raws[1], raws[2], before, before, taps[1], taps[2], beta, decay, moves)
+    )(raws[1], raws[2], before, taps[1], taps[2], beta, decay, moves)
     gain = norm_gain.reshape(1, DV)
 
     def local():

time: 72.1 us -> 71.4 us (level)
  no operation moved by 1% of the time
where the time goes in v11:
time: 71.4 us; the launch traced here: 71.1 us
  Pallas kernels  38.8 us (54%)
  starting transfers between devices  17.8 us (25%)
  waiting for transfers between devices  13.1 us (18%)
  other arithmetic  1.15 us (2%)
    pallas_call x1, Pallas kernels, local(): pl.pallas_call(local_kernel, grid=(steps,), in_specs=[columns_of(length,...  13.1 us
    ppermute x2, starting transfers between devices, shifted(): return lax.ppermute(value, axis, [(i, i + by) for i in range(count - by)])  8.56 us
    pallas_call x1, Pallas kernels, local_steps(): pl.pallas_call(later_kernel, grid=(steps,), in_specs=[vmem, vmem, vmem, v...  8.29 us
    all_to_all x1, waiting for transfers between devices, starts_of(): lax.all_to_all(starts.reshape(heads, DK, DV), axis, 0, 0, axis_index_grou...  7.67 us
    pallas_call x1, Pallas kernels, projected(): pl.pallas_call(project_kernel if halves else whole_kernel, in_specs=[pl.B...  7.27 us
    pallas_call x1, Pallas kernels, local_steps(): pl.pallas_call(states_kernel, grid=(1,), in_specs=[vmem, hbm, vmem, vmem,...  6.26 us
    all_to_all x1, starting transfers between devices, starts_of(): lax.all_to_all(pairs, axis, 0, 0, axis_index_groups=groups, tiled=True)  4.75 us
    all_to_all x1, starting transfers between devices, starts_of(): lax.all_to_all(starts.reshape(heads, DK, DV), axis, 0, 0, axis_index_grou...  4.44 us
  transfers between devices with their start and end apart: 5, of which 4 were waited for; matrix products, arithmetic and copies ran while one was open for 0% of the time, Pallas kernels for 30%

profile of v11, /device:TPU:0, one launch (start us, length us, event | category | flops | bytes accessed | tf_op | source)
XLA Modules:
  0.0 71.1 jit_solution(11766288223078067401)
XLA Ops:
  0.0 0.0 copy-start.2
  0.0 0.0 copy-start
  0.0 0.0 copy-start.4
  0.0 0.0 copy-start.6
  0.0 0.0 copy-start.7
  0.0 0.0 copy-start.5
  0.0 1.7 %tails.1 = bf16[3,4096]{1,0:T(4,128)(2,1)} custom-call(bf16[384,2048]{1,0:T(8,128)(2,1)} %value_hbm.3, bf16[384,1024]{1,0:T(8,128)(2,1)} %query_ref.1, bf16[384,1024]{1,0:T(8,128)(2,1)} %key_ref.3), custom_call_target="tpu_custom_call" | custom-call | tf_op jit(solution)/shard_map/tails/pallas_call | solution.py:735
  1.7 4.9 %collective-permute-start = (bf16[3,4096]{1,0:T(4,128)(2,1)}, bf16[3,4096]{1,0:T(4,128)(2,1)S(1)}, u32[]{:S(2)}, u32[]{:S(2)}) collective-permute-start(bf16[3,4096]{1,0:T(4,128)(2,1)} %tails.1), channel_id=1, source_target_pairs={{0,2},{2,4},{4,6},{6,8},{8,10},{10,12},{12,14},{14,16},{16,18},{18... | collective-permute-start | bytes 73736 | tf_op jit(solution)/shard_map/ppermute | solution.py:571
  6.6 0.0 copy-done.2
  6.6 0.0 copy-done
  6.6 0.0 copy-done.4
  6.6 0.0 copy-done.6
  6.6 0.0 copy-done.7
  6.6 0.0 copy-done.5
  6.6 8.3 %later.1 = (bf16[16,256,384]{2,1,0:T(8,128)(2,1)}, bf16[16,2,128,256]{3,2,1,0:T(8,128)(2,1)}) custom-call(bf16[384,1024]{1,0:T(8,128)(2,1)S(1)} %copy-done.2, bf16[384,2048]{1,0:T(8,128)(2,1)S(1)} %copy-done, f32[4,1024]{1,0:T(4,128)S(1)} %copy-done.7, f32[4,2048]{1,0:T(4,128)S(1)} %copy-done.5, f32[16,384]{1,0:T(8,128)S(1)} %bitcast.10, f32[16,384]{1,0:T(8,128)S(1)} %bitcast.8), custom_call_target="tpu_custom_call" | custom-call | flops 3019898880 | tf_op jit(solution)/shard_map/later/pallas_call | solution.py:451
  14.9 0.0 collective-permute-done.before_ref.query_before
  14.9 0.0 copy-start.3
  14.9 6.3 %states.1 = (bf16[16,128,256]{2,1,0:T(8,128)(2,1)}, bf16[16,128,384]{2,1,0:T(8,128)(2,1)}, bf16[2,16,128,256]{3,2,1,0:T(8,128)(2,1)}) custom-call(bf16[384,1024]{1,0:T(8,128)(2,1)S(1)} %copy-done.2, bf16[384,2048]{1,0:T(8,128)(2,1)} %value_hbm.3, bf16[3,4096]{1,0:T(4,128)(2,1)S(1)} %collective-permute-done.before_ref.query_before, f32[4,1024]{1,0:T(4,128)S(1)} %copy-done.7, ...), custom_call_target="tpu_custom_call" | custom-call | flops 2013265920 | tf_op jit(solution)/shard_map/states/pallas_call | solution.py:476
  21.2 0.0 copy-done.3
  21.2 4.8 %all-to-all-start = ((bf16[16,128,256]{2,1,0:T(8,128)(2,1)}), bf16[16,128,256]{2,1,0:T(8,128)(2,1)S(1)}, u32[]{:S(2)}, u32[]{:S(2)}) async-start(bf16[16,128,256]{2,1,0:T(8,128)(2,1)} %get-tuple-element.20), calls=%async_computation | async-start | bytes 2097152 | tf_op jit(solution)/shard_map/all_to_all | solution.py:594
  26.0 13.1 %local.1 = (bf16[6,384,256]{2,1,0:T(8,128)(2,1)}, bf16[18,384,256]{2,1,0:T(8,128)(2,1)}) custom-call(bf16[384,1024]{1,0:T(8,128)(2,1)} %query_ref.1, bf16[3,4096]{1,0:T(4,128)(2,1)} %copy-done.3, f32[4,1024]{1,0:T(4,128)} %query_taps.1, f32[16,384]{1,0:T(8,128)} %bitcast.7, bf16[16,128,384]{2,1,0:T(8,128)(2,1)} %get-tuple-element.21.first_solved, ...), custom_call_target="tpu_custom_call" | custom-call | flops 1207959552 | tf_op jit(solution)/shard_map/local/pallas_call | solution.py:511
  39.1 1.3 %all-to-all-done = bf16[16,128,256]{2,1,0:T(8,128)(2,1)S(1)} async-done(((bf16[16,128,256]{2,1,0:T(8,128)(2,1)}), bf16[16,128,256]{2,1,0:T(8,128)(2,1)S(1)}, u32[]{:S(2)}, u32[]{:S(2)}) %all-to-all-start) | async-done | bytes 1048608 | tf_op jit(solution)/shard_map/all_to_all | solution.py:594
  40.4 1.1 %prefix.1 = (bf16[8,2,128,256]{3,2,1,0:T(8,128)(2,1)S(1)}, bf16[2,128,128]{2,1,0:T(8,128)(2,1)S(1)}) custom-call(bf16[8,2,128,256]{3,2,1,0:T(8,128)(2,1)S(1)} %bitcast.6), custom_call_target="tpu_custom_call" | custom-call | tf_op jit(solution)/shard_map/prefix/pallas_call | solution.py:596
  41.5 0.0 copy-start.1
  41.5 3.7 %collective-permute-start.1 = (bf16[2,128,128]{2,1,0:T(8,128)(2,1)S(1)}, bf16[2,128,128]{2,1,0:T(8,128)(2,1)S(1)}, u32[]{:S(2)}, u32[]{:S(2)}) collective-permute-start(bf16[2,128,128]{2,1,0:T(8,128)(2,1)S(1)} %get-tuple-element.28), channel_id=1, source_target_pairs={{0,16},{2,18},{4,20},{6,22},{8,24},{10,26},{12,28},{14,30},{1,17},... | collective-permute-start | bytes 196616 | tf_op jit(solution)/shard_map/ppermute | solution.py:571
  45.2 1.9 %collective-permute-done.1.start_ref = bf16[2,128,128]{2,1,0:T(8,128)(2,1)S(1)} collective-permute-done((bf16[2,128,128]{2,1,0:T(8,128)(2,1)S(1)}, bf16[2,128,128]{2,1,0:T(8,128)(2,1)S(1)}, u32[]{:S(2)}, u32[]{:S(2)}) %collective-permute-start.1) | collective-permute-done | bytes 65568 | tf_op jit(solution)/shard_map/ppermute | solution.py:571
  47.1 1.1 %apply.1 = bf16[8,2,128,128]{3,2,1,0:T(8,128)(2,1)} custom-call(bf16[8,2,128,256]{3,2,1,0:T(8,128)(2,1)S(1)} %get-tuple-element.27.prefix_ref, bf16[2,128,128]{2,1,0:T(8,128)(2,1)S(1)} %collective-permute-done.1.start_ref), custom_call_target="tpu_custom_call" | custom-call | tf_op jit(solution)/shard_map/apply/pallas_call | solution.py:605
  48.2 4.4 %all-to-all-start.1 = ((bf16[16,128,128]{2,1,0:T(8,128)(2,1)}), bf16[16,128,128]{2,1,0:T(8,128)(2,1)S(1)}, u32[]{:S(2)}, u32[]{:S(2)}) async-start(bf16[16,128,128]{2,1,0:T(8,128)(2,1)} %bitcast.5), calls=%async_computation.1 | async-start | bytes 1048576 | tf_op jit(solution)/shard_map/all_to_all | solution.py:611
  52.6 7.7 %all-to-all-done.1.starts_ref = bf16[16,128,128]{2,1,0:T(8,128)(2,1)S(1)} async-done(((bf16[16,128,128]{2,1,0:T(8,128)(2,1)}), bf16[16,128,128]{2,1,0:T(8,128)(2,1)S(1)}, u32[]{:S(2)}, u32[]{:S(2)}) %all-to-all-start.1) | async-done | bytes 524320 | tf_op jit(solution)/shard_map/all_to_all | solution.py:611
  60.3 0.0 copy-done.1
  60.3 7.3 %project.1 = (bf16[192,2048]{1,0:T(8,128)(2,1)S(1)}, bf16[192,2048]{1,0:T(8,128)(2,1)S(1)}) custom-call(s32[1]{0:T(128)} %bitcast.place_ref, bf16[16,128,128]{2,1,0:T(8,128)(2,1)S(1)} %all-to-all-done.1.starts_ref, bf16[6,384,256]{2,1,0:T(8,128)(2,1)S(1)} %copy-done.1, bf16[18,384,256]{2,1,0:T(8,128)(2,1)} %get-tuple-element.30.parts_hbm, ...), custom_call_target="tpu_custom_call" | custom-call | tf_op jit(solution)/shard_map/project/pallas_call | solution.py:694
  67.6 0.1 collective-permute-start.2
  67.7 2.3 %collective-permute-done.2 = bf16[192,2048]{1,0:T(8,128)(2,1)S(1)} collective-permute-done((bf16[192,2048]{1,0:T(8,128)(2,1)S(1)}, bf16[192,2048]{1,0:T(8,128)(2,1)S(1)}, u32[]{:S(2)}, u32[]{:S(2)}) %collective-permute-start.2) | collective-permute-done | bytes 786464 | tf_op jit(solution)/shard_map/ppermute | solution.py:712
  69.9 1.2 %add_convert_fusion = bf16[192,2048]{1,0:T(8,128)(2,1)} fusion(bf16[192,2048]{1,0:T(8,128)(2,1)S(1)} %collective-permute-done.2, bf16[192,2048]{1,0:T(8,128)(2,1)S(1)} %get-tuple-element.31), kind=kLoop, calls=%fused_computation | loop fusion | flops 1572864 | bytes 2359296 | tf_op jit(solution)/shard_map/convert_element_type | solution.py:713
Async XLA Ops:
  0.0 6.6 %copy-start.2 = (bf16[384,1024]{1,0:T(8,128)(2,1)S(1)}, bf16[384,1024]{1,0:T(8,128)(2,1)}, u32[]{:S(2)}) copy-start(bf16[384,1024]{1,0:T(8,128)(2,1)} %key_ref.3) | copy-start | bytes 2359300
  0.0 6.6 %copy-start = (bf16[384,2048]{1,0:T(8,128)(2,1)S(1)}, bf16[384,2048]{1,0:T(8,128)(2,1)}, u32[]{:S(2)}) copy-start(bf16[384,2048]{1,0:T(8,128)(2,1)} %value_hbm.3) | copy-start | bytes 4718596
  0.0 6.6 %copy-start.4 = (f32[384,16]{0,1:T(8,128)S(1)}, f32[384,16]{0,1:T(8,128)}, u32[]{:S(2)}) copy-start(f32[384,16]{0,1:T(8,128)} %param.19) | copy-start | bytes 73732
  0.0 6.6 %copy-start.6 = (f32[384,16]{0,1:T(8,128)S(1)}, f32[384,16]{0,1:T(8,128)}, u32[]{:S(2)}) copy-start(f32[384,16]{0,1:T(8,128)} %param.18) | copy-start | bytes 73732
  0.0 6.6 %copy-start.7 = (f32[4,1024]{1,0:T(4,128)S(1)}, f32[4,1024]{1,0:T(4,128)}, u32[]{:S(2)}) copy-start(f32[4,1024]{1,0:T(4,128)} %key_taps.3) | copy-start | bytes 49156
  0.0 6.6 %copy-start.5 = (f32[4,2048]{1,0:T(4,128)S(1)}, f32[4,2048]{1,0:T(4,128)}, u32[]{:S(2)}) copy-start(f32[4,2048]{1,0:T(4,128)} %value_taps.3) | copy-start | bytes 98308
  1.7 13.2 %collective-permute-start = (bf16[3,4096]{1,0:T(4,128)(2,1)}, bf16[3,4096]{1,0:T(4,128)(2,1)S(1)}, u32[]{:S(2)}, u32[]{:S(2)}) collective-permute-start(bf16[3,4096]{1,0:T(4,128)(2,1)} %tails.1), channel_id=1, source_target_pairs={{0,2},{2,4},{4,6},{6,8},{8,10},{10,12},{12,14},{14,16},{16,18},{18... | collective-permute-start | bytes 73736 | tf_op jit(solution)/shard_map/ppermute | solution.py:571
  14.9 6.3 %copy-start.3 = (bf16[3,4096]{1,0:T(4,128)(2,1)}, bf16[3,4096]{1,0:T(4,128)(2,1)S(1)}, u32[]{:S(2)}) copy-start(bf16[3,4096]{1,0:T(4,128)(2,1)S(1)} %collective-permute-done.before_ref.query_before) | copy-start | bytes 73732
  21.2 19.1 %all-to-all-start = ((bf16[16,128,256]{2,1,0:T(8,128)(2,1)}), bf16[16,128,256]{2,1,0:T(8,128)(2,1)S(1)}, u32[]{:S(2)}, u32[]{:S(2)}) async-start(bf16[16,128,256]{2,1,0:T(8,128)(2,1)} %get-tuple-element.20), calls=%async_computation | async-start | bytes 2097152 | tf_op jit(solution)/shard_map/all_to_all | solution.py:594
  41.5 18.8 %copy-start.1 = (bf16[6,384,256]{2,1,0:T(8,128)(2,1)S(1)}, bf16[6,384,256]{2,1,0:T(8,128)(2,1)}, u32[]{:S(2)}) copy-start(bf16[6,384,256]{2,1,0:T(8,128)(2,1)} %get-tuple-element.29.ahead_ref) | copy-start | bytes 3538948
  41.5 5.6 %collective-permute-start.1 = (bf16[2,128,128]{2,1,0:T(8,128)(2,1)S(1)}, bf16[2,128,128]{2,1,0:T(8,128)(2,1)S(1)}, u32[]{:S(2)}, u32[]{:S(2)}) collective-permute-start(bf16[2,128,128]{2,1,0:T(8,128)(2,1)S(1)} %get-tuple-element.28), channel_id=1, source_target_pairs={{0,16},{2,18},{4,20},{6,22},{8,24},{10,26},{12,28},{14,30},{1,17},... | collective-permute-start | bytes 196616 | tf_op jit(solution)/shard_map/ppermute | solution.py:571
  48.2 12.1 %all-to-all-start.1 = ((bf16[16,128,128]{2,1,0:T(8,128)(2,1)}), bf16[16,128,128]{2,1,0:T(8,128)(2,1)S(1)}, u32[]{:S(2)}, u32[]{:S(2)}) async-start(bf16[16,128,128]{2,1,0:T(8,128)(2,1)} %bitcast.5), calls=%async_computation.1 | async-start | bytes 1048576 | tf_op jit(solution)/shard_map/all_to_all | solution.py:611
  67.6 2.4 %collective-permute-start.2 = (bf16[192,2048]{1,0:T(8,128)(2,1)S(1)}, bf16[192,2048]{1,0:T(8,128)(2,1)S(1)}, u32[]{:S(2)}, u32[]{:S(2)}) collective-permute-start(bf16[192,2048]{1,0:T(8,128)(2,1)S(1)} %get-tuple-element.32), channel_id=1, source_target_pairs={{0,1},{1,0},{2,3},{3,2},{4,5},{5,4},{6,7},{7,6},{8,9},{9,8},{10,11... | collective-permute-start | bytes 2359304 | tf_op jit(solution)/shard_map/ppermute | solution.py:712

commit v12 on v11

--- a/solution.py
+++ b/solution.py
@@ -646,16 +646,19 @@
     weights(0).start()
     if groups > 1:
         parts(1).start()
+    following = normed_group(0)
+    if groups > 1:
         weights(1).start()
-    following = normed_group(0)
+    if groups > 2:
+        parts(2).start()
     for g in range(groups):
         weights(g).wait()
-        if g + 2 < groups:
-            weights(g + 2).start()
         if g + 1 < groups:
             parts(g + 1).wait()
         if g + 2 < groups:
-            parts(g + 2).start()
+            weights(g + 2).start()
+        if g + 3 < groups:
+            parts(g + 3).start()
         normed = following
         if g + 1 < groups:
             following = normed_group(g + 1)

time: 71.4 us -> 70.5 us (0.987)
  Pallas kernels: 38.8 us -> 37.9 us
    pallas_call x1, Pallas kernels: 7.27 us -> 6.36 us  [projected(): pl.pallas_call(project_kernel if halves else whole_kernel, in_specs=[pl.B...]
  transfers between devices with their start and end apart: 5 -> 5, of which waited for: 4 -> 4; matrix products, arithmetic and copies ran while one was open for 0% -> 0% of each run, Pallas kernels for 30% -> 31%
where the time goes in v12:
time: 70.5 us; the launch traced here: 70.2 us
  Pallas kernels  37.9 us (54%)
  starting transfers between devices  17.8 us (25%)
  waiting for transfers between devices  13.1 us (19%)
  other arithmetic  1.15 us (2%)
    pallas_call x1, Pallas kernels, local(): pl.pallas_call(local_kernel, grid=(steps,), in_specs=[columns_of(length,...  13.1 us
    ppermute x2, starting transfers between devices, shifted(): return lax.ppermute(value, axis, [(i, i + by) for i in range(count - by)])  8.56 us
    pallas_call x1, Pallas kernels, local_steps(): pl.pallas_call(later_kernel, grid=(steps,), in_specs=[vmem, vmem, vmem, v...  8.29 us
    all_to_all x1, waiting for transfers between devices, starts_of(): lax.all_to_all(starts.reshape(heads, DK, DV), axis, 0, 0, axis_index_grou...  7.67 us
    pallas_call x1, Pallas kernels, projected(): pl.pallas_call(project_kernel if halves else whole_kernel, in_specs=[pl.B...  6.36 us
    pallas_call x1, Pallas kernels, local_steps(): pl.pallas_call(states_kernel, grid=(1,), in_specs=[vmem, hbm, vmem, vmem,...  6.26 us
    all_to_all x1, starting transfers between devices, starts_of(): lax.all_to_all(pairs, axis, 0, 0, axis_index_groups=groups, tiled=True)  4.75 us
    all_to_all x1, starting transfers between devices, starts_of(): lax.all_to_all(starts.reshape(heads, DK, DV), axis, 0, 0, axis_index_grou...  4.44 us
  transfers between devices with their start and end apart: 5, of which 4 were waited for; matrix products, arithmetic and copies ran while one was open for 0% of the time, Pallas kernels for 31%

profile of v12, /device:TPU:0, one launch (start us, length us, event | category | flops | bytes accessed | tf_op | source)
XLA Modules:
  0.0 70.2 jit_solution(6399364134243284847)
XLA Ops:
  0.0 0.0 copy-start.2
  0.0 0.0 copy-start
  0.0 0.0 copy-start.4
  0.0 0.0 copy-start.6
  0.0 0.0 copy-start.7
  0.0 0.0 copy-start.5
  0.0 1.7 %tails.1 = bf16[3,4096]{1,0:T(4,128)(2,1)} custom-call(bf16[384,2048]{1,0:T(8,128)(2,1)} %value_hbm.3, bf16[384,1024]{1,0:T(8,128)(2,1)} %query_ref.1, bf16[384,1024]{1,0:T(8,128)(2,1)} %key_ref.3), custom_call_target="tpu_custom_call" | custom-call | tf_op jit(solution)/shard_map/tails/pallas_call | solution.py:738
  1.7 4.9 %collective-permute-start = (bf16[3,4096]{1,0:T(4,128)(2,1)}, bf16[3,4096]{1,0:T(4,128)(2,1)S(1)}, u32[]{:S(2)}, u32[]{:S(2)}) collective-permute-start(bf16[3,4096]{1,0:T(4,128)(2,1)} %tails.1), channel_id=1, source_target_pairs={{0,2},{2,4},{4,6},{6,8},{8,10},{10,12},{12,14},{14,16},{16,18},{18... | collective-permute-start | bytes 73736 | tf_op jit(solution)/shard_map/ppermute | solution.py:571
  6.6 0.0 copy-done.2
  6.6 0.0 copy-done
  6.6 0.0 copy-done.4
  6.6 0.0 copy-done.6
  6.6 0.0 copy-done.7
  6.6 0.0 copy-done.5
  6.6 8.3 %later.1 = (bf16[16,256,384]{2,1,0:T(8,128)(2,1)}, bf16[16,2,128,256]{3,2,1,0:T(8,128)(2,1)}) custom-call(bf16[384,1024]{1,0:T(8,128)(2,1)S(1)} %copy-done.2, bf16[384,2048]{1,0:T(8,128)(2,1)S(1)} %copy-done, f32[4,1024]{1,0:T(4,128)S(1)} %copy-done.7, f32[4,2048]{1,0:T(4,128)S(1)} %copy-done.5, f32[16,384]{1,0:T(8,128)S(1)} %bitcast.10, f32[16,384]{1,0:T(8,128)S(1)} %bitcast.8), custom_call_target="tpu_custom_call" | custom-call | flops 3019898880 | tf_op jit(solution)/shard_map/later/pallas_call | solution.py:451
  14.9 0.0 collective-permute-done.before_ref.query_before
  14.9 0.0 copy-start.3
  14.9 6.3 %states.1 = (bf16[16,128,256]{2,1,0:T(8,128)(2,1)}, bf16[16,128,384]{2,1,0:T(8,128)(2,1)}, bf16[2,16,128,256]{3,2,1,0:T(8,128)(2,1)}) custom-call(bf16[384,1024]{1,0:T(8,128)(2,1)S(1)} %copy-done.2, bf16[384,2048]{1,0:T(8,128)(2,1)} %value_hbm.3, bf16[3,4096]{1,0:T(4,128)(2,1)S(1)} %collective-permute-done.before_ref.query_before, f32[4,1024]{1,0:T(4,128)S(1)} %copy-done.7, ...), custom_call_target="tpu_custom_call" | custom-call | flops 2013265920 | tf_op jit(solution)/shard_map/states/pallas_call | solution.py:476
  21.2 0.0 copy-done.3
  21.2 4.8 %all-to-all-start = ((bf16[16,128,256]{2,1,0:T(8,128)(2,1)}), bf16[16,128,256]{2,1,0:T(8,128)(2,1)S(1)}, u32[]{:S(2)}, u32[]{:S(2)}) async-start(bf16[16,128,256]{2,1,0:T(8,128)(2,1)} %get-tuple-element.20), calls=%async_computation | async-start | bytes 2097152 | tf_op jit(solution)/shard_map/all_to_all | solution.py:594
  26.0 13.1 %local.1 = (bf16[6,384,256]{2,1,0:T(8,128)(2,1)}, bf16[18,384,256]{2,1,0:T(8,128)(2,1)}) custom-call(bf16[384,1024]{1,0:T(8,128)(2,1)} %query_ref.1, bf16[3,4096]{1,0:T(4,128)(2,1)} %copy-done.3, f32[4,1024]{1,0:T(4,128)} %query_taps.1, f32[16,384]{1,0:T(8,128)} %bitcast.7, bf16[16,128,384]{2,1,0:T(8,128)(2,1)} %get-tuple-element.21.first_solved, ...), custom_call_target="tpu_custom_call" | custom-call | flops 1207959552 | tf_op jit(solution)/shard_map/local/pallas_call | solution.py:511
  39.1 1.3 %all-to-all-done = bf16[16,128,256]{2,1,0:T(8,128)(2,1)S(1)} async-done(((bf16[16,128,256]{2,1,0:T(8,128)(2,1)}), bf16[16,128,256]{2,1,0:T(8,128)(2,1)S(1)}, u32[]{:S(2)}, u32[]{:S(2)}) %all-to-all-start) | async-done | bytes 1048608 | tf_op jit(solution)/shard_map/all_to_all | solution.py:594
  40.4 1.1 %prefix.1 = (bf16[8,2,128,256]{3,2,1,0:T(8,128)(2,1)S(1)}, bf16[2,128,128]{2,1,0:T(8,128)(2,1)S(1)}) custom-call(bf16[8,2,128,256]{3,2,1,0:T(8,128)(2,1)S(1)} %bitcast.6), custom_call_target="tpu_custom_call" | custom-call | tf_op jit(solution)/shard_map/prefix/pallas_call | solution.py:596
  41.5 0.0 copy-start.1
  41.5 3.7 %collective-permute-start.1 = (bf16[2,128,128]{2,1,0:T(8,128)(2,1)S(1)}, bf16[2,128,128]{2,1,0:T(8,128)(2,1)S(1)}, u32[]{:S(2)}, u32[]{:S(2)}) collective-permute-start(bf16[2,128,128]{2,1,0:T(8,128)(2,1)S(1)} %get-tuple-element.28), channel_id=1, source_target_pairs={{0,16},{2,18},{4,20},{6,22},{8,24},{10,26},{12,28},{14,30},{1,17},... | collective-permute-start | bytes 196616 | tf_op jit(solution)/shard_map/ppermute | solution.py:571
  45.2 1.9 %collective-permute-done.1.start_ref = bf16[2,128,128]{2,1,0:T(8,128)(2,1)S(1)} collective-permute-done((bf16[2,128,128]{2,1,0:T(8,128)(2,1)S(1)}, bf16[2,128,128]{2,1,0:T(8,128)(2,1)S(1)}, u32[]{:S(2)}, u32[]{:S(2)}) %collective-permute-start.1) | collective-permute-done | bytes 65568 | tf_op jit(solution)/shard_map/ppermute | solution.py:571
  47.1 1.1 %apply.1 = bf16[8,2,128,128]{3,2,1,0:T(8,128)(2,1)} custom-call(bf16[8,2,128,256]{3,2,1,0:T(8,128)(2,1)S(1)} %get-tuple-element.27.prefix_ref, bf16[2,128,128]{2,1,0:T(8,128)(2,1)S(1)} %collective-permute-done.1.start_ref), custom_call_target="tpu_custom_call" | custom-call | tf_op jit(solution)/shard_map/apply/pallas_call | solution.py:605
  48.2 4.4 %all-to-all-start.1 = ((bf16[16,128,128]{2,1,0:T(8,128)(2,1)}), bf16[16,128,128]{2,1,0:T(8,128)(2,1)S(1)}, u32[]{:S(2)}, u32[]{:S(2)}) async-start(bf16[16,128,128]{2,1,0:T(8,128)(2,1)} %bitcast.5), calls=%async_computation.1 | async-start | bytes 1048576 | tf_op jit(solution)/shard_map/all_to_all | solution.py:611
  52.6 7.7 %all-to-all-done.1.starts_ref = bf16[16,128,128]{2,1,0:T(8,128)(2,1)S(1)} async-done(((bf16[16,128,128]{2,1,0:T(8,128)(2,1)}), bf16[16,128,128]{2,1,0:T(8,128)(2,1)S(1)}, u32[]{:S(2)}, u32[]{:S(2)}) %all-to-all-start.1) | async-done | bytes 524320 | tf_op jit(solution)/shard_map/all_to_all | solution.py:611
  60.3 0.0 copy-done.1
  60.3 6.4 %project.1 = (bf16[192,2048]{1,0:T(8,128)(2,1)S(1)}, bf16[192,2048]{1,0:T(8,128)(2,1)S(1)}) custom-call(s32[1]{0:T(128)} %bitcast.place_ref, bf16[16,128,128]{2,1,0:T(8,128)(2,1)S(1)} %all-to-all-done.1.starts_ref, bf16[6,384,256]{2,1,0:T(8,128)(2,1)S(1)} %copy-done.1, bf16[18,384,256]{2,1,0:T(8,128)(2,1)} %get-tuple-element.30.parts_hbm, ...), custom_call_target="tpu_custom_call" | custom-call | tf_op jit(solution)/shard_map/project/pallas_call | solution.py:697
  66.7 0.1 collective-permute-start.2
  66.8 2.3 %collective-permute-done.2 = bf16[192,2048]{1,0:T(8,128)(2,1)S(1)} collective-permute-done((bf16[192,2048]{1,0:T(8,128)(2,1)S(1)}, bf16[192,2048]{1,0:T(8,128)(2,1)S(1)}, u32[]{:S(2)}, u32[]{:S(2)}) %collective-permute-start.2) | collective-permute-done | bytes 786464 | tf_op jit(solution)/shard_map/ppermute | solution.py:715
  69.0 1.2 %add_convert_fusion = bf16[192,2048]{1,0:T(8,128)(2,1)} fusion(bf16[192,2048]{1,0:T(8,128)(2,1)S(1)} %collective-permute-done.2, bf16[192,2048]{1,0:T(8,128)(2,1)S(1)} %get-tuple-element.31), kind=kLoop, calls=%fused_computation | loop fusion | flops 1572864 | bytes 2359296 | tf_op jit(solution)/shard_map/convert_element_type | solution.py:716
Async XLA Ops:
  0.0 6.6 %copy-start.2 = (bf16[384,1024]{1,0:T(8,128)(2,1)S(1)}, bf16[384,1024]{1,0:T(8,128)(2,1)}, u32[]{:S(2)}) copy-start(bf16[384,1024]{1,0:T(8,128)(2,1)} %key_ref.3) | copy-start | bytes 2359300
  0.0 6.6 %copy-start = (bf16[384,2048]{1,0:T(8,128)(2,1)S(1)}, bf16[384,2048]{1,0:T(8,128)(2,1)}, u32[]{:S(2)}) copy-start(bf16[384,2048]{1,0:T(8,128)(2,1)} %value_hbm.3) | copy-start | bytes 4718596
  0.0 6.6 %copy-start.4 = (f32[384,16]{0,1:T(8,128)S(1)}, f32[384,16]{0,1:T(8,128)}, u32[]{:S(2)}) copy-start(f32[384,16]{0,1:T(8,128)} %param.19) | copy-start | bytes 73732
  0.0 6.6 %copy-start.6 = (f32[384,16]{0,1:T(8,128)S(1)}, f32[384,16]{0,1:T(8,128)}, u32[]{:S(2)}) copy-start(f32[384,16]{0,1:T(8,128)} %param.18) | copy-start | bytes 73732
  0.0 6.6 %copy-start.7 = (f32[4,1024]{1,0:T(4,128)S(1)}, f32[4,1024]{1,0:T(4,128)}, u32[]{:S(2)}) copy-start(f32[4,1024]{1,0:T(4,128)} %key_taps.3) | copy-start | bytes 49156
  0.0 6.6 %copy-start.5 = (f32[4,2048]{1,0:T(4,128)S(1)}, f32[4,2048]{1,0:T(4,128)}, u32[]{:S(2)}) copy-start(f32[4,2048]{1,0:T(4,128)} %value_taps.3) | copy-start | bytes 98308
  1.7 13.2 %collective-permute-start = (bf16[3,4096]{1,0:T(4,128)(2,1)}, bf16[3,4096]{1,0:T(4,128)(2,1)S(1)}, u32[]{:S(2)}, u32[]{:S(2)}) collective-permute-start(bf16[3,4096]{1,0:T(4,128)(2,1)} %tails.1), channel_id=1, source_target_pairs={{0,2},{2,4},{4,6},{6,8},{8,10},{10,12},{12,14},{14,16},{16,18},{18... | collective-permute-start | bytes 73736 | tf_op jit(solution)/shard_map/ppermute | solution.py:571
  14.9 6.3 %copy-start.3 = (bf16[3,4096]{1,0:T(4,128)(2,1)}, bf16[3,4096]{1,0:T(4,128)(2,1)S(1)}, u32[]{:S(2)}) copy-start(bf16[3,4096]{1,0:T(4,128)(2,1)S(1)} %collective-permute-done.before_ref.query_before) | copy-start | bytes 73732
  21.2 19.1 %all-to-all-start = ((bf16[16,128,256]{2,1,0:T(8,128)(2,1)}), bf16[16,128,256]{2,1,0:T(8,128)(2,1)S(1)}, u32[]{:S(2)}, u32[]{:S(2)}) async-start(bf16[16,128,256]{2,1,0:T(8,128)(2,1)} %get-tuple-element.20), calls=%async_computation | async-start | bytes 2097152 | tf_op jit(solution)/shard_map/all_to_all | solution.py:594
  41.5 18.8 %copy-start.1 = (bf16[6,384,256]{2,1,0:T(8,128)(2,1)S(1)}, bf16[6,384,256]{2,1,0:T(8,128)(2,1)}, u32[]{:S(2)}) copy-start(bf16[6,384,256]{2,1,0:T(8,128)(2,1)} %get-tuple-element.29.ahead_ref) | copy-start | bytes 3538948
  41.5 5.6 %collective-permute-start.1 = (bf16[2,128,128]{2,1,0:T(8,128)(2,1)S(1)}, bf16[2,128,128]{2,1,0:T(8,128)(2,1)S(1)}, u32[]{:S(2)}, u32[]{:S(2)}) collective-permute-start(bf16[2,128,128]{2,1,0:T(8,128)(2,1)S(1)} %get-tuple-element.28), channel_id=1, source_target_pairs={{0,16},{2,18},{4,20},{6,22},{8,24},{10,26},{12,28},{14,30},{1,17},... | collective-permute-start | bytes 196616 | tf_op jit(solution)/shard_map/ppermute | solution.py:571
  48.2 12.1 %all-to-all-start.1 = ((bf16[16,128,128]{2,1,0:T(8,128)(2,1)}), bf16[16,128,128]{2,1,0:T(8,128)(2,1)S(1)}, u32[]{:S(2)}, u32[]{:S(2)}) async-start(bf16[16,128,128]{2,1,0:T(8,128)(2,1)} %bitcast.5), calls=%async_computation.1 | async-start | bytes 1048576 | tf_op jit(solution)/shard_map/all_to_all | solution.py:611
  66.7 2.4 %collective-permute-start.2 = (bf16[192,2048]{1,0:T(8,128)(2,1)S(1)}, bf16[192,2048]{1,0:T(8,128)(2,1)S(1)}, u32[]{:S(2)}, u32[]{:S(2)}) collective-permute-start(bf16[192,2048]{1,0:T(8,128)(2,1)S(1)} %get-tuple-element.32), channel_id=1, source_target_pairs={{0,1},{1,0},{2,3},{3,2},{4,5},{5,4},{6,7},{7,6},{8,9},{9,8},{10,11... | collective-permute-start | bytes 2359304 | tf_op jit(solution)/shard_map/ppermute | solution.py:715

commit v13 on v12

--- a/solution.py
+++ b/solution.py
@@ -247,25 +247,29 @@
     )
     tail = jnp.exp(fade[:, CHUNK - 1 : CHUNK] - fade)
 
-    def leaving(held, out, at_step, kind):
-        here = pl.ds(at_step * heads, heads)
-        return pltpu.make_async_copy(held.at[here], out.at[here], sem.at[kind, at_step])
-
-    solved = [one.astype(BF16) for one in solved]
-    for pack, (chunk, head) in enumerate(packs):
-        solved_ref[step * heads + head, part_of(chunk - 1), : DV + DK] = solved[pack]
-    leaving(solved_ref, solved_hbm, step, 0).start()
-    for pack, (chunk, head) in enumerate(packs):
-        moves_ref[step * heads + head, chunk - 1] = mul(
-            turned[chunk, head // repeat_by] * tail[pack : pack + 1, :], solved[pack]
-        ).astype(BF16)
-    leaving(moves_ref, moves_hbm, step, 1).start()
+    several = min(HEADS_AT_ONCE, heads)
+
+    def leaving(held, out, group, kind):
+        here = pl.ds(group * several, several)
+        return pltpu.make_async_copy(held.at[here], out.at[here], sem.at[kind, group])
+
+    for at in range(0, heads, several):
+        group = (step * heads + at) // several
+        own = [(pack, c, head) for pack, (c, head) in enumerate(packs) if at <= head < at + several]
+        for pack, chunk, head in own:
+            solved_ref[step * heads + head, part_of(chunk - 1), : DV + DK] = solved[pack].astype(BF16)
+        leaving(solved_ref, solved_hbm, group, 0).start()
+        for pack, chunk, head in own:
+            moves_ref[step * heads + head, chunk - 1] = mul(
+                turned[chunk, head // repeat_by] * tail[pack : pack + 1, :], solved[pack]
+            ).astype(BF16)
+        leaving(moves_ref, moves_hbm, group, 1).start()
 
     @pl.when(step == pl.num_programs(0) - 1)
     def _():
-        for at_step in range(sem.shape[1]):
-            leaving(solved_ref, solved_hbm, at_step, 0).wait()
-            leaving(moves_ref, moves_hbm, at_step, 1).wait()
+        for group in range(sem.shape[1]):
+            leaving(solved_ref, solved_hbm, group, 0).wait()
+            leaving(moves_ref, moves_hbm, group, 1).wait()
 
 
 def states_kernel(
@@ -445,7 +449,7 @@
         logits = pl.BlockSpec((held, length), lambda step: (step * heads // held, 0))
         return key_heads // each, each * DK, heads * DV, of_heads, logits
 
-    each = math.gcd(4, key_heads)
+    each = math.gcd(8, key_heads)
     steps, narrow, wide, of_heads, logits = split(each)
     later = length - CHUNK
     solved, moves = pl.pallas_call(
@@ -464,7 +468,7 @@
             pltpu.VMEM((each * repeat_by, later + 16, DV), F32),
             pltpu.VMEM((value_heads, later, DV + 2 * DK), BF16),
             pltpu.VMEM((value_heads, chunks - 1, DK, DV + DK), BF16),
-            pltpu.SemaphoreType.DMA((2, steps)),
+            pltpu.SemaphoreType.DMA((2, value_heads // min(HEADS_AT_ONCE, wide // DV))),
         ],
         compiler_params=in_vmem(50),
         cost_estimate=pl.CostEstimate(flops=30 * work, bytes_accessed=0, transcendentals=0),

time: 70.5 us -> 70.5 us (level)
  no operation moved by 1% of the time
where the time goes in v13:
time: 70.5 us; the launch traced here: 70.2 us
  Pallas kernels  37.9 us (54%)
  starting transfers between devices  17.8 us (25%)
  waiting for transfers between devices  13.1 us (19%)
  other arithmetic  1.15 us (2%)
    pallas_call x1, Pallas kernels, local(): pl.pallas_call(local_kernel, grid=(steps,), in_specs=[columns_of(length,...  13.1 us
    ppermute x2, starting transfers between devices, shifted(): return lax.ppermute(value, axis, [(i, i + by) for i in range(count - by)])  8.55 us
    pallas_call x1, Pallas kernels, local_steps(): pl.pallas_call(later_kernel, grid=(steps,), in_specs=[vmem, vmem, vmem, v...  8.29 us
    all_to_all x1, waiting for transfers between devices, starts_of(): lax.all_to_all(starts.reshape(heads, DK, DV), axis, 0, 0, axis_index_grou...  7.67 us
    pallas_call x1, Pallas kernels, projected(): pl.pallas_call(project_kernel if halves else whole_kernel, in_specs=[pl.B...  6.36 us
    pallas_call x1, Pallas kernels, local_steps(): pl.pallas_call(states_kernel, grid=(1,), in_specs=[vmem, hbm, vmem, vmem,...  6.25 us
    all_to_all x1, starting transfers between devices, starts_of(): lax.all_to_all(pairs, axis, 0, 0, axis_index_groups=groups, tiled=True)  4.75 us
    all_to_all x1, starting transfers between devices, starts_of(): lax.all_to_all(starts.reshape(heads, DK, DV), axis, 0, 0, axis_index_grou...  4.45 us
  transfers between devices with their start and end apart: 5, of which 4 were waited for; matrix products, arithmetic and copies ran while one was open for 0% of the time, Pallas kernels for 31%

profile of v13, /device:TPU:0, one launch (start us, length us, event | category | flops | bytes accessed | tf_op | source)
XLA Modules:
  0.0 70.2 jit_solution(8557596524754394171)
XLA Ops:
  0.0 0.0 copy-start.2
  0.0 0.0 copy-start
  0.0 0.0 copy-start.4
  0.0 0.0 copy-start.6
  0.0 0.0 copy-start.7
  0.0 0.0 copy-start.5
  0.0 1.7 %tails.1 = bf16[3,4096]{1,0:T(4,128)(2,1)} custom-call(bf16[384,2048]{1,0:T(8,128)(2,1)} %value_hbm.3, bf16[384,1024]{1,0:T(8,128)(2,1)} %query_ref.1, bf16[384,1024]{1,0:T(8,128)(2,1)} %key_ref.3), custom_call_target="tpu_custom_call" | custom-call | tf_op jit(solution)/shard_map/tails/pallas_call | solution.py:742
  1.7 4.9 %collective-permute-start = (bf16[3,4096]{1,0:T(4,128)(2,1)}, bf16[3,4096]{1,0:T(4,128)(2,1)S(1)}, u32[]{:S(2)}, u32[]{:S(2)}) collective-permute-start(bf16[3,4096]{1,0:T(4,128)(2,1)} %tails.1), channel_id=1, source_target_pairs={{0,2},{2,4},{4,6},{6,8},{8,10},{10,12},{12,14},{14,16},{16,18},{18... | collective-permute-start | bytes 73736 | tf_op jit(solution)/shard_map/ppermute | solution.py:575
  6.6 0.0 copy-done.2
  6.6 0.0 copy-done
  6.6 0.0 copy-done.4
  6.6 0.0 copy-done.6
  6.6 0.0 copy-done.7
  6.6 0.0 copy-done.5
  6.6 8.3 %later.1 = (bf16[16,256,384]{2,1,0:T(8,128)(2,1)}, bf16[16,2,128,256]{3,2,1,0:T(8,128)(2,1)}) custom-call(bf16[384,1024]{1,0:T(8,128)(2,1)S(1)} %copy-done.2, bf16[384,2048]{1,0:T(8,128)(2,1)S(1)} %copy-done, f32[4,1024]{1,0:T(4,128)S(1)} %copy-done.7, f32[4,2048]{1,0:T(4,128)S(1)} %copy-done.5, f32[16,384]{1,0:T(8,128)S(1)} %bitcast.10, f32[16,384]{1,0:T(8,128)S(1)} %bitcast.8), custom_call_target="tpu_custom_call" | custom-call | flops 3019898880 | tf_op jit(solution)/shard_map/later/pallas_call | solution.py:455
  14.9 0.0 collective-permute-done.before_ref.query_before
  14.9 0.0 copy-start.3
  14.9 6.3 %states.1 = (bf16[16,128,256]{2,1,0:T(8,128)(2,1)}, bf16[16,128,384]{2,1,0:T(8,128)(2,1)}, bf16[2,16,128,256]{3,2,1,0:T(8,128)(2,1)}) custom-call(bf16[384,1024]{1,0:T(8,128)(2,1)S(1)} %copy-done.2, bf16[384,2048]{1,0:T(8,128)(2,1)} %value_hbm.3, bf16[3,4096]{1,0:T(4,128)(2,1)S(1)} %collective-permute-done.before_ref.query_before, f32[4,1024]{1,0:T(4,128)S(1)} %copy-done.7, ...), custom_call_target="tpu_custom_call" | custom-call | flops 2013265920 | tf_op jit(solution)/shard_map/states/pallas_call | solution.py:480
  21.2 0.0 copy-done.3
  21.2 4.8 %all-to-all-start = ((bf16[16,128,256]{2,1,0:T(8,128)(2,1)}), bf16[16,128,256]{2,1,0:T(8,128)(2,1)S(1)}, u32[]{:S(2)}, u32[]{:S(2)}) async-start(bf16[16,128,256]{2,1,0:T(8,128)(2,1)} %get-tuple-element.20), calls=%async_computation | async-start | bytes 2097152 | tf_op jit(solution)/shard_map/all_to_all | solution.py:598
  26.0 13.1 %local.1 = (bf16[6,384,256]{2,1,0:T(8,128)(2,1)}, bf16[18,384,256]{2,1,0:T(8,128)(2,1)}) custom-call(bf16[384,1024]{1,0:T(8,128)(2,1)} %query_ref.1, bf16[3,4096]{1,0:T(4,128)(2,1)} %copy-done.3, f32[4,1024]{1,0:T(4,128)} %query_taps.1, f32[16,384]{1,0:T(8,128)} %bitcast.7, bf16[16,128,384]{2,1,0:T(8,128)(2,1)} %get-tuple-element.21.first_solved, ...), custom_call_target="tpu_custom_call" | custom-call | flops 1207959552 | tf_op jit(solution)/shard_map/local/pallas_call | solution.py:515
  39.1 1.3 %all-to-all-done = bf16[16,128,256]{2,1,0:T(8,128)(2,1)S(1)} async-done(((bf16[16,128,256]{2,1,0:T(8,128)(2,1)}), bf16[16,128,256]{2,1,0:T(8,128)(2,1)S(1)}, u32[]{:S(2)}, u32[]{:S(2)}) %all-to-all-start) | async-done | bytes 1048608 | tf_op jit(solution)/shard_map/all_to_all | solution.py:598
  40.4 1.1 %prefix.1 = (bf16[8,2,128,256]{3,2,1,0:T(8,128)(2,1)S(1)}, bf16[2,128,128]{2,1,0:T(8,128)(2,1)S(1)}) custom-call(bf16[8,2,128,256]{3,2,1,0:T(8,128)(2,1)S(1)} %bitcast.6), custom_call_target="tpu_custom_call" | custom-call | tf_op jit(solution)/shard_map/prefix/pallas_call | solution.py:600
  41.5 0.0 copy-start.1
  41.5 3.7 %collective-permute-start.1 = (bf16[2,128,128]{2,1,0:T(8,128)(2,1)S(1)}, bf16[2,128,128]{2,1,0:T(8,128)(2,1)S(1)}, u32[]{:S(2)}, u32[]{:S(2)}) collective-permute-start(bf16[2,128,128]{2,1,0:T(8,128)(2,1)S(1)} %get-tuple-element.28), channel_id=1, source_target_pairs={{0,16},{2,18},{4,20},{6,22},{8,24},{10,26},{12,28},{14,30},{1,17},... | collective-permute-start | bytes 196616 | tf_op jit(solution)/shard_map/ppermute | solution.py:575
  45.2 1.9 %collective-permute-done.1.start_ref = bf16[2,128,128]{2,1,0:T(8,128)(2,1)S(1)} collective-permute-done((bf16[2,128,128]{2,1,0:T(8,128)(2,1)S(1)}, bf16[2,128,128]{2,1,0:T(8,128)(2,1)S(1)}, u32[]{:S(2)}, u32[]{:S(2)}) %collective-permute-start.1) | collective-permute-done | bytes 65568 | tf_op jit(solution)/shard_map/ppermute | solution.py:575
  47.1 1.1 %apply.1 = bf16[8,2,128,128]{3,2,1,0:T(8,128)(2,1)} custom-call(bf16[8,2,128,256]{3,2,1,0:T(8,128)(2,1)S(1)} %get-tuple-element.27.prefix_ref, bf16[2,128,128]{2,1,0:T(8,128)(2,1)S(1)} %collective-permute-done.1.start_ref), custom_call_target="tpu_custom_call" | custom-call | tf_op jit(solution)/shard_map/apply/pallas_call | solution.py:609
  48.2 4.4 %all-to-all-start.1 = ((bf16[16,128,128]{2,1,0:T(8,128)(2,1)}), bf16[16,128,128]{2,1,0:T(8,128)(2,1)S(1)}, u32[]{:S(2)}, u32[]{:S(2)}) async-start(bf16[16,128,128]{2,1,0:T(8,128)(2,1)} %bitcast.5), calls=%async_computation.1 | async-start | bytes 1048576 | tf_op jit(solution)/shard_map/all_to_all | solution.py:615
  52.6 7.7 %all-to-all-done.1.starts_ref = bf16[16,128,128]{2,1,0:T(8,128)(2,1)S(1)} async-done(((bf16[16,128,128]{2,1,0:T(8,128)(2,1)}), bf16[16,128,128]{2,1,0:T(8,128)(2,1)S(1)}, u32[]{:S(2)}, u32[]{:S(2)}) %all-to-all-start.1) | async-done | bytes 524320 | tf_op jit(solution)/shard_map/all_to_all | solution.py:615
  60.3 0.0 copy-done.1
  60.3 6.4 %project.1 = (bf16[192,2048]{1,0:T(8,128)(2,1)S(1)}, bf16[192,2048]{1,0:T(8,128)(2,1)S(1)}) custom-call(s32[1]{0:T(128)} %bitcast.place_ref, bf16[16,128,128]{2,1,0:T(8,128)(2,1)S(1)} %all-to-all-done.1.starts_ref, bf16[6,384,256]{2,1,0:T(8,128)(2,1)S(1)} %copy-done.1, bf16[18,384,256]{2,1,0:T(8,128)(2,1)} %get-tuple-element.30.parts_hbm, ...), custom_call_target="tpu_custom_call" | custom-call | tf_op jit(solution)/shard_map/project/pallas_call | solution.py:701
  66.7 0.1 collective-permute-start.2
  66.8 2.3 %collective-permute-done.2 = bf16[192,2048]{1,0:T(8,128)(2,1)S(1)} collective-permute-done((bf16[192,2048]{1,0:T(8,128)(2,1)S(1)}, bf16[192,2048]{1,0:T(8,128)(2,1)S(1)}, u32[]{:S(2)}, u32[]{:S(2)}) %collective-permute-start.2) | collective-permute-done | bytes 786464 | tf_op jit(solution)/shard_map/ppermute | solution.py:719
  69.0 1.2 %add_convert_fusion = bf16[192,2048]{1,0:T(8,128)(2,1)} fusion(bf16[192,2048]{1,0:T(8,128)(2,1)S(1)} %collective-permute-done.2, bf16[192,2048]{1,0:T(8,128)(2,1)S(1)} %get-tuple-element.31), kind=kLoop, calls=%fused_computation | loop fusion | flops 1572864 | bytes 2359296 | tf_op jit(solution)/shard_map/convert_element_type | solution.py:720
Async XLA Ops:
  0.0 6.6 %copy-start.2 = (bf16[384,1024]{1,0:T(8,128)(2,1)S(1)}, bf16[384,1024]{1,0:T(8,128)(2,1)}, u32[]{:S(2)}) copy-start(bf16[384,1024]{1,0:T(8,128)(2,1)} %key_ref.3) | copy-start | bytes 2359300
  0.0 6.6 %copy-start = (bf16[384,2048]{1,0:T(8,128)(2,1)S(1)}, bf16[384,2048]{1,0:T(8,128)(2,1)}, u32[]{:S(2)}) copy-start(bf16[384,2048]{1,0:T(8,128)(2,1)} %value_hbm.3) | copy-start | bytes 4718596
  0.0 6.6 %copy-start.4 = (f32[384,16]{0,1:T(8,128)S(1)}, f32[384,16]{0,1:T(8,128)}, u32[]{:S(2)}) copy-start(f32[384,16]{0,1:T(8,128)} %param.19) | copy-start | bytes 73732
  0.0 6.6 %copy-start.6 = (f32[384,16]{0,1:T(8,128)S(1)}, f32[384,16]{0,1:T(8,128)}, u32[]{:S(2)}) copy-start(f32[384,16]{0,1:T(8,128)} %param.18) | copy-start | bytes 73732
  0.0 6.6 %copy-start.7 = (f32[4,1024]{1,0:T(4,128)S(1)}, f32[4,1024]{1,0:T(4,128)}, u32[]{:S(2)}) copy-start(f32[4,1024]{1,0:T(4,128)} %key_taps.3) | copy-start | bytes 49156
  0.0 6.6 %copy-start.5 = (f32[4,2048]{1,0:T(4,128)S(1)}, f32[4,2048]{1,0:T(4,128)}, u32[]{:S(2)}) copy-start(f32[4,2048]{1,0:T(4,128)} %value_taps.3) | copy-start | bytes 98308
  1.7 13.2 %collective-permute-start = (bf16[3,4096]{1,0:T(4,128)(2,1)}, bf16[3,4096]{1,0:T(4,128)(2,1)S(1)}, u32[]{:S(2)}, u32[]{:S(2)}) collective-permute-start(bf16[3,4096]{1,0:T(4,128)(2,1)} %tails.1), channel_id=1, source_target_pairs={{0,2},{2,4},{4,6},{6,8},{8,10},{10,12},{12,14},{14,16},{16,18},{18... | collective-permute-start | bytes 73736 | tf_op jit(solution)/shard_map/ppermute | solution.py:575
  14.9 6.3 %copy-start.3 = (bf16[3,4096]{1,0:T(4,128)(2,1)}, bf16[3,4096]{1,0:T(4,128)(2,1)S(1)}, u32[]{:S(2)}) copy-start(bf16[3,4096]{1,0:T(4,128)(2,1)S(1)} %collective-permute-done.before_ref.query_before) | copy-start | bytes 73732
  21.2 19.2 %all-to-all-start = ((bf16[16,128,256]{2,1,0:T(8,128)(2,1)}), bf16[16,128,256]{2,1,0:T(8,128)(2,1)S(1)}, u32[]{:S(2)}, u32[]{:S(2)}) async-start(bf16[16,128,256]{2,1,0:T(8,128)(2,1)} %get-tuple-element.20), calls=%async_computation | async-start | bytes 2097152 | tf_op jit(solution)/shard_map/all_to_all | solution.py:598
  41.5 18.8 %copy-start.1 = (bf16[6,384,256]{2,1,0:T(8,128)(2,1)S(1)}, bf16[6,384,256]{2,1,0:T(8,128)(2,1)}, u32[]{:S(2)}) copy-start(bf16[6,384,256]{2,1,0:T(8,128)(2,1)} %get-tuple-element.29.ahead_ref) | copy-start | bytes 3538948
  41.5 5.6 %collective-permute-start.1 = (bf16[2,128,128]{2,1,0:T(8,128)(2,1)S(1)}, bf16[2,128,128]{2,1,0:T(8,128)(2,1)S(1)}, u32[]{:S(2)}, u32[]{:S(2)}) collective-permute-start(bf16[2,128,128]{2,1,0:T(8,128)(2,1)S(1)} %get-tuple-element.28), channel_id=1, source_target_pairs={{0,16},{2,18},{4,20},{6,22},{8,24},{10,26},{12,28},{14,30},{1,17},... | collective-permute-start | bytes 196616 | tf_op jit(solution)/shard_map/ppermute | solution.py:575
  48.2 12.1 %all-to-all-start.1 = ((bf16[16,128,128]{2,1,0:T(8,128)(2,1)}), bf16[16,128,128]{2,1,0:T(8,128)(2,1)S(1)}, u32[]{:S(2)}, u32[]{:S(2)}) async-start(bf16[16,128,128]{2,1,0:T(8,128)(2,1)} %bitcast.5), calls=%async_computation.1 | async-start | bytes 1048576 | tf_op jit(solution)/shard_map/all_to_all | solution.py:615
  66.7 2.4 %collective-permute-start.2 = (bf16[192,2048]{1,0:T(8,128)(2,1)S(1)}, bf16[192,2048]{1,0:T(8,128)(2,1)S(1)}, u32[]{:S(2)}, u32[]{:S(2)}) collective-permute-start(bf16[192,2048]{1,0:T(8,128)(2,1)S(1)} %get-tuple-element.32), channel_id=1, source_target_pairs={{0,1},{1,0},{2,3},{3,2},{4,5},{5,4},{6,7},{7,6},{8,9},{9,8},{10,11... | collective-permute-start | bytes 2359304 | tf_op jit(solution)/shard_map/ppermute | solution.py:719

commit v14 on v13

--- a/solution.py
+++ b/solution.py
@@ -285,7 +285,6 @@
     value_copy = pltpu.make_async_copy(value_hbm.at[pl.ds(0, CHUNK)], value_ref, value_sem)
     value_copy.start()
     incoming = pltpu.make_async_copy(moves_hbm, moves_ref, in_sem)
-    incoming.start()
 
     key_at = before_ref.shape[1] - key_ref.shape[1]
     widen(key_padded, 5, 3, before_ref[:, key_at:])
@@ -301,6 +300,7 @@
 
     def value_rows():
         value_copy.wait()
+        incoming.start()
         widen(value_padded, 5, 3, before_ref[:, : value_ref.shape[1]])
         widen(value_padded, 8, CHUNK, value_ref[...])
 
@@ -657,16 +657,15 @@
         parts(2).start()
     for g in range(groups):
         weights(g).wait()
-        if g + 1 < groups:
-            parts(g + 1).wait()
         if g + 2 < groups:
             weights(g + 2).start()
-        if g + 3 < groups:
-            parts(g + 3).start()
         normed = following
-        if g + 1 < groups:
-            following = normed_group(g + 1)
         for at in range(0, width, block):
+            if g + 1 < groups and at == (width // block // 2 * block if g == 0 else 0):
+                parts(g + 1).wait()
+                if g + 3 < groups:
+                    parts(g + 3).start()
+                following = normed_group(g + 1)
             added = jnp.dot(
                 normed, weight_ref[g * each * DV : (g + 1) * each * DV, at : at + block],
                 preferred_element_type=F32,

time: 70.5 us -> 70.1 us (level)
  no operation moved by 1% of the time
where the time goes in v14:
time: 70.1 us; the launch traced here: 69.8 us
  Pallas kernels  37.5 us (53%)
  starting transfers between devices  17.8 us (25%)
  waiting for transfers between devices  13.1 us (19%)
  other arithmetic  1.15 us (2%)
    pallas_call x1, Pallas kernels, local(): pl.pallas_call(local_kernel, grid=(steps,), in_specs=[columns_of(length,...  13.1 us
    ppermute x2, starting transfers between devices, shifted(): return lax.ppermute(value, axis, [(i, i + by) for i in range(count - by)])  8.56 us
    pallas_call x1, Pallas kernels, local_steps(): pl.pallas_call(later_kernel, grid=(steps,), in_specs=[vmem, vmem, vmem, v...  8.29 us
    all_to_all x1, waiting for transfers between devices, starts_of(): lax.all_to_all(starts.reshape(heads, DK, DV), axis, 0, 0, axis_index_grou...  7.67 us
    pallas_call x1, Pallas kernels, projected(): pl.pallas_call(project_kernel if halves else whole_kernel, in_specs=[pl.B...  6.24 us
    pallas_call x1, Pallas kernels, local_steps(): pl.pallas_call(states_kernel, grid=(1,), in_specs=[vmem, hbm, vmem, vmem,...  6 us
    all_to_all x1, starting transfers between devices, starts_of(): lax.all_to_all(pairs, axis, 0, 0, axis_index_groups=groups, tiled=True)  4.74 us
    all_to_all x1, starting transfers between devices, starts_of(): lax.all_to_all(starts.reshape(heads, DK, DV), axis, 0, 0, axis_index_grou...  4.41 us
  transfers between devices with their start and end apart: 5, of which 4 were waited for; matrix products, arithmetic and copies ran while one was open for 0% of the time, Pallas kernels for 31%

profile of v14, /device:TPU:0, one launch (start us, length us, event | category | flops | bytes accessed | tf_op | source)
XLA Modules:
  0.0 69.8 jit_solution(7901154680672440975)
XLA Ops:
  0.0 0.0 copy-start.2
  0.0 0.0 copy-start
  0.0 0.0 copy-start.4
  0.0 0.0 copy-start.6
  0.0 0.0 copy-start.7
  0.0 0.0 copy-start.5
  0.0 1.7 %tails.1 = bf16[3,4096]{1,0:T(4,128)(2,1)} custom-call(bf16[384,2048]{1,0:T(8,128)(2,1)} %value_hbm.3, bf16[384,1024]{1,0:T(8,128)(2,1)} %query_ref.1, bf16[384,1024]{1,0:T(8,128)(2,1)} %key_ref.3), custom_call_target="tpu_custom_call" | custom-call | tf_op jit(solution)/shard_map/tails/pallas_call | solution.py:741
  1.7 4.9 %collective-permute-start = (bf16[3,4096]{1,0:T(4,128)(2,1)}, bf16[3,4096]{1,0:T(4,128)(2,1)S(1)}, u32[]{:S(2)}, u32[]{:S(2)}) collective-permute-start(bf16[3,4096]{1,0:T(4,128)(2,1)} %tails.1), channel_id=1, source_target_pairs={{0,2},{2,4},{4,6},{6,8},{8,10},{10,12},{12,14},{14,16},{16,18},{18... | collective-permute-start | bytes 73736 | tf_op jit(solution)/shard_map/ppermute | solution.py:575
  6.6 0.0 copy-done.2
  6.6 0.0 copy-done
  6.6 0.0 copy-done.4
  6.6 0.0 copy-done.6
  6.6 0.0 copy-done.7
  6.6 0.0 copy-done.5
  6.6 8.3 %later.1 = (bf16[16,256,384]{2,1,0:T(8,128)(2,1)}, bf16[16,2,128,256]{3,2,1,0:T(8,128)(2,1)}) custom-call(bf16[384,1024]{1,0:T(8,128)(2,1)S(1)} %copy-done.2, bf16[384,2048]{1,0:T(8,128)(2,1)S(1)} %copy-done, f32[4,1024]{1,0:T(4,128)S(1)} %copy-done.7, f32[4,2048]{1,0:T(4,128)S(1)} %copy-done.5, f32[16,384]{1,0:T(8,128)S(1)} %bitcast.10, f32[16,384]{1,0:T(8,128)S(1)} %bitcast.8), custom_call_target="tpu_custom_call" | custom-call | flops 3019898880 | tf_op jit(solution)/shard_map/later/pallas_call | solution.py:455
  14.9 0.0 collective-permute-done.before_ref.query_before
  14.9 0.0 copy-start.3
  14.9 6.0 %states.1 = (bf16[16,128,256]{2,1,0:T(8,128)(2,1)}, bf16[16,128,384]{2,1,0:T(8,128)(2,1)}, bf16[2,16,128,256]{3,2,1,0:T(8,128)(2,1)}) custom-call(bf16[384,1024]{1,0:T(8,128)(2,1)S(1)} %copy-done.2, bf16[384,2048]{1,0:T(8,128)(2,1)} %value_hbm.3, bf16[3,4096]{1,0:T(4,128)(2,1)S(1)} %collective-permute-done.before_ref.query_before, f32[4,1024]{1,0:T(4,128)S(1)} %copy-done.7, ...), custom_call_target="tpu_custom_call" | custom-call | flops 2013265920 | tf_op jit(solution)/shard_map/states/pallas_call | solution.py:480
  20.9 0.0 copy-done.3
  21.0 4.7 %all-to-all-start = ((bf16[16,128,256]{2,1,0:T(8,128)(2,1)}), bf16[16,128,256]{2,1,0:T(8,128)(2,1)S(1)}, u32[]{:S(2)}, u32[]{:S(2)}) async-start(bf16[16,128,256]{2,1,0:T(8,128)(2,1)} %get-tuple-element.20), calls=%async_computation | async-start | bytes 2097152 | tf_op jit(solution)/shard_map/all_to_all | solution.py:598
  25.7 13.1 %local.1 = (bf16[6,384,256]{2,1,0:T(8,128)(2,1)}, bf16[18,384,256]{2,1,0:T(8,128)(2,1)}) custom-call(bf16[384,1024]{1,0:T(8,128)(2,1)} %query_ref.1, bf16[3,4096]{1,0:T(4,128)(2,1)} %copy-done.3, f32[4,1024]{1,0:T(4,128)} %query_taps.1, f32[16,384]{1,0:T(8,128)} %bitcast.7, bf16[16,128,384]{2,1,0:T(8,128)(2,1)} %get-tuple-element.21.first_solved, ...), custom_call_target="tpu_custom_call" | custom-call | flops 1207959552 | tf_op jit(solution)/shard_map/local/pallas_call | solution.py:515
  38.8 1.3 %all-to-all-done = bf16[16,128,256]{2,1,0:T(8,128)(2,1)S(1)} async-done(((bf16[16,128,256]{2,1,0:T(8,128)(2,1)}), bf16[16,128,256]{2,1,0:T(8,128)(2,1)S(1)}, u32[]{:S(2)}, u32[]{:S(2)}) %all-to-all-start) | async-done | bytes 1048608 | tf_op jit(solution)/shard_map/all_to_all | solution.py:598
  40.1 1.1 %prefix.1 = (bf16[8,2,128,256]{3,2,1,0:T(8,128)(2,1)S(1)}, bf16[2,128,128]{2,1,0:T(8,128)(2,1)S(1)}) custom-call(bf16[8,2,128,256]{3,2,1,0:T(8,128)(2,1)S(1)} %bitcast.6), custom_call_target="tpu_custom_call" | custom-call | tf_op jit(solution)/shard_map/prefix/pallas_call | solution.py:600
  41.2 0.0 copy-start.1
  41.3 3.7 %collective-permute-start.1 = (bf16[2,128,128]{2,1,0:T(8,128)(2,1)S(1)}, bf16[2,128,128]{2,1,0:T(8,128)(2,1)S(1)}, u32[]{:S(2)}, u32[]{:S(2)}) collective-permute-start(bf16[2,128,128]{2,1,0:T(8,128)(2,1)S(1)} %get-tuple-element.28), channel_id=1, source_target_pairs={{0,16},{2,18},{4,20},{6,22},{8,24},{10,26},{12,28},{14,30},{1,17},... | collective-permute-start | bytes 196616 | tf_op jit(solution)/shard_map/ppermute | solution.py:575
  45.0 1.9 %collective-permute-done.1.start_ref = bf16[2,128,128]{2,1,0:T(8,128)(2,1)S(1)} collective-permute-done((bf16[2,128,128]{2,1,0:T(8,128)(2,1)S(1)}, bf16[2,128,128]{2,1,0:T(8,128)(2,1)S(1)}, u32[]{:S(2)}, u32[]{:S(2)}) %collective-permute-start.1) | collective-permute-done | bytes 65568 | tf_op jit(solution)/shard_map/ppermute | solution.py:575
  46.9 1.1 %apply.1 = bf16[8,2,128,128]{3,2,1,0:T(8,128)(2,1)} custom-call(bf16[8,2,128,256]{3,2,1,0:T(8,128)(2,1)S(1)} %get-tuple-element.27.prefix_ref, bf16[2,128,128]{2,1,0:T(8,128)(2,1)S(1)} %collective-permute-done.1.start_ref), custom_call_target="tpu_custom_call" | custom-call | tf_op jit(solution)/shard_map/apply/pallas_call | solution.py:609
  47.9 4.4 %all-to-all-start.1 = ((bf16[16,128,128]{2,1,0:T(8,128)(2,1)}), bf16[16,128,128]{2,1,0:T(8,128)(2,1)S(1)}, u32[]{:S(2)}, u32[]{:S(2)}) async-start(bf16[16,128,128]{2,1,0:T(8,128)(2,1)} %bitcast.5), calls=%async_computation.1 | async-start | bytes 1048576 | tf_op jit(solution)/shard_map/all_to_all | solution.py:615
  52.4 7.7 %all-to-all-done.1.starts_ref = bf16[16,128,128]{2,1,0:T(8,128)(2,1)S(1)} async-done(((bf16[16,128,128]{2,1,0:T(8,128)(2,1)}), bf16[16,128,128]{2,1,0:T(8,128)(2,1)S(1)}, u32[]{:S(2)}, u32[]{:S(2)}) %all-to-all-start.1) | async-done | bytes 524320 | tf_op jit(solution)/shard_map/all_to_all | solution.py:615
  60.0 0.0 copy-done.1
  60.0 6.2 %project.1 = (bf16[192,2048]{1,0:T(8,128)(2,1)S(1)}, bf16[192,2048]{1,0:T(8,128)(2,1)S(1)}) custom-call(s32[1]{0:T(128)} %bitcast.place_ref, bf16[16,128,128]{2,1,0:T(8,128)(2,1)S(1)} %all-to-all-done.1.starts_ref, bf16[6,384,256]{2,1,0:T(8,128)(2,1)S(1)} %copy-done.1, bf16[18,384,256]{2,1,0:T(8,128)(2,1)} %get-tuple-element.30.parts_hbm, ...), custom_call_target="tpu_custom_call" | custom-call | tf_op jit(solution)/shard_map/project/pallas_call | solution.py:700
  66.3 0.1 collective-permute-start.2
  66.4 2.3 %collective-permute-done.2 = bf16[192,2048]{1,0:T(8,128)(2,1)S(1)} collective-permute-done((bf16[192,2048]{1,0:T(8,128)(2,1)S(1)}, bf16[192,2048]{1,0:T(8,128)(2,1)S(1)}, u32[]{:S(2)}, u32[]{:S(2)}) %collective-permute-start.2) | collective-permute-done | bytes 786464 | tf_op jit(solution)/shard_map/ppermute | solution.py:718
  68.6 1.2 %add_convert_fusion = bf16[192,2048]{1,0:T(8,128)(2,1)} fusion(bf16[192,2048]{1,0:T(8,128)(2,1)S(1)} %collective-permute-done.2, bf16[192,2048]{1,0:T(8,128)(2,1)S(1)} %get-tuple-element.31), kind=kLoop, calls=%fused_computation | loop fusion | flops 1572864 | bytes 2359296 | tf_op jit(solution)/shard_map/convert_element_type | solution.py:719
Async XLA Ops:
  0.0 6.6 %copy-start.2 = (bf16[384,1024]{1,0:T(8,128)(2,1)S(1)}, bf16[384,1024]{1,0:T(8,128)(2,1)}, u32[]{:S(2)}) copy-start(bf16[384,1024]{1,0:T(8,128)(2,1)} %key_ref.3) | copy-start | bytes 2359300
  0.0 6.6 %copy-start = (bf16[384,2048]{1,0:T(8,128)(2,1)S(1)}, bf16[384,2048]{1,0:T(8,128)(2,1)}, u32[]{:S(2)}) copy-start(bf16[384,2048]{1,0:T(8,128)(2,1)} %value_hbm.3) | copy-start | bytes 4718596
  0.0 6.6 %copy-start.4 = (f32[384,16]{0,1:T(8,128)S(1)}, f32[384,16]{0,1:T(8,128)}, u32[]{:S(2)}) copy-start(f32[384,16]{0,1:T(8,128)} %param.19) | copy-start | bytes 73732
  0.0 6.6 %copy-start.6 = (f32[384,16]{0,1:T(8,128)S(1)}, f32[384,16]{0,1:T(8,128)}, u32[]{:S(2)}) copy-start(f32[384,16]{0,1:T(8,128)} %param.18) | copy-start | bytes 73732
  0.0 6.6 %copy-start.7 = (f32[4,1024]{1,0:T(4,128)S(1)}, f32[4,1024]{1,0:T(4,128)}, u32[]{:S(2)}) copy-start(f32[4,1024]{1,0:T(4,128)} %key_taps.3) | copy-start | bytes 49156
  0.0 6.6 %copy-start.5 = (f32[4,2048]{1,0:T(4,128)S(1)}, f32[4,2048]{1,0:T(4,128)}, u32[]{:S(2)}) copy-start(f32[4,2048]{1,0:T(4,128)} %value_taps.3) | copy-start | bytes 98308
  1.7 13.2 %collective-permute-start = (bf16[3,4096]{1,0:T(4,128)(2,1)}, bf16[3,4096]{1,0:T(4,128)(2,1)S(1)}, u32[]{:S(2)}, u32[]{:S(2)}) collective-permute-start(bf16[3,4096]{1,0:T(4,128)(2,1)} %tails.1), channel_id=1, source_target_pairs={{0,2},{2,4},{4,6},{6,8},{8,10},{10,12},{12,14},{14,16},{16,18},{18... | collective-permute-start | bytes 73736 | tf_op jit(solution)/shard_map/ppermute | solution.py:575
  14.9 6.0 %copy-start.3 = (bf16[3,4096]{1,0:T(4,128)(2,1)}, bf16[3,4096]{1,0:T(4,128)(2,1)S(1)}, u32[]{:S(2)}) copy-start(bf16[3,4096]{1,0:T(4,128)(2,1)S(1)} %collective-permute-done.before_ref.query_before) | copy-start | bytes 73732
  21.0 19.1 %all-to-all-start = ((bf16[16,128,256]{2,1,0:T(8,128)(2,1)}), bf16[16,128,256]{2,1,0:T(8,128)(2,1)S(1)}, u32[]{:S(2)}, u32[]{:S(2)}) async-start(bf16[16,128,256]{2,1,0:T(8,128)(2,1)} %get-tuple-element.20), calls=%async_computation | async-start | bytes 2097152 | tf_op jit(solution)/shard_map/all_to_all | solution.py:598
  41.2 18.8 %copy-start.1 = (bf16[6,384,256]{2,1,0:T(8,128)(2,1)S(1)}, bf16[6,384,256]{2,1,0:T(8,128)(2,1)}, u32[]{:S(2)}) copy-start(bf16[6,384,256]{2,1,0:T(8,128)(2,1)} %get-tuple-element.29.ahead_ref) | copy-start | bytes 3538948
  41.3 5.6 %collective-permute-start.1 = (bf16[2,128,128]{2,1,0:T(8,128)(2,1)S(1)}, bf16[2,128,128]{2,1,0:T(8,128)(2,1)S(1)}, u32[]{:S(2)}, u32[]{:S(2)}) collective-permute-start(bf16[2,128,128]{2,1,0:T(8,128)(2,1)S(1)} %get-tuple-element.28), channel_id=1, source_target_pairs={{0,16},{2,18},{4,20},{6,22},{8,24},{10,26},{12,28},{14,30},{1,17},... | collective-permute-start | bytes 196616 | tf_op jit(solution)/shard_map/ppermute | solution.py:575
  47.9 12.1 %all-to-all-start.1 = ((bf16[16,128,128]{2,1,0:T(8,128)(2,1)}), bf16[16,128,128]{2,1,0:T(8,128)(2,1)S(1)}, u32[]{:S(2)}, u32[]{:S(2)}) async-start(bf16[16,128,128]{2,1,0:T(8,128)(2,1)} %bitcast.5), calls=%async_computation.1 | async-start | bytes 1048576 | tf_op jit(solution)/shard_map/all_to_all | solution.py:615
  66.3 2.4 %collective-permute-start.2 = (bf16[192,2048]{1,0:T(8,128)(2,1)S(1)}, bf16[192,2048]{1,0:T(8,128)(2,1)S(1)}, u32[]{:S(2)}, u32[]{:S(2)}) collective-permute-start(bf16[192,2048]{1,0:T(8,128)(2,1)S(1)} %get-tuple-element.32), channel_id=1, source_target_pairs={{0,1},{1,0},{2,3},{3,2},{4,5},{5,4},{6,7},{7,6},{8,9},{9,8},{10,11... | collective-permute-start | bytes 2359304 | tf_op jit(solution)/shard_map/ppermute | solution.py:718
